TPU v7x, 32 devices: a whole 2x2x4 slice. The times are simulated.
32 devices in a mesh: group: 2 (over y), expert: 4 (over z), tensor: 4 (over x, core).
Axes of the slice: x: 2, y: 2, z: 4, core: 2. Of those that a mesh axis runs over, the one named last changes fastest.
Arguments:
- residual: float32 [256, 3584], P(('group', 'expert')), parts along dimension 0, may hold values from -30 to 30
- attention_part: bfloat16 [4, 256, 3584], P('tensor', ('group', 'expert')), parts along dimension 1, may hold values from -2.5 to 2.5
- norm_gain: float32 [3584], replicated, may hold values from 0.25 to 1.75
- expert_ids: int32 [256, 2], P(('group', 'expert')), parts along dimension 0, may hold values from 0 to 3, all different within a row; in each aligned block of 32 rows (0 to 31, 32 to 63, ...) at most 17 rows name the same one
- gate_weights: float32 [256, 2], P(('group', 'expert')), parts along dimension 0, may hold values from 0.1 to 0.9
- w_gate: bfloat16 [4, 3584, 1024], P('expert', None, 'tensor'), may hold values from -0.09375 to 0.09375
- w_up: bfloat16 [4, 3584, 1024], P('expert', None, 'tensor'), may hold values from -0.09375 to 0.09375
- w_down: bfloat16 [4, 1024, 3584], P('expert', 'tensor'), may hold values from -0.1875 to 0.1875
Outputs:
- layer_out: float32 [256, 3584], P(('group', 'expert'), 'tensor'), parts along dimension 0
There are 2 independent parts, one for each index of `group`. A program takes and returns all parts, laid end to end along the dimension named above; an argument that names none is the same for every part. Nothing has to cross between parts.
Inputs may be any that keep to these rules, and one draw needn't show every extreme that they name: `expert_ids`: each row names 2 different experts; within the rows of one index of the expert axis (aligned blocks of 32 rows) no expert is named by more than 17 rows, a bound that some block reaches.
All inputs are finite; a program needn't handle non-finite values.
Results may differ from a plain program's by a relative error of at most 0.0055.
Values may be sent and summed in bfloat16 or wider, within the bound.
No kernel may reach another device: no remote copies, remote signals or barrier semaphores. Data moves between devices by JAX's collectives and lax.ppermute only.
A program may use at most 64 MiB of HBM per device.

v0:
```python
import jax
import jax.numpy as jnp
from jax import lax
from jax.sharding import PartitionSpec as P

CAP = 17


EPSILON = 1e-06


def expert_block(inputs, gate_weight, up_weight, down_weight):
    gated = jnp.dot(inputs, gate_weight, preferred_element_type=jnp.float32)
    upward = jnp.dot(inputs, up_weight, preferred_element_type=jnp.float32)
    active = (jax.nn.silu(gated) * upward).astype(jnp.bfloat16)
    return jnp.dot(active, down_weight, preferred_element_type=jnp.float32)


def local(residual, attention_part, norm_gain, expert_ids, gate_weights, w_gate, w_up, w_down):
    row_count, feature_count = residual.shape
    top_count = expert_ids.shape[1]
    tensor_count = lax.axis_size("tensor")
    expert_count = lax.axis_size("expert")
    column_width = feature_count // tensor_count
    column_start = lax.axis_index("tensor") * column_width
    partials = attention_part[0].astype(jnp.float32)
    attention = lax.psum(partials.astype(jnp.bfloat16), "tensor").astype(jnp.float32)
    hidden = residual + attention
    inverse = lax.rsqrt(jnp.mean(hidden * hidden, axis=1, keepdims=True) + EPSILON)
    normed = (hidden * inverse * norm_gain).astype(jnp.bfloat16)
    hidden_columns = lax.dynamic_slice_in_dim(hidden, column_start, column_width, 1)
    flat_ids = expert_ids.reshape(-1)
    onehot = (flat_ids[:, None] == jnp.arange(expert_count, dtype=jnp.int32)[None, :]).astype(
        jnp.int32
    )
    before = jnp.cumsum(onehot, axis=0) - onehot
    position = jnp.sum(before * onehot, axis=1)
    slot_index = flat_ids * CAP + position
    slot_total = expert_count * CAP
    matches = jnp.arange(slot_total, dtype=jnp.int32)[:, None] == slot_index[None, :]
    dispatch_table = jnp.any(matches.reshape(slot_total, row_count, top_count), axis=2).astype(
        jnp.bfloat16
    )
    outgoing = jnp.dot(dispatch_table, normed, preferred_element_type=jnp.float32).astype(
        jnp.bfloat16
    )
    outgoing = outgoing.reshape(expert_count, CAP, normed.shape[1])
    arrived = lax.all_to_all(outgoing, "expert", split_axis=0, concat_axis=0, tiled=True)
    held_count = arrived.shape[1]
    stacked = arrived.reshape(expert_count * held_count, feature_count)
    produced = expert_block(stacked, w_gate[0], w_up[0], w_down[0])
    produced = produced.reshape(expert_count, held_count, feature_count)
    result_rows = lax.all_to_all(
        produced.astype(jnp.bfloat16), "expert", split_axis=0, concat_axis=0, tiled=True
    )
    picked = jnp.take(result_rows.reshape(slot_total, result_rows.shape[2]), slot_index, axis=0)
    weighted = gate_weights[:, :, None] * picked.reshape(row_count, top_count, -1).astype(
        jnp.float32
    )
    combined = jnp.sum(weighted, axis=1)
    combined = lax.psum_scatter(
        combined.astype(jnp.bfloat16), "tensor", scatter_dimension=1, tiled=True
    ).astype(jnp.float32)
    return hidden_columns + combined


def solution(mesh):
    in_specs = (
        P(("group", "expert"), None),
        P("tensor", ("group", "expert"), None),
        P(),
        P(("group", "expert"), None),
        P(("group", "expert"), None),
        P("expert", None, "tensor"),
        P("expert", None, "tensor"),
        P("expert", "tensor", None),
    )
    out_specs = P(("group", "expert"), "tensor")
    return jax.shard_map(local, mesh=mesh, in_specs=in_specs, out_specs=out_specs, check_vma=False)
```

profile of v0, /device:TPU:0, one launch (start us, length us, event | category | flops | bytes accessed | tf_op | source)
XLA Modules:
  0.0 129.4 jit_solution(4328106526848287153)
XLA Ops:
  6.5 0.7 all-reduce.2.cloned.1.call-update
  7.3 0.8 copy.23
  8.0 0.1 reshape.84
  8.2 0.1 reduce_window_sum.11
  8.3 0.2 select_reduce_fusion
  8.5 0.1 reduce_sum.32
  8.7 0.7 compare_and_fusion
  9.4 0.1 fusion.14
  9.5 34.8 %all-reduce.2.cloned.1.call-done = bf16[32,3584]{1,0:T(8,128)(2,1)} async-done(((bf16[32,3584]{1,0:T(8,128)(2,1)}), bf16[32,3584]{1,0:T(8,128)(2,1)}) %all-reduce.2.cloned.1.call-update) | async-done | bytes 229392 | tf_op jit(solution)/shard_map/psum | solution.py:27
  44.2 1.2 multiply_reduce_fusion.1
  45.5 0.8 copy-done.1
  46.3 1.1 convolution_convert_fusion.1
  47.4 0.2 reshape.85
  47.5 21.3 %all_to_all.10 = bf16[4,17,3584]{2,1,0:T(8,128)(2,1)S(1)} all-to-all(bf16[4,17,3584]{2,1,0:T(8,128)(2,1)S(1)} %reshape.85), channel_id=1, replica_groups=mesh['group'=2,'expert'=4,'tensor'=4] {'expert'}, dimensions={0} | all-to-all | bytes 974848 | tf_op jit(solution)/shard_map/all_to_all | solution.py:48
  68.8 0.2 reshape.86
  69.0 2.1 %fusion.3 = f32[68,256]{1,0:T(8,128)S(1)} fusion(bf16[68,3584]{1,0:T(8,128)(2,1)S(1)} %reshape.86, bf16[1,3584,256]{2,1,0:T(8,128)(2,1)} %param.13), kind=kOutput, calls=%fused_computation.6 | convolution fusion | flops 124780544 | bytes 2392064 | tf_op jit(solution)/shard_map/dot_general | solution.py:13
  71.1 0.5 fusion.8
  71.6 1.3 %convolution_convert_fusion = bf16[4,17,3584]{2,1,0:T(8,128)(2,1)} fusion(bf16[4,17,256]{2,1,0:T(8,128)(2,1)S(1)} %dot_general.17, bf16[1,256,3584]{2,1,0:T(8,128)(2,1)S(1)} %copy-done), kind=kOutput, calls=%fused_computation.1 | convolution fusion | flops 125024256 | bytes 2357248 | tf_op jit(solution)/shard_map/dot_general | solution.py:16
  72.9 3.5 %all-to-all-start.1 = ((bf16[4,17,3584]{2,1,0:T(8,128)(2,1)}), bf16[4,17,3584]{2,1,0:T(8,128)(2,1)S(1)}, u32[]{:S(2)}, u32[]{:S(2)}) async-start(bf16[4,17,3584]{2,1,0:T(8,128)(2,1)} %convolution_convert_fusion), calls=%async_computation.1 | async-start | bytes 1376256 | tf_op jit(solution)/shard_map/all_to_all | solution.py:53
  76.4 0.1 copy.26
  76.5 0.1 mul.75
  76.6 0.1 copy.25
  76.8 0.1 copy.22
  76.9 16.4 %all-to-all-done.1 = bf16[4,17,3584]{2,1,0:T(8,128)(2,1)S(1)} async-done(((bf16[4,17,3584]{2,1,0:T(8,128)(2,1)}), bf16[4,17,3584]{2,1,0:T(8,128)(2,1)S(1)}, u32[]{:S(2)}, u32[]{:S(2)}) %all-to-all-start.1) | async-done | bytes 487456 | tf_op jit(solution)/shard_map/all_to_all | solution.py:53
  93.3 0.2 reshape.87
  93.5 0.8 gather_fusion
  94.3 0.2 gather.7
  94.5 1.5 %multiply_reduce_fusion = bf16[32,3584]{1,0:T(8,128)(2,1)S(1)} fusion(bf16[32,2,3584]{2,1,0:T(2,128)(2,1)S(1)} %gather.7, pred[32,2]{1,0:T(8,128)(4,1)S(1)} %copy.25, f32[32,2]{1,0:T(8,128)S(1)} %copy.22), kind=kLoop, calls=%fused_computation.10 | loop fusion | flops 802816 | bytes 688448 | tf_op jit(solution)/shard_map/reduce_sum | solution.py:60
  96.0 1.2 copy.27
  97.3 22.6 %reduce-scatter.4.cloned.1.call-done = bf16[896,32]{1,0:T(8,128)(2,1)} async-done(((bf16[3584,32]{1,0:T(8,128)(2,1)}), bf16[896,32]{1,0:T(8,128)(2,1)}) %reduce-scatter.4.cloned.1.call-update) | async-done | bytes 57360
  119.9 1.1 copy.28
  121.0 1.6 %convert_add_fusion.1 = f32[32,896]{1,0:T(8,128)} fusion(bf16[32,896]{1,0:T(8,128)(2,1)S(1)} %copy.28, f32[32,3584]{1,0:T(8,128)} %copy-done.1, s32[]{:T(128)S(6)} %select_n.25), kind=kLoop, calls=%fused_computation.17 | loop fusion | flops 57344 | bytes 286724 | tf_op jit(solution)/shard_map/add | solution.py:64
  (19 shorter events, 0.3 us)
Async XLA Ops:
  6.5 65.0 %copy-start = (bf16[1,256,3584]{2,1,0:T(8,128)(2,1)S(1)}, bf16[1,256,3584]{2,1,0:T(8,128)(2,1)}, u32[]{:S(2)}) copy-start(bf16[1,256,3584]{2,1,0:T(8,128)(2,1)} %param.15) | copy-start | bytes 5505028
  6.5 37.7 %all-reduce.2.cloned.1.call-start = ((), (), s32[]{:S(2)}) async-start(), calls=%async_computation.3 | async-start | bytes 458752 | tf_op jit(solution)/shard_map/psum | solution.py:27
  45.5 0.8 copy-start.1
  69.0 2.1 %copy-start.2 = (bf16[1,3584,256]{2,1,0:T(8,128)(2,1)S(1)}, bf16[1,3584,256]{2,1,0:T(8,128)(2,1)}, u32[]{:S(2)}) copy-start(bf16[1,3584,256]{2,1,0:T(8,128)(2,1)} %param.14) | copy-start | bytes 5505028
  71.6 4.9 %copy-start.3 = (s32[32,2]{0,1:T(2,128)S(1)}, s32[32,2]{0,1:T(2,128)}, u32[]{:S(2)}) copy-start(s32[32,2]{0,1:T(2,128)} %param.11) | copy-start | bytes 772
  71.6 5.2 %copy-start.4 = (f32[32,2]{0,1:T(2,128)S(1)}, f32[32,2]{0,1:T(2,128)}, u32[]{:S(2)}) copy-start(f32[32,2]{0,1:T(2,128)} %param.12) | copy-start | bytes 772
  72.9 20.4 %all-to-all-start.1 = ((bf16[4,17,3584]{2,1,0:T(8,128)(2,1)}), bf16[4,17,3584]{2,1,0:T(8,128)(2,1)S(1)}, u32[]{:S(2)}, u32[]{:S(2)}) async-start(bf16[4,17,3584]{2,1,0:T(8,128)(2,1)} %convolution_convert_fusion), calls=%async_computation.1 | async-start | bytes 1376256 | tf_op jit(solution)/shard_map/all_to_all | solution.py:53
  76.4 43.5 %reduce-scatter.4.cloned.1.call-start = ((), (), s32[]{:S(2)}) async-start(), calls=%async_computation.4 | async-start | bytes 1146880
Sparse Core Ops, SparseCore 0:
  9.7 34.5 all-reduce.1
  97.4 22.4 reduce-scatter.3
where the time goes:
time: 130 us; the launch traced here: 129 us
  waiting for transfers between devices  74.6 us (57%)
  blocking collectives  21.3 us (16%)
  between operations  13.6 us (10%)
  local copies, waits for them, and re-layouts  6.03 us (5%)
  other arithmetic  5.48 us (4%)
  matrix products  4.9 us (4%)
  starting transfers between devices  3.53 us (3%)
    psum x1, waiting for transfers between devices, local(): lax.psum(partials.astype(jnp.bfloat16), 'tensor').astype(jnp.float32)  34.8 us
    unnamed x3, waiting for transfers between devices  23.4 us
    all_to_all x1, blocking collectives, local(): lax.all_to_all(outgoing, 'expert', split_axis=0, concat_axis=0, tiled=True)  21.3 us
    all_to_all x1, waiting for transfers between devices, local(): lax.all_to_all(produced.astype(jnp.bfloat16), 'expert', split_axis=0, con...  16.4 us
    unnamed x14, local copies, waits for them, and re-layouts  3.93 us
    all_to_all x1, starting transfers between devices, local(): lax.all_to_all(produced.astype(jnp.bfloat16), 'expert', split_axis=0, con...  3.48 us
  transfers between devices with their start and end apart: 3, of which 3 were waited for; matrix products, arithmetic and copies ran while one was open for 2% of the time, Pallas kernels for 0%

commit v1 on v0

v1 whole, which is shorter than its diff:
```python
import jax
import jax.numpy as jnp
from jax import lax
from jax.sharding import PartitionSpec as P

CAP = 17
EPSILON = 1e-06


def xor_permute(value, axis, step):
    count = lax.axis_size(axis)
    return lax.ppermute(value, axis, [(i, i ^ step) for i in range(count)])


def split_pair(value):
    high = value.astype(jnp.bfloat16)
    return high, (value - high.astype(jnp.float32)).astype(jnp.bfloat16)


def local(residual, attention_part, norm_gain, expert_ids, gate_weights, w_gate, w_up, w_down):
    rows, features = residual.shape
    tensor_count = lax.axis_size("tensor")
    expert_count = lax.axis_size("expert")
    tensor = lax.axis_index("tensor")
    expert = lax.axis_index("expert")
    quarter = features // tensor_count
    outer = tensor_count // 2
    side = tensor % 2

    def strips(value):
        shaped = value.reshape(value.shape[0], outer, 2, quarter)
        return lax.dynamic_index_in_dim(shaped, side, 2, keepdims=False)

    part = attention_part[0]
    near = xor_permute(part, "tensor", 1)
    chip = strips(part.astype(jnp.float32) + near.astype(jnp.float32))
    chip_sent = chip.astype(jnp.bfloat16)
    far = [xor_permute(chip_sent, "tensor", 2 * step) for step in range(1, outer)]

    relative = expert_ids ^ expert
    blocks = jnp.arange(expert_count, dtype=jnp.int32)
    chosen = relative[:, :, None] == blocks[None, None, :]
    named = jnp.any(chosen, axis=1)
    gates = jnp.sum(jnp.where(chosen, gate_weights[:, :, None], 0.0), axis=1)
    below = jnp.arange(rows)[:, None] > jnp.arange(rows)[None, :]
    position = jnp.dot(below.astype(jnp.bfloat16), named.astype(jnp.bfloat16), preferred_element_type=jnp.float32)
    slots = jnp.arange(CAP, dtype=jnp.float32)
    table = (position.T[:, None, :] == slots[None, :, None]) & named.T[:, None, :]
    mixing = jnp.where(table, gates.T[:, None, :], 0.0).reshape(expert_count * CAP, rows)
    table = table.astype(jnp.bfloat16)

    hidden = strips(residual) + chip
    for value in far:
        hidden = hidden + value.astype(jnp.float32)
    squares = jnp.sum(hidden * hidden, axis=(1, 2))
    high, low = split_pair(squares)
    extra = jnp.zeros((rows, 128), jnp.bfloat16).at[:, 0].set(high).at[:, 1].set(low)
    gained = (hidden * strips(norm_gain[None])).astype(jnp.bfloat16).reshape(rows, outer * quarter)
    sent = jnp.concatenate([gained, extra], axis=1)
    arrived = []
    for step in range(expert_count):
        block = jnp.dot(table[step], sent, preferred_element_type=jnp.float32).astype(jnp.bfloat16)
        arrived.append(xor_permute(block, "expert", step) if step else block)
    other = [xor_permute(block, "tensor", 1) for block in arrived]
    arrived, other = jnp.concatenate(arrived, axis=0), jnp.concatenate(other, axis=0)

    def columns(value):
        return value[:, : outer * quarter].reshape(-1, outer, quarter)

    first = jnp.where(side == 0, arrived, other)
    second = jnp.where(side == 0, other, arrived)
    inputs = jnp.stack([columns(first), columns(second)], axis=2).reshape(-1, features)
    tails = (arrived[:, outer * quarter :].astype(jnp.float32), other[:, outer * quarter :].astype(jnp.float32))
    total = tails[0][:, 0] + tails[0][:, 1] + tails[1][:, 0] + tails[1][:, 1]
    inverse = lax.rsqrt(total / features + EPSILON)[:, None]
    gated = jnp.dot(inputs, w_gate[0], preferred_element_type=jnp.float32) * inverse
    upward = jnp.dot(inputs, w_up[0], preferred_element_type=jnp.float32) * inverse
    active = (jax.nn.silu(gated) * upward).astype(jnp.bfloat16)
    produced = jnp.dot(active, w_down[0], preferred_element_type=jnp.float32)

    def own_columns(index):
        return lax.dynamic_slice_in_dim(produced, index * quarter, quarter, 1)

    reduced = own_columns(tensor)
    for step in range(1, tensor_count):
        piece = own_columns(tensor ^ step).astype(jnp.bfloat16)
        reduced = reduced + xor_permute(piece, "tensor", step).astype(jnp.float32)
    reduced = reduced.astype(jnp.bfloat16).reshape(expert_count, CAP, quarter)
    returned = [xor_permute(reduced[k], "expert", k) if k else reduced[k] for k in range(expert_count)]
    returned = jnp.concatenate(returned, axis=0)
    high, low = split_pair(mixing)
    dims = (((0,), (0,)), ((), ()))
    combined = lax.dot_general(high, returned, dims, preferred_element_type=jnp.float32)
    combined = combined + lax.dot_general(low, returned, dims, preferred_element_type=jnp.float32)
    return lax.dynamic_index_in_dim(hidden, tensor // 2, 1, keepdims=False) + combined


def solution(mesh):
    in_specs = (
        P(("group", "expert"), None),
        P("tensor", ("group", "expert"), None),
        P(),
        P(("group", "expert"), None),
        P(("group", "expert"), None),
        P("expert", None, "tensor"),
        P("expert", None, "tensor"),
        P("expert", "tensor", None),
    )
    out_specs = P(("group", "expert"), "tensor")
    return jax.shard_map(local, mesh=mesh, in_specs=in_specs, out_specs=out_specs, check_vma=False)
```

time: 130 us -> 57.5 us (0.44)
  waiting for transfers between devices: 74.6 us -> 20.5 us
  blocking collectives: 21.3 us -> 0 us
  between operations: 13.6 us -> 0.39 us
  starting transfers between devices: 3.53 us -> 14.9 us
  other arithmetic: 5.48 us -> 9.17 us
  matrix products: 4.9 us -> 6.38 us
    psum x1 -> x0, waiting for transfers between devices: 34.8 us -> none  [local(): lax.psum(partials.astype(jnp.bfloat16), 'tensor').astype(jnp.float32)]
    unnamed x3 -> x0, waiting for transfers between devices: 23.4 us -> none
    all_to_all x1 -> x0, blocking collectives: 21.3 us -> none  [local(): lax.all_to_all(outgoing, 'expert', split_axis=0, concat_axis=0, tiled=True)]
    ppermute x0 -> x15, waiting for transfers between devices: none -> 20.5 us  [xor_permute(): return lax.ppermute(value, axis, [(i, i ^ step) for i in range(count)])]
    all_to_all x1 -> x0, waiting for transfers between devices: 16.4 us -> none  [local(): lax.all_to_all(produced.astype(jnp.bfloat16), 'expert', split_axis=0, con...]
    ppermute x0 -> x15, starting transfers between devices: none -> 14.9 us  [xor_permute(): return lax.ppermute(value, axis, [(i, i ^ step) for i in range(count)])]
    another operation x1 -> x4, other arithmetic: 0.1 us -> 3.67 us  [local(): before = jnp.cumsum(onehot, axis=0) - onehot]
    all_to_all x1 -> x0, starting transfers between devices: 3.48 us -> none  [local(): lax.all_to_all(produced.astype(jnp.bfloat16), 'expert', split_axis=0, con...]
  transfers between devices with their start and end apart: 3 -> 15, of which waited for: 3 -> 9; matrix products, arithmetic and copies ran while one was open for 2% -> 10% of each run, Pallas kernels for 0% -> 0%
where the time goes in v1:
time: 57.5 us; the launch traced here: 57.1 us
  waiting for transfers between devices  20.5 us (36%)
  starting transfers between devices  14.9 us (26%)
  other arithmetic  9.17 us (16%)
  matrix products  6.38 us (11%)
  local copies, waits for them, and re-layouts  5.77 us (10%)
    ppermute x15, waiting for transfers between devices, xor_permute(): return lax.ppermute(value, axis, [(i, i ^ step) for i in range(count)])  20.5 us
    ppermute x15, starting transfers between devices, xor_permute(): return lax.ppermute(value, axis, [(i, i ^ step) for i in range(count)])  14.9 us
    dot_general x1, matrix products, local(): produced = jnp.dot(active, w_down[0], preferred_element_type=jnp.float32)  2.68 us
    another operation x3, other arithmetic  2.57 us
    dot_general x1, matrix products, local(): jnp.dot(inputs, w_gate[0], preferred_element_type=jnp.float32) * inverse  1.95 us
    reshape x2, local copies, waits for them, and re-layouts, strips(): shaped = value.reshape(value.shape[0], outer, 2, quarter)  1.62 us
  transfers between devices with their start and end apart: 15, of which 9 were waited for; matrix products, arithmetic and copies ran while one was open for 10% of the time, Pallas kernels for 0%

profile of v1, /device:TPU:0, one launch (start us, length us, event | category | flops | bytes accessed | tf_op | source)
XLA Modules:
  0.0 57.1 jit_solution(10530635903023134501)
XLA Ops:
  0.5 0.8 %broadcast_xor_fusion = s32[32,2]{0,1:T(2,128)S(1)} fusion(s32[32,2]{0,1:T(2,128)} %param.15, s32[]{:T(128)S(6)} %axis_index.25), kind=kLoop, calls=%fused_computation.78 | loop fusion | flops 64 | bytes 516 | tf_op jit(solution)/shard_map/xor | solution.py:40
  1.4 0.7 %reshape_broadcast_in_dim.3 = f32[1,2,2,896]{3,2,1,0:T(2,128)S(1)} reshape(f32[3584]{0:T(1024)} %param.14) | data formatting | bytes 28672 | tf_op jit(solution)/shard_map/reshape;broadcast_in_dim | solution.py:31
  2.2 1.3 %reshape.100 = f32[32,2,2,896]{3,2,1,0:T(2,128)S(1)} reshape(f32[32,3584]{1,0:T(8,128)} %param.12) | data formatting | bytes 917504 | tf_op jit(solution)/shard_map/reshape | solution.py:31
  3.5 0.7 %compare_reduce_fusion.1 = pred[]{:T(512)} fusion(), kind=kLoop, calls=%fused_computation.76 | loop fusion | flops 5 | bytes 1 | tf_op jit(solution)/shard_map/reduce.2
  4.2 0.6 %compare_reduce_fusion = pred[]{:T(512)} fusion(), kind=kLoop, calls=%fused_computation.75 | loop fusion | flops 5 | bytes 1 | tf_op jit(solution)/shard_map/reduce.3
  4.8 1.0 %convert_add_fusion = f32[32,3584]{1,0:T(8,128)S(1)} fusion(bf16[32,3584]{1,0:T(8,128)(2,1)S(1)} %collective-permute-done, bf16[1,32,3584]{2,1,0:T(8,128)(2,1)} %param.13), kind=kLoop, calls=%fused_computation.16 | loop fusion | flops 344064 | bytes 917504 | tf_op jit(solution)/shard_map/add | solution.py:36
  6.5 2.6 %collective-permute-start.1 = (bf16[32,2,896]{2,1,0:T(2,128)(2,1)S(1)}, bf16[32,2,896]{2,1,0:T(2,128)(2,1)S(1)}, u32[]{:S(2)}, u32[]{:S(2)}) collective-permute-start(bf16[32,2,896]{2,1,0:T(2,128)(2,1)S(1)} %bitcast.62), channel_id=1, source_target_pairs={{0,2},{1,3},{2,0},{3,1},{4,6},{5,7},{6,4},{7,5},{8,10},{9,11},{10,... | collective-permute-start | bytes 344072 | tf_op jit(solution)/shard_map/ppermute | solution.py:12
  9.3 3.5 %collective-permute-done.1 = bf16[32,2,896]{2,1,0:T(2,128)(2,1)S(1)} collective-permute-done((bf16[32,2,896]{2,1,0:T(2,128)(2,1)S(1)}, bf16[32,2,896]{2,1,0:T(2,128)(2,1)S(1)}, u32[]{:S(2)}, u32[]{:S(2)}) %collective-permute-start.1) | collective-permute-done | bytes 114720 | tf_op jit(solution)/shard_map/ppermute | solution.py:12
  13.1 0.7 %copy-done.1 = f32[32,2,896]{2,1,0:T(2,128)} copy-done((f32[32,2,896]{2,1,0:T(2,128)}, f32[32,2,896]{2,1,0:T(2,128)S(1)}, u32[]{:S(2)}) %copy-start.1) | copy-done | bytes 229400
  14.1 1.3 %fusion.36 = (bf16[32,1]{1,0:T(8,128)(2,1)S(1)}, bf16[32,1]{1,0:T(8,128)(2,1)S(1)}) fusion(f32[32,1]{1,0:T(8,128)S(1)} %copy.39, pred[]{:T(512)} %compare_reduce_fusion, pred[]{:T(512)} %compare_reduce_fusion.1), kind=kLoop, calls=%fused_computation.62 | loop fusion | flops 192 | bytes 258 | tf_op jit(solution)/shard_map/select.19
  16.1 3.9 %collective-permute-start.4 = (bf16[17,1920]{1,0:T(8,128)(2,1)S(1)}, bf16[17,1920]{1,0:T(8,128)(2,1)S(1)}, u32[]{:S(2)}, u32[]{:S(2)}) collective-permute-start(bf16[17,1920]{1,0:T(8,128)(2,1)S(1)} %convolution_convert_fusion), channel_id=1, source_target_pairs={{0,12},{4,8},{8,4},{12,0},{1,13},{5,9},{9,5},{13,1},{2,14},{6,10},... | collective-permute-start | bytes 195848 | tf_op jit(solution)/shard_map/ppermute | solution.py:12
  20.0 0.6 %collective-permute-start.2 = (bf16[17,1920]{1,0:T(8,128)(2,1)S(1)}, bf16[17,1920]{1,0:T(8,128)(2,1)S(1)}, u32[]{:S(2)}, u32[]{:S(2)}) collective-permute-start(bf16[17,1920]{1,0:T(8,128)(2,1)S(1)} %convolution_convert_fusion.2), channel_id=1, source_target_pairs={{0,4},{4,0},{8,12},{12,8},{1,5},{5,1},{9,13},{13,9},{2,6},{6,2},{1... | collective-permute-start | bytes 195848 | tf_op jit(solution)/shard_map/ppermute | solution.py:12
  20.9 2.5 %collective-permute-done.4 = bf16[17,1920]{1,0:T(8,128)(2,1)S(1)} collective-permute-done((bf16[17,1920]{1,0:T(8,128)(2,1)S(1)}, bf16[17,1920]{1,0:T(8,128)(2,1)S(1)}, u32[]{:S(2)}, u32[]{:S(2)}) %collective-permute-start.4) | collective-permute-done | bytes 65312 | tf_op jit(solution)/shard_map/ppermute | solution.py:12
  23.3 4.1 %collective-permute-done.3 = bf16[17,1920]{1,0:T(8,128)(2,1)S(1)} collective-permute-done((bf16[17,1920]{1,0:T(8,128)(2,1)S(1)}, bf16[17,1920]{1,0:T(8,128)(2,1)S(1)}, u32[]{:S(2)}, u32[]{:S(2)}) %collective-permute-start.3) | collective-permute-done | bytes 65312 | tf_op jit(solution)/shard_map/ppermute | solution.py:12
  27.5 0.6 %collective-permute-start.6 = (bf16[17,1920]{1,0:T(8,128)(2,1)S(1)}, bf16[17,1920]{1,0:T(8,128)(2,1)}, u32[]{:S(2)}, u32[]{:S(2)}) collective-permute-start(bf16[17,1920]{1,0:T(8,128)(2,1)S(1)} %collective-permute-done.2), channel_id=1, source_target_pairs={{0,1},{1,0},{2,3},{3,2},{4,5},{5,4},{6,7},{7,6},{8,9},{9,8},{10,11... | collective-permute-start | bytes 195848 | tf_op jit(solution)/shard_map/ppermute | solution.py:12
  28.1 0.6 %collective-permute-done.7 = bf16[17,1920]{1,0:T(8,128)(2,1)S(1)} collective-permute-done((bf16[17,1920]{1,0:T(8,128)(2,1)S(1)}, bf16[17,1920]{1,0:T(8,128)(2,1)S(1)}, u32[]{:S(2)}, u32[]{:S(2)}) %collective-permute-start.7) | collective-permute-done | bytes 65312 | tf_op jit(solution)/shard_map/ppermute | solution.py:12
  29.2 1.0 %pad_maximum_fusion.2 = bf16[68,1920]{1,0:T(8,128)(2,1)S(1)} fusion(bf16[17,1920]{1,0:T(8,128)(2,1)S(1)} %collective-permute-done.8, bf16[17,1920]{1,0:T(8,128)(2,1)S(1)} %collective-permute-done.7, bf16[17,1920]{1,0:T(8,128)(2,1)} %collective-permute-done.6, bf16[17,1920]{1,0:T(8,128)(2,1)S(1)} %collective-permute-done.5), kind=kLoop, calls=%fused_computation.18 | loop fusion | flops 1044480 | bytes 522240 | tf_op jit(solution)/shard_map/concatenate | solution.py:65
  30.4 1.1 %pad_maximum_fusion = bf16[68,2,2,896]{3,2,1,0:T(2,128)(2,1)S(1)} fusion(bf16[68,2,1,896]{3,2,1,0:T(2,128)(2,1)S(1)} %stack_reshape.9, bf16[68,2,1,896]{3,2,1,0:T(2,128)(2,1)S(1)} %stack_reshape.8), kind=kLoop, calls=%fused_computation.15 | loop fusion | flops 974848 | bytes 974848 | tf_op jit(solution)/shard_map/stack | solution.py:72
  31.9 0.7 %maximum_convert_fusion = f32[68,128]{1,0:T(8,128)S(1)} fusion(bf16[17,1920]{1,0:T(8,128)(2,1)S(1)} %collective-permute-done.8, bf16[17,1920]{1,0:T(8,128)(2,1)} %copy-done.3, bf16[17,1920]{1,0:T(8,128)(2,1)} %collective-permute-done.6, bf16[17,1920]{1,0:T(8,128)(2,1)S(1)} %collective-permute-done.5), kind=kLoop, calls=%fused_computation.51 | loop fusion | flops 69632 | bytes 295936 | tf_op jit(solution)/shard_map/convert_element_type | solution.py:73
  32.8 2.0 %fusion.6 = f32[68,256]{1,0:T(8,128)S(1)} fusion(bf16[68,3584]{1,0:T(8,128)(2,1)S(1)} %reshape.103, bf16[1,3584,256]{2,1,0:T(8,128)(2,1)} %param.17, f32[68]{0:T(128)S(1)} %fusion.32), kind=kOutput, calls=%fused_computation.11 | convolution fusion | flops 124797952 | bytes 2392336 | tf_op jit(solution)/shard_map/dot_general | solution.py:76
  34.8 2.7 %fusion = f32[68,3584]{1,0:T(8,128)S(1)} fusion(bf16[1,256,3584]{2,1,0:T(8,128)(2,1)S(1)} %copy-done, bf16[68,3584]{1,0:T(8,128)(2,1)S(1)} %reshape.103, bf16[1,3584,256]{2,1,0:T(8,128)(2,1)} %param.18, f32[68,256]{1,0:T(8,128)S(1)} %fusion.6, f32[68]{0:T(128)S(1)} %fusion.32), kind=kOutput, calls=%fused_computation.4 | convolution fusion | flops 249682944 | bytes 5202192 | tf_op jit(solution)/shard_map/dot_general | solution.py:79
  37.5 0.8 %dynamic-slice_convert_fusion.2 = (bf16[68,896]{1,0:T(8,128)(2,1)}, bf16[68,896]{1,0:T(8,128)(2,1)}, bf16[68,896]{1,0:T(8,128)(2,1)S(1)}) fusion(f32[68,3584]{1,0:T(8,128)S(1)} %fusion, s32[]{:T(128)S(6)} %select_n.65, s32[]{:T(128)S(6)} %select_n.67, s32[]{:T(128)S(6)} %select_n.66), kind=kLoop, calls=%fused_computation.22 | loop fusion | bytes 731148 | tf_op jit(solution)/shard_map/convert_element_type | solution.py:86
  38.6 1.2 %collective-permute-start.11 = (bf16[68,896]{1,0:T(8,128)(2,1)}, bf16[68,896]{1,0:T(8,128)(2,1)}, u32[]{:S(2)}, u32[]{:S(2)}) collective-permute-start(bf16[68,896]{1,0:T(8,128)(2,1)} %get-tuple-element.32), channel_id=1, source_target_pairs={{0,3},{1,2},{2,1},{3,0},{4,7},{5,6},{6,5},{7,4},{8,11},{9,10},{10,... | collective-permute-start | bytes 365576 | tf_op jit(solution)/shard_map/ppermute | solution.py:12
  39.8 0.6 collective-permute-start.10
  41.0 3.3 %collective-permute-done.11 = bf16[68,896]{1,0:T(8,128)(2,1)} collective-permute-done((bf16[68,896]{1,0:T(8,128)(2,1)}, bf16[68,896]{1,0:T(8,128)(2,1)}, u32[]{:S(2)}, u32[]{:S(2)}) %collective-permute-start.11) | collective-permute-done | bytes 121888 | tf_op jit(solution)/shard_map/ppermute | solution.py:12
  44.3 3.1 %collective-permute-done.10 = bf16[68,896]{1,0:T(8,128)(2,1)} collective-permute-done((bf16[68,896]{1,0:T(8,128)(2,1)S(1)}, bf16[68,896]{1,0:T(8,128)(2,1)}, u32[]{:S(2)}, u32[]{:S(2)}) %collective-permute-start.10) | collective-permute-done | bytes 121888 | tf_op jit(solution)/shard_map/ppermute | solution.py:12
  47.4 1.0 %add_convert_fusion = bf16[68,896]{1,0:T(8,128)(2,1)S(1)} fusion(bf16[68,896]{1,0:T(8,128)(2,1)} %collective-permute-done.11, bf16[68,896]{1,0:T(8,128)(2,1)} %collective-permute-done.10, bf16[68,896]{1,0:T(8,128)(2,1)S(1)} %collective-permute-done.9, f32[68,3584]{1,0:T(8,128)S(1)} %fusion, s32[]{:T(128)S(6)} %select_n.64), kind=kLoop, calls=%fused_computation.19 | loop fusion | flops 426496 | bytes 731140 | tf_op jit(solution)/shard_map/convert_element_type | solution.py:88
  48.5 2.6 %collective-permute-start.14 = (bf16[17,896]{1,0:T(8,128)(2,1)S(1)}, bf16[17,896]{1,0:T(8,128)(2,1)S(1)}, u32[]{:S(2)}, u32[]{:S(2)}) collective-permute-start(bf16[17,896]{1,0:T(8,128)(2,1)S(1)} %get-tuple-element.37), channel_id=1, source_target_pairs={{0,12},{4,8},{8,4},{12,0},{1,13},{5,9},{9,5},{13,1},{2,14},{6,10},... | collective-permute-start | bytes 91400 | tf_op jit(solution)/shard_map/ppermute | solution.py:12
  51.1 1.8 %collective-permute-start.12 = (bf16[17,896]{1,0:T(8,128)(2,1)S(1)}, bf16[17,896]{1,0:T(8,128)(2,1)S(1)}, u32[]{:S(2)}, u32[]{:S(2)}) collective-permute-start(bf16[17,896]{1,0:T(8,128)(2,1)S(1)} %get-tuple-element.39), channel_id=1, source_target_pairs={{0,4},{4,0},{8,12},{12,8},{1,5},{5,1},{9,13},{13,9},{2,6},{6,2},{1... | collective-permute-start | bytes 91400 | tf_op jit(solution)/shard_map/ppermute | solution.py:12
  53.1 1.3 %collective-permute-done.14 = bf16[17,896]{1,0:T(8,128)(2,1)S(1)} collective-permute-done((bf16[17,896]{1,0:T(8,128)(2,1)S(1)}, bf16[17,896]{1,0:T(8,128)(2,1)S(1)}, u32[]{:S(2)}, u32[]{:S(2)}) %collective-permute-start.14) | collective-permute-done | bytes 30496 | tf_op jit(solution)/shard_map/ppermute | solution.py:12
  54.4 1.7 %collective-permute-done.13 = bf16[17,896]{1,0:T(8,128)(2,1)S(1)} collective-permute-done((bf16[17,896]{1,0:T(8,128)(2,1)S(1)}, bf16[17,896]{1,0:T(8,128)(2,1)S(1)}, u32[]{:S(2)}, u32[]{:S(2)}) %collective-permute-start.13) | collective-permute-done | bytes 30496 | tf_op jit(solution)/shard_map/ppermute | solution.py:12
  56.3 0.8 %bitcast_add_fusion = f32[32,896]{1,0:T(8,128)} fusion(f32[32,1,896]{2,1,0:T(1,128)S(1)} %constant_dynamic-slice_fusion.1, f32[32,896]{1,0:T(8,128)S(1)} %fusion.37, f32[68,32]{0,1:T(8,128)S(1)} %broadcast_in_dim.40, pred[68,32]{0,1:T(32,128)(4,1)S(1)} %copy.44, f32[68,32]{0,1:T(8,128)S(1)} %copy.43, f32[68]{0:T(128)S(1)} %eq.49, ...), kind=kOutput, calls=%fused_computation.34 | convolution fusion | flops 4450688 | bytes 485776 | tf_op jit(solution)/shard_map/dot_general | solution.py:93
  (64 shorter events, 5.6 us)
Async XLA Ops:
  0.0 34.7 %copy-start = (bf16[1,256,3584]{2,1,0:T(8,128)(2,1)S(1)}, bf16[1,256,3584]{2,1,0:T(8,128)(2,1)}, u32[]{:S(2)}) copy-start(bf16[1,256,3584]{2,1,0:T(8,128)(2,1)} %param.19) | copy-start | bytes 5505028
  0.0 4.8 %collective-permute-start = (bf16[32,3584]{1,0:T(8,128)(2,1)}, bf16[32,3584]{1,0:T(8,128)(2,1)S(1)}, u32[]{:S(2)}, u32[]{:S(2)}) collective-permute-start(bf16[32,3584]{1,0:T(8,128)(2,1)} %bitcast.61), channel_id=1, source_target_pairs={{0,1},{1,0},{2,3},{3,2},{4,5},{5,4},{6,7},{7,6},{8,9},{9,8},{10,11... | collective-permute-start | bytes 688136 | tf_op jit(solution)/shard_map/ppermute | solution.py:12
  6.5 6.3 %collective-permute-start.1 = (bf16[32,2,896]{2,1,0:T(2,128)(2,1)S(1)}, bf16[32,2,896]{2,1,0:T(2,128)(2,1)S(1)}, u32[]{:S(2)}, u32[]{:S(2)}) collective-permute-start(bf16[32,2,896]{2,1,0:T(2,128)(2,1)S(1)} %bitcast.62), channel_id=1, source_target_pairs={{0,2},{1,3},{2,0},{3,1},{4,6},{5,7},{6,4},{7,5},{8,10},{9,11},{10,... | collective-permute-start | bytes 344072 | tf_op jit(solution)/shard_map/ppermute | solution.py:12
  13.0 0.7 %copy-start.1 = (f32[32,2,896]{2,1,0:T(2,128)}, f32[32,2,896]{2,1,0:T(2,128)S(1)}, u32[]{:S(2)}) copy-start(f32[32,2,896]{2,1,0:T(2,128)S(1)} %get-tuple-element.30) | copy-start | bytes 688132
  16.1 7.3 %collective-permute-start.4 = (bf16[17,1920]{1,0:T(8,128)(2,1)S(1)}, bf16[17,1920]{1,0:T(8,128)(2,1)S(1)}, u32[]{:S(2)}, u32[]{:S(2)}) collective-permute-start(bf16[17,1920]{1,0:T(8,128)(2,1)S(1)} %convolution_convert_fusion), channel_id=1, source_target_pairs={{0,12},{4,8},{8,4},{12,0},{1,13},{5,9},{9,5},{13,1},{2,14},{6,10},... | collective-permute-start | bytes 195848 | tf_op jit(solution)/shard_map/ppermute | solution.py:12
  20.0 7.5 %collective-permute-start.3 = (bf16[17,1920]{1,0:T(8,128)(2,1)S(1)}, bf16[17,1920]{1,0:T(8,128)(2,1)S(1)}, u32[]{:S(2)}, u32[]{:S(2)}) collective-permute-start(bf16[17,1920]{1,0:T(8,128)(2,1)S(1)} %convolution_convert_fusion.1), channel_id=1, source_target_pairs={{0,8},{4,12},{8,0},{12,4},{1,9},{5,13},{9,1},{13,5},{2,10},{6,14},... | collective-permute-start | bytes 195848 | tf_op jit(solution)/shard_map/ppermute | solution.py:12
  20.0 7.5 %collective-permute-start.2 = (bf16[17,1920]{1,0:T(8,128)(2,1)S(1)}, bf16[17,1920]{1,0:T(8,128)(2,1)S(1)}, u32[]{:S(2)}, u32[]{:S(2)}) collective-permute-start(bf16[17,1920]{1,0:T(8,128)(2,1)S(1)} %convolution_convert_fusion.2), channel_id=1, source_target_pairs={{0,4},{4,0},{8,12},{12,8},{1,5},{5,1},{9,13},{13,9},{2,6},{6,2},{1... | collective-permute-start | bytes 195848 | tf_op jit(solution)/shard_map/ppermute | solution.py:12
  20.8 7.4 %collective-permute-start.5 = (bf16[17,1920]{1,0:T(8,128)(2,1)S(1)}, bf16[17,1920]{1,0:T(8,128)(2,1)S(1)}, u32[]{:S(2)}, u32[]{:S(2)}) collective-permute-start(bf16[17,1920]{1,0:T(8,128)(2,1)S(1)} %convolution_convert_fusion.3), channel_id=1, source_target_pairs={{0,1},{1,0},{2,3},{3,2},{4,5},{5,4},{6,7},{7,6},{8,9},{9,8},{10,11... | collective-permute-start | bytes 195848 | tf_op jit(solution)/shard_map/ppermute | solution.py:12
  23.3 4.8 %collective-permute-start.8 = (bf16[17,1920]{1,0:T(8,128)(2,1)S(1)}, bf16[17,1920]{1,0:T(8,128)(2,1)S(1)}, u32[]{:S(2)}, u32[]{:S(2)}) collective-permute-start(bf16[17,1920]{1,0:T(8,128)(2,1)S(1)} %collective-permute-done.4), channel_id=1, source_target_pairs={{0,1},{1,0},{2,3},{3,2},{4,5},{5,4},{6,7},{7,6},{8,9},{9,8},{10,11... | collective-permute-start | bytes 195848 | tf_op jit(solution)/shard_map/ppermute | solution.py:12
  27.4 1.3 %collective-permute-start.7 = (bf16[17,1920]{1,0:T(8,128)(2,1)S(1)}, bf16[17,1920]{1,0:T(8,128)(2,1)S(1)}, u32[]{:S(2)}, u32[]{:S(2)}) collective-permute-start(bf16[17,1920]{1,0:T(8,128)(2,1)S(1)} %collective-permute-done.3), channel_id=1, source_target_pairs={{0,1},{1,0},{2,3},{3,2},{4,5},{5,4},{6,7},{7,6},{8,9},{9,8},{10,11... | collective-permute-start | bytes 195848 | tf_op jit(solution)/shard_map/ppermute | solution.py:12
  27.5 1.6 %collective-permute-start.6 = (bf16[17,1920]{1,0:T(8,128)(2,1)S(1)}, bf16[17,1920]{1,0:T(8,128)(2,1)}, u32[]{:S(2)}, u32[]{:S(2)}) collective-permute-start(bf16[17,1920]{1,0:T(8,128)(2,1)S(1)} %collective-permute-done.2), channel_id=1, source_target_pairs={{0,1},{1,0},{2,3},{3,2},{4,5},{5,4},{6,7},{7,6},{8,9},{9,8},{10,11... | collective-permute-start | bytes 195848 | tf_op jit(solution)/shard_map/ppermute | solution.py:12
  28.7 1.5 %copy-start.3 = (bf16[17,1920]{1,0:T(8,128)(2,1)}, bf16[17,1920]{1,0:T(8,128)(2,1)S(1)}, u32[]{:S(2)}) copy-start(bf16[17,1920]{1,0:T(8,128)(2,1)S(1)} %collective-permute-done.7) | copy-start | bytes 195844
  34.7 5.8 %copy-start.4 = (f32[32,2]{0,1:T(2,128)S(1)}, f32[32,2]{0,1:T(2,128)}, u32[]{:S(2)}) copy-start(f32[32,2]{0,1:T(2,128)} %param.16) | copy-start | bytes 772
  37.4 15.5 %copy-start.2 = (f32[32,2,896]{2,1,0:T(2,128)S(1)}, f32[32,2,896]{2,1,0:T(2,128)}, u32[]{:S(2)}) copy-start(f32[32,2,896]{2,1,0:T(2,128)} %copy-done.1) | copy-start | bytes 688132
  38.2 2.8 %collective-permute-start.9 = (bf16[68,896]{1,0:T(8,128)(2,1)}, bf16[68,896]{1,0:T(8,128)(2,1)S(1)}, u32[]{:S(2)}, u32[]{:S(2)}) collective-permute-start(bf16[68,896]{1,0:T(8,128)(2,1)} %get-tuple-element.31), channel_id=1, source_target_pairs={{0,1},{1,0},{2,3},{3,2},{4,5},{5,4},{6,7},{7,6},{8,9},{9,8},{10,11... | collective-permute-start | bytes 365576 | tf_op jit(solution)/shard_map/ppermute | solution.py:12
  38.6 5.7 %collective-permute-start.11 = (bf16[68,896]{1,0:T(8,128)(2,1)}, bf16[68,896]{1,0:T(8,128)(2,1)}, u32[]{:S(2)}, u32[]{:S(2)}) collective-permute-start(bf16[68,896]{1,0:T(8,128)(2,1)} %get-tuple-element.32), channel_id=1, source_target_pairs={{0,3},{1,2},{2,1},{3,0},{4,7},{5,6},{6,5},{7,4},{8,11},{9,10},{10,... | collective-permute-start | bytes 365576 | tf_op jit(solution)/shard_map/ppermute | solution.py:12
  39.8 7.6 %collective-permute-start.10 = (bf16[68,896]{1,0:T(8,128)(2,1)S(1)}, bf16[68,896]{1,0:T(8,128)(2,1)}, u32[]{:S(2)}, u32[]{:S(2)}) collective-permute-start(bf16[68,896]{1,0:T(8,128)(2,1)S(1)} %get-tuple-element.33), channel_id=1, source_target_pairs={{0,2},{1,3},{2,0},{3,1},{4,6},{5,7},{6,4},{7,5},{8,10},{9,11},{10,... | collective-permute-start | bytes 365576 | tf_op jit(solution)/shard_map/ppermute | solution.py:12
  48.5 5.9 %collective-permute-start.14 = (bf16[17,896]{1,0:T(8,128)(2,1)S(1)}, bf16[17,896]{1,0:T(8,128)(2,1)S(1)}, u32[]{:S(2)}, u32[]{:S(2)}) collective-permute-start(bf16[17,896]{1,0:T(8,128)(2,1)S(1)} %get-tuple-element.37), channel_id=1, source_target_pairs={{0,12},{4,8},{8,4},{12,0},{1,13},{5,9},{9,5},{13,1},{2,14},{6,10},... | collective-permute-start | bytes 91400 | tf_op jit(solution)/shard_map/ppermute | solution.py:12
  51.1 4.9 %collective-permute-start.13 = (bf16[17,896]{1,0:T(8,128)(2,1)S(1)}, bf16[17,896]{1,0:T(8,128)(2,1)S(1)}, u32[]{:S(2)}, u32[]{:S(2)}) collective-permute-start(bf16[17,896]{1,0:T(8,128)(2,1)S(1)} %get-tuple-element.38), channel_id=1, source_target_pairs={{0,8},{4,12},{8,0},{12,4},{1,9},{5,13},{9,1},{13,5},{2,10},{6,14},... | collective-permute-start | bytes 91400 | tf_op jit(solution)/shard_map/ppermute | solution.py:12
  51.1 4.9 %collective-permute-start.12 = (bf16[17,896]{1,0:T(8,128)(2,1)S(1)}, bf16[17,896]{1,0:T(8,128)(2,1)S(1)}, u32[]{:S(2)}, u32[]{:S(2)}) collective-permute-start(bf16[17,896]{1,0:T(8,128)(2,1)S(1)} %get-tuple-element.39), channel_id=1, source_target_pairs={{0,4},{4,0},{8,12},{12,8},{1,5},{5,1},{9,13},{13,9},{2,6},{6,2},{1... | collective-permute-start | bytes 91400 | tf_op jit(solution)/shard_map/ppermute | solution.py:12

commit v2 on v1

--- a/solution.py
+++ b/solution.py
@@ -1,10 +1,18 @@
+import functools
+
 import jax
 import jax.numpy as jnp
 from jax import lax
+from jax.experimental import pallas as pl
+from jax.experimental.pallas import tpu as pltpu
 from jax.sharding import PartitionSpec as P
 
 CAP = 17
 EPSILON = 1e-06
+LANES = 128
+MAIN = 16
+FLOPS = 4 << 30
+BF16, F32 = jnp.bfloat16, jnp.float32
 
 
 def xor_permute(value, axis, step):
@@ -17,7 +25,281 @@
     return high, (value - high.astype(jnp.float32)).astype(jnp.bfloat16)
 
 
-def local(residual, attention_part, norm_gain, expert_ids, gate_weights, w_gate, w_up, w_down):
+def call(kernel, outs, *args, scratch=(), vmem=8 << 20, flops=FLOPS, name=None):
+    vmem_spec = pl.BlockSpec(memory_space=pltpu.VMEM)
+    moved = sum(a.size * a.dtype.itemsize for a in (*args, *outs))
+    return pl.pallas_call(
+        kernel,
+        out_shape=tuple(outs),
+        in_specs=[vmem_spec] * len(args),
+        out_specs=(vmem_spec,) * len(outs),
+        scratch_shapes=list(scratch),
+        compiler_params=pltpu.CompilerParams(vmem_limit_bytes=vmem),
+        cost_estimate=pl.CostEstimate(flops=flops, bytes_accessed=moved, transcendentals=0),
+        name=name,
+    )(*args)
+
+
+def out(shape, dtype):
+    return jax.ShapeDtypeStruct(shape, dtype)
+
+
+def iota(shape, dim):
+    return lax.broadcasted_iota(jnp.int32, shape, dim)
+
+
+def onehot(mask):
+    return jnp.where(mask, 1.0, 0.0)
+
+
+def dot(left, right, contract=((1,), (0,))):
+    return lax.dot_general(left, right, (contract, ((), ())), preferred_element_type=F32)
+
+
+def strip(index, quarter):
+    return pl.ds(pl.multiple_of(index * quarter, LANES), quarter)
+
+
+def constant_kernel(rows, before_ref, spread_ref):
+    before_ref[...] = onehot(iota((rows, rows), 0) < iota((rows, rows), 1)).astype(BF16)
+    shape = spread_ref.shape
+    spread_ref[...] = onehot(iota(shape, 0) == iota(shape, 1) % rows).astype(BF16)
+
+
+def table_kernel(experts, rows, chunks, before_ref, spread_ref, ids_ref, gates_ref, table_ref, tails_ref, high_ref, low_ref):
+    expert = lax.axis_index("expert")
+    relative = ids_ref[...] ^ expert
+    gates = gates_ref[...]
+    kinds = iota((8, rows), 0)
+    named, gate = jnp.zeros((8, rows), jnp.bool_), jnp.zeros((8, rows), F32)
+    for choice in range(relative.shape[0]):
+        hit = relative[choice : choice + 1] == kinds
+        named = named | hit
+        gate = gate + jnp.where(hit, gates[choice : choice + 1], 0.0)
+    position = dot(onehot(named).astype(BF16), before_ref[...])
+    position = jnp.where(named, position, -1.0)
+    slot = iota((MAIN, rows), 0).astype(F32)
+    pieces = [onehot(position[k : k + 1] == slot) for k in range(experts)]
+    tail = onehot(position == float(MAIN))
+    rest = table_ref.shape[0] - experts * MAIN - 8
+    table = jnp.concatenate([*pieces, tail, jnp.zeros((rest, rows), F32)], axis=0)
+    table_ref[...] = table.astype(BF16)
+    wide = jnp.concatenate([jnp.broadcast_to(tail[k : k + 1], (MAIN, rows)) for k in range(experts)], axis=0)
+    spread = dot(wide.astype(BF16), spread_ref[...])
+    shape = (experts * MAIN, rows * chunks)
+    tails_ref[...] = jnp.where(iota(shape, 0) % MAIN == iota(shape, 1) // rows, spread, 0.0).astype(BF16)
+    for k in range(experts):
+        last = jnp.where(iota((8, rows), 0) == k, tail, 0.0)
+        mixing = jnp.concatenate([pieces[k], last], axis=0) * gate[k : k + 1]
+        high, low = split_pair(mixing)
+        high_ref[k], low_ref[k] = high, low
+
+
+def chip_kernel(quarter, part_ref, near_ref, after_ref, chip_ref, sent_ref):
+    del after_ref
+    side = lax.axis_index("tensor") % 2
+    for o in range(2):
+        columns = strip(2 * o + side, quarter)
+        total = part_ref[:, columns].astype(F32) + near_ref[:, columns].astype(F32)
+        chip_ref[:, o * quarter : (o + 1) * quarter] = total
+        sent_ref[:, o * quarter : (o + 1) * quarter] = total.astype(BF16)
+
+
+def dispatch_kernel(quarter, experts, residual_ref, chip_ref, far_ref, gain_ref, table_ref, tails_ref, hidden_ref, *block_refs):
+    tensor = lax.axis_index("tensor")
+    side = tensor % 2
+    rows = chip_ref.shape[0]
+    squares = jnp.zeros((rows, 1), F32)
+    gained = []
+    for o in range(2):
+        here = slice(o * quarter, (o + 1) * quarter)
+        columns = strip(2 * o + side, quarter)
+        hidden = residual_ref[:, columns] + chip_ref[:, here] + far_ref[:, here].astype(F32)
+        squares = squares + jnp.sum(hidden * hidden, axis=1, keepdims=True)
+        gained.append((hidden * gain_ref[:, columns]).astype(BF16))
+
+        @pl.when(o == tensor // 2)
+        def _():
+            hidden_ref[...] = hidden
+
+    table = table_ref[...]
+    main = table[: experts * MAIN]
+    lanes = jnp.sum(jnp.where(iota((rows, rows), 0) == iota((rows, rows), 1), squares, 0.0), axis=0, keepdims=True)
+    high = lanes.astype(BF16).astype(F32)
+    pick = iota((MAIN, rows), 0)
+    pair = jnp.where(pick == 0, high, jnp.where(pick == 1, lanes - high, 0.0)).astype(BF16)
+    slots = dot(pair, table, ((1,), (1,)))
+    for o in range(2):
+        picked = dot(main, gained[o]).astype(BF16)
+        for k in range(experts):
+            block_refs[k][:, o * quarter : (o + 1) * quarter] = picked[k * MAIN : (k + 1) * MAIN]
+    parts = [g[:, i * LANES : (i + 1) * LANES] for g in gained for i in range(quarter // LANES)]
+    tile = dot(tails_ref[...], jnp.concatenate(parts, axis=0))
+    row = iota(tile.shape, 0) % MAIN
+    tile = jnp.where(row == MAIN - 2, slots[0:1], jnp.where(row == MAIN - 1, slots[1:2], tile)).astype(BF16)
+    for k in range(experts):
+        block_refs[k][:, 2 * quarter :] = tile[k * MAIN : (k + 1) * MAIN]
+
+
+def pack_kernel(experts, *refs):
+    for ref, k in zip(refs, reversed(range(experts))):
+        refs[-1][k * MAIN : (k + 1) * MAIN] = ref[...]
+
+
+def project(quarter, experts, ref, which, gate_ref, up_ref):
+    chunks = 2 * quarter // LANES
+    shape = (chunks * MAIN, experts * MAIN)
+    block = iota(shape, 0) % MAIN
+    spread = onehot((iota(shape, 1) == block * MAIN + iota(shape, 0) // MAIN) & (block < experts)).astype(BF16)
+    last = dot(spread, ref[:, 2 * quarter :]).astype(BF16)
+    gated = upward = 0.0
+    per = quarter // LANES
+    for o in range(2):
+        tails = jnp.concatenate([last[j * MAIN : (j + 1) * MAIN] for j in range(o * per, (o + 1) * per)], axis=1)
+        inputs = jnp.concatenate([ref[:, o * quarter : (o + 1) * quarter], tails], axis=0)
+        here = strip(2 * o + which, quarter)
+        gated = gated + dot(inputs, gate_ref[0, here, :])
+        upward = upward + dot(inputs, up_ref[0, here, :])
+    return gated, upward
+
+
+def own_kernel(quarter, experts, own_ref, gate_ref, up_ref, gated_ref, upward_ref):
+    side = lax.axis_index("tensor") % 2
+    gated_ref[...], upward_ref[...] = project(quarter, experts, own_ref, side, gate_ref, up_ref)
+
+
+def other_kernel(
+    quarter, experts, own_ref, other_ref, gated_ref, upward_ref, gate_ref, up_ref, down_ref, active_ref, sent_ref
+):
+    side = lax.axis_index("tensor") % 2
+    main, features = experts * MAIN, 4 * quarter
+    lane = iota((1, LANES), 1)
+    total = jnp.zeros((1, LANES), F32)
+    for ref in (own_ref, other_ref):
+        for k in range(experts):
+            pair = ref[k * MAIN : (k + 1) * MAIN, 2 * quarter :].astype(F32)
+            value = pair[MAIN - 2 : MAIN - 1] + pair[MAIN - 1 : MAIN]
+            total = total + jnp.where((lane // MAIN == k) | (lane == main + k), value, 0.0)
+    gated, upward = project(quarter, experts, other_ref, 1 - side, gate_ref, up_ref)
+    gated, upward = gated + gated_ref[...], upward + upward_ref[...]
+    shape = (gated.shape[0], LANES)
+    column = jnp.sum(jnp.where(iota(shape, 0) == iota(shape, 1), total, 0.0), axis=1, keepdims=True)
+    inverse = lax.rsqrt(column / features + EPSILON)
+    gated, upward = gated * inverse, upward * inverse
+    active = (gated / (1.0 + jnp.exp(-gated)) * upward).astype(BF16)
+    active_ref[...] = active
+    for o in range(2):
+        value = dot(active, down_ref[0, :, strip(2 * o + 1 - side, quarter)]).astype(BF16)
+        sent_ref[:, o * quarter : (o + 1) * quarter] = value[: sent_ref.shape[0]]
+
+
+def kept_kernel(quarter, active_ref, down_ref, kept_ref):
+    side = lax.axis_index("tensor") % 2
+    for o in range(2):
+        value = dot(active_ref[...], down_ref[0, :, strip(2 * o + side, quarter)]).astype(BF16)
+        kept_ref[:, o * quarter : (o + 1) * quarter] = value[: kept_ref.shape[0]]
+
+
+def near_kernel(quarter, kept_ref, near_ref, own_ref, sent_ref):
+    o = lax.axis_index("tensor") // 2
+    for ref, index in ((own_ref, o), (sent_ref, 1 - o)):
+        columns = strip(index, quarter)
+        ref[...] = (kept_ref[:, columns].astype(F32) + near_ref[:, columns].astype(F32)).astype(ref.dtype)
+
+
+def far_kernel(experts, own_ref, far_ref, *block_refs):
+    total = own_ref[...] + far_ref[...].astype(F32)
+    main = experts * MAIN
+    for k in range(experts):
+        block = jnp.concatenate([total[k * MAIN : (k + 1) * MAIN], total[main : main + 8]], axis=0)
+        block_refs[k][...] = block.astype(BF16)
+
+
+def combine_kernel(experts, hidden_ref, high_ref, low_ref, *refs):
+    total = hidden_ref[...]
+    for ref, k in zip(refs, reversed(range(experts))):
+        value = ref[...]
+        total = total + dot(high_ref[k], value, ((0,), (0,))) + dot(low_ref[k], value, ((0,), (0,)))
+    refs[-1][...] = total
+
+
+def local_kernels(residual, attention_part, norm_gain, expert_ids, gate_weights, w_gate, w_up, w_down):
+    rows, features = residual.shape
+    experts = lax.axis_size("expert")
+    quarter = features // 4
+    width = 2 * quarter
+    chunks = width // LANES
+    steps = range(1, experts)
+    part = attention_part[0]
+    near = xor_permute(part, "tensor", 1)
+    before, spread = call(
+        functools.partial(constant_kernel, rows), (out((rows, rows), BF16), out((rows, rows * chunks), BF16))
+    )
+    mix = out((experts, MAIN + 8, rows), BF16)
+    table, tails, high, low = call(
+        functools.partial(table_kernel, experts, rows, chunks),
+        (out((LANES, rows), BF16), out((experts * MAIN, rows * chunks), BF16), mix, mix),
+        before,
+        spread,
+        expert_ids.T,
+        gate_weights.T,
+    )
+    chip, chip_sent = call(
+        functools.partial(chip_kernel, quarter), (out((rows, width), F32), out((rows, width), BF16)), part, near, high
+    )
+    far = xor_permute(chip_sent, "tensor", 2)
+    block = out((MAIN, width + LANES), BF16)
+    hidden, *blocks = call(
+        functools.partial(dispatch_kernel, quarter, experts),
+        (out((rows, quarter), F32), *[block] * experts),
+        residual,
+        chip,
+        far,
+        norm_gain[None],
+        table,
+        tails,
+    )
+    arrived = [*[xor_permute(blocks[k], "expert", k) for k in reversed(steps)], blocks[0]]
+    packed = out((experts * MAIN, width + LANES), BF16)
+    (arrived,) = call(functools.partial(pack_kernel, experts), (packed,), *arrived, flops=0)
+    other = xor_permute(arrived, "tensor", 1)
+    used, slots = experts * MAIN + 8, (experts + 1) * MAIN
+    hidden_count = w_gate.shape[2]
+    sums = out((slots, hidden_count), F32)
+    gated, upward = call(functools.partial(own_kernel, quarter, experts), (sums, sums), arrived, w_gate, w_up)
+    active, sent = call(
+        functools.partial(other_kernel, quarter, experts),
+        (out((slots, hidden_count), BF16), out((used, width), BF16)),
+        arrived,
+        other,
+        gated,
+        upward,
+        w_gate,
+        w_up,
+        w_down,
+    )
+    (kept,) = call(functools.partial(kept_kernel, quarter), (out((used, width), BF16),), active, w_down)
+    near = xor_permute(sent, "tensor", 1)
+    own, sent = call(
+        functools.partial(near_kernel, quarter), (out((used, quarter), F32), out((used, quarter), BF16)), kept, near
+    )
+    far = xor_permute(sent, "tensor", 2)
+    blocks = call(functools.partial(far_kernel, experts), [out((MAIN + 8, quarter), BF16)] * experts, own, far)
+    blocks = [*[xor_permute(blocks[k], "expert", k) for k in reversed(steps)], blocks[0]]
+    (result,) = call(functools.partial(combine_kernel, experts), (out((rows, quarter), F32),), hidden, high, low, *blocks)
+    return result
+
+
+def local(residual, *others):
+    rows, features = residual.shape
+    fits = lax.axis_size("tensor") == 4 and lax.axis_size("expert") == 4 and rows % 16 == 0 and rows <= LANES
+    quarter = features // 4
+    if fits and quarter % LANES == 0 and 2 * quarter // LANES <= MAIN - 2:
+        return local_kernels(residual, *others)
+    return local_general(residual, *others)
+
+
+def local_general(residual, attention_part, norm_gain, expert_ids, gate_weights, w_gate, w_up, w_down):
     rows, features = residual.shape
     tensor_count = lax.axis_size("tensor")
     expert_count = lax.axis_size("expert")

time: 57.5 us -> 36 us (0.63)
  other arithmetic: 9.17 us -> 0 us
  matrix products: 6.38 us -> 0 us
  local copies, waits for them, and re-layouts: 5.77 us -> 0.26 us
  Pallas kernels: 0 us -> 3.42 us
  waiting for transfers between devices: 20.5 us -> 17.9 us
  starting transfers between devices: 14.9 us -> 14.2 us
    dot_general x9 -> x0, matrix products: 6.38 us -> none  [the longest x1 2.68 us: local(): produced = jnp.dot(active, w_down[0], preferred_element_type=jnp.float32)]
    another operation x4 -> x0, other arithmetic: 3.67 us -> none
    pallas_call x0 -> x11, Pallas kernels: none -> 3.42 us  [call(): pl.pallas_call(kernel, out_shape=tuple(outs), in_specs=[vmem_spec] * len(...]
    ppermute x15 -> x11, waiting for transfers between devices: 20.5 us -> 17.9 us  [xor_permute(): return lax.ppermute(value, axis, [(i, i ^ step) for i in range(count)])]
    convert_element_type x4 -> x0, other arithmetic: 2.05 us -> none  [the longest x1 1.03 us: local(): reduced = reduced.astype(jnp.bfloat16).reshape(expert_count, CAP, quarter)]
    reshape x3 -> x0, local copies, waits for them, and re-layouts: 1.94 us -> none  [the longest x2 1.62 us: strips(): shaped = value.reshape(value.shape[0], outer, 2, quarter)]
    concatenate x2 -> x0, other arithmetic: 1.08 us -> none  [the longest x1 0.99 us: local(): jnp.concatenate(other, axis=0)]
    add x1 -> x0, other arithmetic: 0.99 us -> none  [local(): chip = strips(part.astype(jnp.float32) + near.astype(jnp.float32))]
  transfers between devices with their start and end apart: 15 -> 11, of which waited for: 9 -> 9; matrix products, arithmetic and copies ran while one was open for 10% -> 0% of each run, Pallas kernels for 0% -> 3%
where the time goes in v2:
time: 36 us; the launch traced here: 35.9 us
  waiting for transfers between devices  17.9 us (50%)
  starting transfers between devices  14.2 us (39%)
  Pallas kernels  3.42 us (10%)
    ppermute x11, waiting for transfers between devices, xor_permute(): return lax.ppermute(value, axis, [(i, i ^ step) for i in range(count)])  17.9 us
    ppermute x11, starting transfers between devices, xor_permute(): return lax.ppermute(value, axis, [(i, i ^ step) for i in range(count)])  14.2 us
    pallas_call x11, Pallas kernels, call(): pl.pallas_call(kernel, out_shape=tuple(outs), in_specs=[vmem_spec] * len(...  3.42 us
  transfers between devices with their start and end apart: 11, of which 9 were waited for; matrix products, arithmetic and copies ran while one was open for 0% of the time, Pallas kernels for 3%

profile of v2, /device:TPU:0, one launch (start us, length us, event | category | flops | bytes accessed | tf_op | source)
XLA Modules:
  0.0 35.9 jit_solution(3508892363326652348)
XLA Ops:
  0.0 0.5 %collective-permute-start = (bf16[32,3584]{1,0:T(8,128)(2,1)}, bf16[32,3584]{1,0:T(8,128)(2,1)S(1)}, u32[]{:S(2)}, u32[]{:S(2)}) collective-permute-start(bf16[32,3584]{1,0:T(8,128)(2,1)} %bitcast.3), channel_id=1, source_target_pairs={{0,1},{1,0},{2,3},{3,2},{4,5},{5,4},{6,7},{7,6},{8,9},{9,8},{10,11... | collective-permute-start | bytes 688136 | tf_op jit(solution)/shard_map/ppermute | solution.py:20
  0.5 0.2 copy-done.5
  0.7 0.0 copy-done.6
  0.7 0.3 shard_map.83
  1.0 0.8 %collective-permute-done.near_ref = bf16[32,3584]{1,0:T(8,128)(2,1)S(1)} collective-permute-done((bf16[32,3584]{1,0:T(8,128)(2,1)}, bf16[32,3584]{1,0:T(8,128)(2,1)S(1)}, u32[]{:S(2)}, u32[]{:S(2)}) %collective-permute-start) | collective-permute-done | bytes 229408 | tf_op jit(solution)/shard_map/ppermute | solution.py:20
  1.8 2.9 %collective-permute-start.1 = (bf16[32,1792]{1,0:T(8,128)(2,1)S(1)}, bf16[32,1792]{1,0:T(8,128)(2,1)S(1)}, u32[]{:S(2)}, u32[]{:S(2)}) collective-permute-start(bf16[32,1792]{1,0:T(8,128)(2,1)S(1)} %get-tuple-element.32), channel_id=1, source_target_pairs={{0,2},{1,3},{2,0},{3,1},{4,6},{5,7},{6,4},{7,5},{8,10},{9,11},{10,... | collective-permute-start | bytes 344072 | tf_op jit(solution)/shard_map/ppermute | solution.py:20
  4.8 3.4 %collective-permute-done.1.far_ref = bf16[32,1792]{1,0:T(8,128)(2,1)S(1)} collective-permute-done((bf16[32,1792]{1,0:T(8,128)(2,1)S(1)}, bf16[32,1792]{1,0:T(8,128)(2,1)S(1)}, u32[]{:S(2)}, u32[]{:S(2)}) %collective-permute-start.1) | collective-permute-done | bytes 114720 | tf_op jit(solution)/shard_map/ppermute | solution.py:20
  8.2 0.5 %shard_map.85 = (f32[32,896]{1,0:T(8,128)S(1)}, bf16[16,1920]{1,0:T(8,128)(2,1)S(1)}, bf16[16,1920]{1,0:T(8,128)(2,1)S(1)}, bf16[16,1920]{1,0:T(8,128)(2,1)S(1)}, bf16[16,1920]{1,0:T(8,128)(2,1)S(1)}) custom-call(f32[32,3584]{1,0:T(8,128)S(1)} %copy-done.3, f32[32,1792]{1,0:T(8,128)S(1)} %get-tuple-element.31.chip_ref, ...), custom_call_target="tpu_custom_call" | custom-call | flops 4294967296 | bytes 1243136 | tf_op jit(solution)/shard_map/pallas_call | solution.py:31
  8.7 3.9 %collective-permute-start.2 = (bf16[16,1920]{1,0:T(8,128)(2,1)S(1)}, bf16[16,1920]{1,0:T(8,128)(2,1)S(1)}, u32[]{:S(2)}, u32[]{:S(2)}) collective-permute-start(bf16[16,1920]{1,0:T(8,128)(2,1)S(1)} %get-tuple-element.37), channel_id=1, source_target_pairs={{0,12},{4,8},{8,4},{12,0},{1,13},{5,9},{9,5},{13,1},{2,14},{6,10},... | collective-permute-start | bytes 184328 | tf_op jit(solution)/shard_map/ppermute | solution.py:20
  12.6 0.0 collective-permute-start.3
  12.6 0.6 %collective-permute-start.4 = (bf16[16,1920]{1,0:T(8,128)(2,1)S(1)}, bf16[16,1920]{1,0:T(8,128)(2,1)S(1)}, u32[]{:S(2)}, u32[]{:S(2)}) collective-permute-start(bf16[16,1920]{1,0:T(8,128)(2,1)S(1)} %get-tuple-element.39), channel_id=1, source_target_pairs={{0,4},{4,0},{8,12},{12,8},{1,5},{5,1},{9,13},{13,9},{2,6},{6,2},{1... | collective-permute-start | bytes 184328 | tf_op jit(solution)/shard_map/ppermute | solution.py:20
  13.2 2.3 %collective-permute-done.2.refs_0_ = bf16[16,1920]{1,0:T(8,128)(2,1)S(1)} collective-permute-done((bf16[16,1920]{1,0:T(8,128)(2,1)S(1)}, bf16[16,1920]{1,0:T(8,128)(2,1)S(1)}, u32[]{:S(2)}, u32[]{:S(2)}) %collective-permute-start.2) | collective-permute-done | bytes 61472 | tf_op jit(solution)/shard_map/ppermute | solution.py:20
  15.5 2.2 %collective-permute-done.3.refs_1_ = bf16[16,1920]{1,0:T(8,128)(2,1)S(1)} collective-permute-done((bf16[16,1920]{1,0:T(8,128)(2,1)S(1)}, bf16[16,1920]{1,0:T(8,128)(2,1)S(1)}, u32[]{:S(2)}, u32[]{:S(2)}) %collective-permute-start.3) | collective-permute-done | bytes 61472 | tf_op jit(solution)/shard_map/ppermute | solution.py:20
  17.7 0.0 collective-permute-done.4.refs_2_
  17.7 0.0 copy-start.2
  17.8 0.1 collective-permute-start.5
  17.9 0.5 %shard_map.87 = (f32[80,256]{1,0:T(8,128)S(1)}, f32[80,256]{1,0:T(8,128)S(1)}) custom-call(bf16[64,1920]{1,0:T(8,128)(2,1)S(1)} %shard_map.86.own_ref, bf16[1,3584,256]{2,1,0:T(8,128)(2,1)S(1)} %copy-done, bf16[1,3584,256]{2,1,0:T(8,128)(2,1)S(1)} %copy-done.1), custom_call_target="tpu_custom_call" | custom-call | flops 4294967296 | bytes 4079616 | tf_op jit(solution)/shard_map/pallas_call | solution.py:31
  18.4 1.0 %collective-permute-done.5.other_ref = bf16[64,1920]{1,0:T(8,128)(2,1)S(1)} collective-permute-done((bf16[64,1920]{1,0:T(8,128)(2,1)S(1)}, bf16[64,1920]{1,0:T(8,128)(2,1)S(1)}, u32[]{:S(2)}, u32[]{:S(2)}) %collective-permute-start.5) | collective-permute-done | bytes 245792 | tf_op jit(solution)/shard_map/ppermute | solution.py:20
  19.3 0.8 %shard_map.88 = (bf16[80,256]{1,0:T(8,128)(2,1)S(1)}, bf16[72,1792]{1,0:T(8,128)(2,1)S(1)}) custom-call(bf16[64,1920]{1,0:T(8,128)(2,1)S(1)} %shard_map.86.own_ref, bf16[64,1920]{1,0:T(8,128)(2,1)S(1)} %collective-permute-done.5.other_ref, f32[80,256]{1,0:T(8,128)S(1)} %get-tuple-element.41.gated_ref, f32[80,256]{1,0:T(8,128)S(1)} %get-tuple-element.42.upward_ref, ...), custom_call_target="tpu_custom_call" | custom-call | flops 4294967296 | bytes 6459392 | tf_op jit(solution)/shard_map/pallas_call | solution.py:31
  20.1 0.2 collective-permute-start.6
  20.3 0.3 shard_map.89.kept_ref
  20.6 1.1 %collective-permute-done.6.near_ref = bf16[72,1792]{1,0:T(8,128)(2,1)S(1)} collective-permute-done((bf16[72,1792]{1,0:T(8,128)(2,1)S(1)}, bf16[72,1792]{1,0:T(8,128)(2,1)S(1)}, u32[]{:S(2)}, u32[]{:S(2)}) %collective-permute-start.6) | collective-permute-done | bytes 258080 | tf_op jit(solution)/shard_map/ppermute | solution.py:20
  21.7 0.1 shard_map.90
  21.8 1.6 %collective-permute-start.7 = (bf16[72,896]{1,0:T(8,128)(2,1)S(1)}, bf16[72,896]{1,0:T(8,128)(2,1)S(1)}, u32[]{:S(2)}, u32[]{:S(2)}) collective-permute-start(bf16[72,896]{1,0:T(8,128)(2,1)S(1)} %get-tuple-element.46), channel_id=1, source_target_pairs={{0,2},{1,3},{2,0},{3,1},{4,6},{5,7},{6,4},{7,5},{8,10},{9,11},{10,... | collective-permute-start | bytes 387080 | tf_op jit(solution)/shard_map/ppermute | solution.py:20
  23.4 4.0 %collective-permute-done.7.far_ref = bf16[72,896]{1,0:T(8,128)(2,1)S(1)} collective-permute-done((bf16[72,896]{1,0:T(8,128)(2,1)S(1)}, bf16[72,896]{1,0:T(8,128)(2,1)S(1)}, u32[]{:S(2)}, u32[]{:S(2)}) %collective-permute-start.7) | collective-permute-done | bytes 129056 | tf_op jit(solution)/shard_map/ppermute | solution.py:20
  27.4 2.4 %collective-permute-start.8 = (bf16[24,896]{1,0:T(8,128)(2,1)S(1)}, bf16[24,896]{1,0:T(8,128)(2,1)S(1)}, u32[]{:S(2)}, u32[]{:S(2)}) collective-permute-start(bf16[24,896]{1,0:T(8,128)(2,1)S(1)} %get-tuple-element.47), channel_id=1, source_target_pairs={{0,12},{4,8},{8,4},{12,0},{1,13},{5,9},{9,5},{13,1},{2,14},{6,10},... | collective-permute-start | bytes 129032 | tf_op jit(solution)/shard_map/ppermute | solution.py:20
  29.8 0.0 collective-permute-start.9
  29.8 2.0 %collective-permute-start.10 = (bf16[24,896]{1,0:T(8,128)(2,1)S(1)}, bf16[24,896]{1,0:T(8,128)(2,1)S(1)}, u32[]{:S(2)}, u32[]{:S(2)}) collective-permute-start(bf16[24,896]{1,0:T(8,128)(2,1)S(1)} %get-tuple-element.49), channel_id=1, source_target_pairs={{0,4},{4,0},{8,12},{12,8},{1,5},{5,1},{9,13},{13,9},{2,6},{6,2},{1... | collective-permute-start | bytes 129032 | tf_op jit(solution)/shard_map/ppermute | solution.py:20
  31.8 1.4 %collective-permute-done.8.refs_0_ = bf16[24,896]{1,0:T(8,128)(2,1)S(1)} collective-permute-done((bf16[24,896]{1,0:T(8,128)(2,1)S(1)}, bf16[24,896]{1,0:T(8,128)(2,1)S(1)}, u32[]{:S(2)}, u32[]{:S(2)}) %collective-permute-start.8) | collective-permute-done | bytes 43040 | tf_op jit(solution)/shard_map/ppermute | solution.py:20
  33.3 1.6 %collective-permute-done.9.refs_1_ = bf16[24,896]{1,0:T(8,128)(2,1)S(1)} collective-permute-done((bf16[24,896]{1,0:T(8,128)(2,1)S(1)}, bf16[24,896]{1,0:T(8,128)(2,1)S(1)}, u32[]{:S(2)}, u32[]{:S(2)}) %collective-permute-start.9) | collective-permute-done | bytes 43040 | tf_op jit(solution)/shard_map/ppermute | solution.py:20
  34.9 0.0 collective-permute-done.10.refs_2_
  34.9 1.0 %shard_map.92 = f32[32,896]{1,0:T(8,128)} custom-call(f32[32,896]{1,0:T(8,128)S(1)} %get-tuple-element.35.hidden_ref, bf16[4,24,32]{2,1,0:T(8,128)(2,1)S(1)} %get-tuple-element.30.after_ref.high_ref, bf16[4,24,32]{2,1,0:T(8,128)(2,1)S(1)} %get-tuple-element.36.low_ref, bf16[24,896]{1,0:T(8,128)(2,1)S(1)} %collective-permute-done.8.refs_0_, ...), custom_call_target="tpu_custom_call" | custom-call | flops 4294967296 | bytes 413696 | tf_op jit(solution)/shard_map/pallas_call | solution.py:31
  (18 shorter events, 0.1 us)
Async XLA Ops:
  0.0 0.7 %copy-start.5 = (s32[32,2]{0,1:T(2,128)S(1)}, s32[32,2]{0,1:T(2,128)}, u32[]{:S(2)}) copy-start(s32[32,2]{0,1:T(2,128)} %param.11) | copy-start | bytes 772
  0.0 0.7 %copy-start.6 = (f32[32,2]{0,1:T(2,128)S(1)}, f32[32,2]{0,1:T(2,128)}, u32[]{:S(2)}) copy-start(f32[32,2]{0,1:T(2,128)} %param.12) | copy-start | bytes 772
  0.0 1.8 %collective-permute-start = (bf16[32,3584]{1,0:T(8,128)(2,1)}, bf16[32,3584]{1,0:T(8,128)(2,1)S(1)}, u32[]{:S(2)}, u32[]{:S(2)}) collective-permute-start(bf16[32,3584]{1,0:T(8,128)(2,1)} %bitcast.3), channel_id=1, source_target_pairs={{0,1},{1,0},{2,3},{3,2},{4,5},{5,4},{6,7},{7,6},{8,9},{9,8},{10,11... | collective-permute-start | bytes 688136 | tf_op jit(solution)/shard_map/ppermute | solution.py:20
  0.7 1.1 %copy-start.4 = (bf16[1,32,3584]{2,1,0:T(8,128)(2,1)S(1)}, bf16[1,32,3584]{2,1,0:T(8,128)(2,1)}, u32[]{:S(2)}) copy-start(bf16[1,32,3584]{2,1,0:T(8,128)(2,1)} %param.9) | copy-start | bytes 688132
  1.8 3.0 %copy-start.7 = (f32[3584]{0:T(1024)S(1)}, f32[3584]{0:T(1024)}, u32[]{:S(2)}) copy-start(f32[3584]{0:T(1024)} %param.10) | copy-start | bytes 43012
  1.8 6.4 %copy-start.3 = (f32[32,3584]{1,0:T(8,128)S(1)}, f32[32,3584]{1,0:T(8,128)}, u32[]{:S(2)}) copy-start(f32[32,3584]{1,0:T(8,128)} %residual_ref.1) | copy-start | bytes 1376260
  1.8 6.4 %collective-permute-start.1 = (bf16[32,1792]{1,0:T(8,128)(2,1)S(1)}, bf16[32,1792]{1,0:T(8,128)(2,1)S(1)}, u32[]{:S(2)}, u32[]{:S(2)}) collective-permute-start(bf16[32,1792]{1,0:T(8,128)(2,1)S(1)} %get-tuple-element.32), channel_id=1, source_target_pairs={{0,2},{1,3},{2,0},{3,1},{4,6},{5,7},{6,4},{7,5},{8,10},{9,11},{10,... | collective-permute-start | bytes 344072 | tf_op jit(solution)/shard_map/ppermute | solution.py:20
  8.2 9.6 %copy-start = (bf16[1,3584,256]{2,1,0:T(8,128)(2,1)S(1)}, bf16[1,3584,256]{2,1,0:T(8,128)(2,1)}, u32[]{:S(2)}) copy-start(bf16[1,3584,256]{2,1,0:T(8,128)(2,1)} %gate_ref.3) | copy-start | bytes 5505028
  8.2 9.6 %copy-start.1 = (bf16[1,3584,256]{2,1,0:T(8,128)(2,1)S(1)}, bf16[1,3584,256]{2,1,0:T(8,128)(2,1)}, u32[]{:S(2)}) copy-start(bf16[1,3584,256]{2,1,0:T(8,128)(2,1)} %up_ref.3) | copy-start | bytes 5505028
  8.7 6.9 %collective-permute-start.2 = (bf16[16,1920]{1,0:T(8,128)(2,1)S(1)}, bf16[16,1920]{1,0:T(8,128)(2,1)S(1)}, u32[]{:S(2)}, u32[]{:S(2)}) collective-permute-start(bf16[16,1920]{1,0:T(8,128)(2,1)S(1)} %get-tuple-element.37), channel_id=1, source_target_pairs={{0,12},{4,8},{8,4},{12,0},{1,13},{5,9},{9,5},{13,1},{2,14},{6,10},... | collective-permute-start | bytes 184328 | tf_op jit(solution)/shard_map/ppermute | solution.py:20
  12.6 5.1 %collective-permute-start.3 = (bf16[16,1920]{1,0:T(8,128)(2,1)S(1)}, bf16[16,1920]{1,0:T(8,128)(2,1)S(1)}, u32[]{:S(2)}, u32[]{:S(2)}) collective-permute-start(bf16[16,1920]{1,0:T(8,128)(2,1)S(1)} %get-tuple-element.38), channel_id=1, source_target_pairs={{0,8},{4,12},{8,0},{12,4},{1,9},{5,13},{9,1},{13,5},{2,10},{6,14},... | collective-permute-start | bytes 184328 | tf_op jit(solution)/shard_map/ppermute | solution.py:20
  12.6 5.1 %collective-permute-start.4 = (bf16[16,1920]{1,0:T(8,128)(2,1)S(1)}, bf16[16,1920]{1,0:T(8,128)(2,1)S(1)}, u32[]{:S(2)}, u32[]{:S(2)}) collective-permute-start(bf16[16,1920]{1,0:T(8,128)(2,1)S(1)} %get-tuple-element.39), channel_id=1, source_target_pairs={{0,4},{4,0},{8,12},{12,8},{1,5},{5,1},{9,13},{13,9},{2,6},{6,2},{1... | collective-permute-start | bytes 184328 | tf_op jit(solution)/shard_map/ppermute | solution.py:20
  17.7 1.6 %copy-start.2 = (bf16[1,256,3584]{2,1,0:T(8,128)(2,1)S(1)}, bf16[1,256,3584]{2,1,0:T(8,128)(2,1)}, u32[]{:S(2)}) copy-start(bf16[1,256,3584]{2,1,0:T(8,128)(2,1)} %down_ref.3) | copy-start | bytes 5505028
  17.8 1.6 %collective-permute-start.5 = (bf16[64,1920]{1,0:T(8,128)(2,1)S(1)}, bf16[64,1920]{1,0:T(8,128)(2,1)S(1)}, u32[]{:S(2)}, u32[]{:S(2)}) collective-permute-start(bf16[64,1920]{1,0:T(8,128)(2,1)S(1)} %shard_map.86.own_ref), channel_id=1, source_target_pairs={{0,1},{1,0},{2,3},{3,2},{4,5},{5,4},{6,7},{7,6},{8,9},{9,8},{10,11... | collective-permute-start | bytes 737288 | tf_op jit(solution)/shard_map/ppermute | solution.py:20
  20.1 1.6 %collective-permute-start.6 = (bf16[72,1792]{1,0:T(8,128)(2,1)S(1)}, bf16[72,1792]{1,0:T(8,128)(2,1)S(1)}, u32[]{:S(2)}, u32[]{:S(2)}) collective-permute-start(bf16[72,1792]{1,0:T(8,128)(2,1)S(1)} %get-tuple-element.44), channel_id=1, source_target_pairs={{0,1},{1,0},{2,3},{3,2},{4,5},{5,4},{6,7},{7,6},{8,9},{9,8},{10,11... | collective-permute-start | bytes 774152 | tf_op jit(solution)/shard_map/ppermute | solution.py:20
  21.8 5.6 %collective-permute-start.7 = (bf16[72,896]{1,0:T(8,128)(2,1)S(1)}, bf16[72,896]{1,0:T(8,128)(2,1)S(1)}, u32[]{:S(2)}, u32[]{:S(2)}) collective-permute-start(bf16[72,896]{1,0:T(8,128)(2,1)S(1)} %get-tuple-element.46), channel_id=1, source_target_pairs={{0,2},{1,3},{2,0},{3,1},{4,6},{5,7},{6,4},{7,5},{8,10},{9,11},{10,... | collective-permute-start | bytes 387080 | tf_op jit(solution)/shard_map/ppermute | solution.py:20
  27.4 5.9 %collective-permute-start.8 = (bf16[24,896]{1,0:T(8,128)(2,1)S(1)}, bf16[24,896]{1,0:T(8,128)(2,1)S(1)}, u32[]{:S(2)}, u32[]{:S(2)}) collective-permute-start(bf16[24,896]{1,0:T(8,128)(2,1)S(1)} %get-tuple-element.47), channel_id=1, source_target_pairs={{0,12},{4,8},{8,4},{12,0},{1,13},{5,9},{9,5},{13,1},{2,14},{6,10},... | collective-permute-start | bytes 129032 | tf_op jit(solution)/shard_map/ppermute | solution.py:20
  29.8 5.1 %collective-permute-start.9 = (bf16[24,896]{1,0:T(8,128)(2,1)S(1)}, bf16[24,896]{1,0:T(8,128)(2,1)S(1)}, u32[]{:S(2)}, u32[]{:S(2)}) collective-permute-start(bf16[24,896]{1,0:T(8,128)(2,1)S(1)} %get-tuple-element.48), channel_id=1, source_target_pairs={{0,8},{4,12},{8,0},{12,4},{1,9},{5,13},{9,1},{13,5},{2,10},{6,14},... | collective-permute-start | bytes 129032 | tf_op jit(solution)/shard_map/ppermute | solution.py:20
  29.8 5.1 %collective-permute-start.10 = (bf16[24,896]{1,0:T(8,128)(2,1)S(1)}, bf16[24,896]{1,0:T(8,128)(2,1)S(1)}, u32[]{:S(2)}, u32[]{:S(2)}) collective-permute-start(bf16[24,896]{1,0:T(8,128)(2,1)S(1)} %get-tuple-element.49), channel_id=1, source_target_pairs={{0,4},{4,0},{8,12},{12,8},{1,5},{5,1},{9,13},{13,9},{2,6},{6,2},{1... | collective-permute-start | bytes 129032 | tf_op jit(solution)/shard_map/ppermute | solution.py:20

commit v3 on v2

--- a/solution.py
+++ b/solution.py
@@ -66,7 +66,7 @@
     spread_ref[...] = onehot(iota(shape, 0) == iota(shape, 1) % rows).astype(BF16)
 
 
-def table_kernel(experts, rows, chunks, before_ref, spread_ref, ids_ref, gates_ref, table_ref, tails_ref, high_ref, low_ref):
+def table_kernel(experts, rows, chunks, before_ref, spread_ref, ids_ref, gates_ref, table_ref, tails_ref, mixing_ref):
     expert = lax.axis_index("expert")
     relative = ids_ref[...] ^ expert
     gates = gates_ref[...]
@@ -88,11 +88,10 @@
     spread = dot(wide.astype(BF16), spread_ref[...])
     shape = (experts * MAIN, rows * chunks)
     tails_ref[...] = jnp.where(iota(shape, 0) % MAIN == iota(shape, 1) // rows, spread, 0.0).astype(BF16)
-    for k in range(experts):
-        last = jnp.where(iota((8, rows), 0) == k, tail, 0.0)
-        mixing = jnp.concatenate([pieces[k], last], axis=0) * gate[k : k + 1]
-        high, low = split_pair(mixing)
-        high_ref[k], low_ref[k] = high, low
+    weighed = [pieces[k] * gate[k : k + 1] for k in range(experts)]
+    mixing = jnp.concatenate([*weighed, tail * gate, jnp.zeros((rest, rows), F32)], axis=0).T
+    high, low = split_pair(mixing)
+    mixing_ref[...] = jnp.concatenate([high, low], axis=0)
 
 
 def chip_kernel(quarter, part_ref, near_ref, after_ref, chip_ref, sent_ref):
@@ -146,16 +145,36 @@
         refs[-1][k * MAIN : (k + 1) * MAIN] = ref[...]
 
 
+def unpack(tiles, chunks):
+    tiles = [tile.astype(F32) for tile in tiles]
+    row = iota((8, LANES), 0)
+    parts = []
+    for j in range(chunks):
+        part = jnp.zeros((8, LANES), F32)
+        for k, tile in enumerate(tiles):
+            part = jnp.where(row == k, tile[j : j + 1], part)
+        parts.append(jnp.concatenate([part, jnp.zeros((MAIN - 8, LANES), F32)], axis=0).astype(BF16))
+    return parts
+
+
+def pack(last, experts):
+    row = iota((8, LANES), 0)
+    tiles = []
+    for k in range(experts):
+        tile = jnp.zeros((8, LANES), F32)
+        for j in range(last.shape[1] // LANES):
+            tile = jnp.where(row == j, last[k : k + 1, j * LANES : (j + 1) * LANES], tile)
+        tiles += [tile, jnp.zeros((MAIN - 8, LANES), F32)]
+    return jnp.concatenate(tiles, axis=0)
+
+
 def project(quarter, experts, ref, which, gate_ref, up_ref):
-    chunks = 2 * quarter // LANES
-    shape = (chunks * MAIN, experts * MAIN)
-    block = iota(shape, 0) % MAIN
-    spread = onehot((iota(shape, 1) == block * MAIN + iota(shape, 0) // MAIN) & (block < experts)).astype(BF16)
-    last = dot(spread, ref[:, 2 * quarter :]).astype(BF16)
+    tiles = [ref[k * MAIN : (k + 1) * MAIN, 2 * quarter :] for k in range(experts)]
+    last = unpack(tiles, 2 * quarter // LANES)
     gated = upward = 0.0
     per = quarter // LANES
     for o in range(2):
-        tails = jnp.concatenate([last[j * MAIN : (j + 1) * MAIN] for j in range(o * per, (o + 1) * per)], axis=1)
+        tails = jnp.concatenate(last[o * per : (o + 1) * per], axis=1)
         inputs = jnp.concatenate([ref[:, o * quarter : (o + 1) * quarter], tails], axis=0)
         here = strip(2 * o + which, quarter)
         gated = gated + dot(inputs, gate_ref[0, here, :])
@@ -188,39 +207,48 @@
     gated, upward = gated * inverse, upward * inverse
     active = (gated / (1.0 + jnp.exp(-gated)) * upward).astype(BF16)
     active_ref[...] = active
+    produce(quarter, active, down_ref, 1 - side, sent_ref)
+
+
+def produce(quarter, active, down_ref, which, ref):
     for o in range(2):
-        value = dot(active, down_ref[0, :, strip(2 * o + 1 - side, quarter)]).astype(BF16)
-        sent_ref[:, o * quarter : (o + 1) * quarter] = value[: sent_ref.shape[0]]
+        value = dot(active, down_ref[0, :, strip(2 * o + which, quarter)]).astype(BF16)
+        ref[:, o * quarter : (o + 1) * quarter] = value[: ref.shape[0]]
 
 
 def kept_kernel(quarter, active_ref, down_ref, kept_ref):
-    side = lax.axis_index("tensor") % 2
-    for o in range(2):
-        value = dot(active_ref[...], down_ref[0, :, strip(2 * o + side, quarter)]).astype(BF16)
-        kept_ref[:, o * quarter : (o + 1) * quarter] = value[: kept_ref.shape[0]]
-
-
-def near_kernel(quarter, kept_ref, near_ref, own_ref, sent_ref):
+    produce(quarter, active_ref[...], down_ref, lax.axis_index("tensor") % 2, kept_ref)
+
+
+def near_kernel(quarter, experts, kept_ref, near_ref, own_ref, far_ref, rest_ref):
     o = lax.axis_index("tensor") // 2
-    for ref, index in ((own_ref, o), (sent_ref, 1 - o)):
+    main, rest = experts * MAIN, rest_ref.shape[0]
+
+    def total(index):
         columns = strip(index, quarter)
-        ref[...] = (kept_ref[:, columns].astype(F32) + near_ref[:, columns].astype(F32)).astype(ref.dtype)
-
-
-def far_kernel(experts, own_ref, far_ref, *block_refs):
-    total = own_ref[...] + far_ref[...].astype(F32)
-    main = experts * MAIN
-    for k in range(experts):
-        block = jnp.concatenate([total[k * MAIN : (k + 1) * MAIN], total[main : main + 8]], axis=0)
-        block_refs[k][...] = block.astype(BF16)
-
-
-def combine_kernel(experts, hidden_ref, high_ref, low_ref, *refs):
-    total = hidden_ref[...]
-    for ref, k in zip(refs, reversed(range(experts))):
-        value = ref[...]
-        total = total + dot(high_ref[k], value, ((0,), (0,))) + dot(low_ref[k], value, ((0,), (0,)))
-    refs[-1][...] = total
+        value = kept_ref[:, columns].astype(F32) + near_ref[:, columns].astype(F32)
+        return value[:main], pack(value[main:], experts)
+
+    value, tiles = total(1 - o)
+    value, tiles = value.astype(BF16), tiles.astype(BF16)
+    far_ref[:, :quarter], far_ref[:, quarter:] = value[rest:], tiles[rest:]
+    rest_ref[:, :quarter], rest_ref[:, quarter:] = value[:rest], tiles[:rest]
+    own_ref[:, :quarter], own_ref[:, quarter:] = total(o)
+
+
+def far_kernel(start, own_ref, far_ref, *block_refs):
+    for i, ref in enumerate(block_refs):
+        here = slice(start + i * MAIN, start + (i + 1) * MAIN)
+        ref[...] = (own_ref[here] + far_ref[i * MAIN : (i + 1) * MAIN].astype(F32)).astype(BF16)
+
+
+def combine_kernel(experts, quarter, hidden_ref, mixing_ref, *refs):
+    rows = hidden_ref.shape[0]
+    blocks = [ref[...] for ref in refs[:experts]][::-1]
+    last = jnp.concatenate(unpack([block[:, quarter:] for block in blocks], quarter // LANES), axis=1)
+    slots = jnp.concatenate([*[block[:, :quarter] for block in blocks], last], axis=0)
+    both = dot(mixing_ref[:, : slots.shape[0]], slots)
+    refs[-1][...] = hidden_ref[...] + both[:rows] + both[rows:]
 
 
 def local_kernels(residual, attention_part, norm_gain, expert_ids, gate_weights, w_gate, w_up, w_down):
@@ -235,17 +263,16 @@
     before, spread = call(
         functools.partial(constant_kernel, rows), (out((rows, rows), BF16), out((rows, rows * chunks), BF16))
     )
-    mix = out((experts, MAIN + 8, rows), BF16)
-    table, tails, high, low = call(
+    table, tails, mixing = call(
         functools.partial(table_kernel, experts, rows, chunks),
-        (out((LANES, rows), BF16), out((experts * MAIN, rows * chunks), BF16), mix, mix),
+        (out((LANES, rows), BF16), out((experts * MAIN, rows * chunks), BF16), out((2 * rows, LANES), BF16)),
         before,
         spread,
         expert_ids.T,
         gate_weights.T,
     )
     chip, chip_sent = call(
-        functools.partial(chip_kernel, quarter), (out((rows, width), F32), out((rows, width), BF16)), part, near, high
+        functools.partial(chip_kernel, quarter), (out((rows, width), F32), out((rows, width), BF16)), part, near, mixing
     )
     far = xor_permute(chip_sent, "tensor", 2)
     block = out((MAIN, width + LANES), BF16)
@@ -263,7 +290,8 @@
     packed = out((experts * MAIN, width + LANES), BF16)
     (arrived,) = call(functools.partial(pack_kernel, experts), (packed,), *arrived, flops=0)
     other = xor_permute(arrived, "tensor", 1)
-    used, slots = experts * MAIN + 8, (experts + 1) * MAIN
+    main, slots = experts * MAIN, (experts + 1) * MAIN
+    packed_width, used = quarter + LANES, main + 8
     hidden_count = w_gate.shape[2]
     sums = out((slots, hidden_count), F32)
     gated, upward = call(functools.partial(own_kernel, quarter, experts), (sums, sums), arrived, w_gate, w_up)
@@ -280,13 +308,22 @@
     )
     (kept,) = call(functools.partial(kept_kernel, quarter), (out((used, width), BF16),), active, w_down)
     near = xor_permute(sent, "tensor", 1)
-    own, sent = call(
-        functools.partial(near_kernel, quarter), (out((used, quarter), F32), out((used, quarter), BF16)), kept, near
-    )
-    far = xor_permute(sent, "tensor", 2)
-    blocks = call(functools.partial(far_kernel, experts), [out((MAIN + 8, quarter), BF16)] * experts, own, far)
+    early = 2
+    rest = main - early * MAIN
+    own, far, others = call(
+        functools.partial(near_kernel, quarter, experts),
+        (out((main, packed_width), F32), out((main - rest, packed_width), BF16), out((rest, packed_width), BF16)),
+        kept,
+        near,
+    )
+    far, others = xor_permute(far, "tensor", 2), xor_permute(others, "tensor", 2)
+    block = out((MAIN, packed_width), BF16)
+    farthest = call(functools.partial(far_kernel, rest), [block] * early, own, far)
+    blocks = [*call(functools.partial(far_kernel, 0), [block] * (experts - early), own, others), *farthest]
     blocks = [*[xor_permute(blocks[k], "expert", k) for k in reversed(steps)], blocks[0]]
-    (result,) = call(functools.partial(combine_kernel, experts), (out((rows, quarter), F32),), hidden, high, low, *blocks)
+    (result,) = call(
+        functools.partial(combine_kernel, experts, quarter), (out((rows, quarter), F32),), hidden, mixing, *blocks
+    )
     return result
 
 

time: 36 us -> 34.7 us (0.964)
  waiting for transfers between devices: 17.9 us -> 16.2 us
  starting transfers between devices: 14.2 us -> 14.8 us
    ppermute x11 -> x12, waiting for transfers between devices: 17.9 us -> 16.2 us  [xor_permute(): return lax.ppermute(value, axis, [(i, i ^ step) for i in range(count)])]
    ppermute x11 -> x12, starting transfers between devices: 14.2 us -> 14.8 us  [xor_permute(): return lax.ppermute(value, axis, [(i, i ^ step) for i in range(count)])]
    pallas_call x11 -> x12, Pallas kernels: 3.42 us -> 3.17 us  [call(): pl.pallas_call(kernel, out_shape=tuple(outs), in_specs=[vmem_spec] * len(...]
  transfers between devices with their start and end apart: 11 -> 12, of which waited for: 9 -> 9; matrix products, arithmetic and copies ran while one was open for 0% -> 0% of each run, Pallas kernels for 3% -> 3%
where the time goes in v3:
time: 34.7 us; the launch traced here: 34.6 us
  waiting for transfers between devices  16.2 us (47%)
  starting transfers between devices  14.8 us (43%)
  Pallas kernels  3.17 us (9%)
    ppermute x12, waiting for transfers between devices, xor_permute(): return lax.ppermute(value, axis, [(i, i ^ step) for i in range(count)])  16.2 us
    ppermute x12, starting transfers between devices, xor_permute(): return lax.ppermute(value, axis, [(i, i ^ step) for i in range(count)])  14.8 us
    pallas_call x12, Pallas kernels, call(): pl.pallas_call(kernel, out_shape=tuple(outs), in_specs=[vmem_spec] * len(...  3.17 us
  transfers between devices with their start and end apart: 12, of which 9 were waited for; matrix products, arithmetic and copies ran while one was open for 0% of the time, Pallas kernels for 3%

profile of v3, /device:TPU:0, one launch (start us, length us, event | category | flops | bytes accessed | tf_op | source)
XLA Modules:
  0.0 34.6 jit_solution(5742668870754069574)
XLA Ops:
  0.0 0.5 %collective-permute-start = (bf16[32,3584]{1,0:T(8,128)(2,1)}, bf16[32,3584]{1,0:T(8,128)(2,1)S(1)}, u32[]{:S(2)}, u32[]{:S(2)}) collective-permute-start(bf16[32,3584]{1,0:T(8,128)(2,1)} %bitcast.3), channel_id=1, source_target_pairs={{0,1},{1,0},{2,3},{3,2},{4,5},{5,4},{6,7},{7,6},{8,9},{9,8},{10,11... | collective-permute-start | bytes 688136 | tf_op jit(solution)/shard_map/ppermute | solution.py:20
  0.5 0.2 copy-done.5
  0.7 0.0 copy-done.6
  0.7 0.3 shard_map.83
  1.0 0.8 %collective-permute-done.near_ref = bf16[32,3584]{1,0:T(8,128)(2,1)S(1)} collective-permute-done((bf16[32,3584]{1,0:T(8,128)(2,1)}, bf16[32,3584]{1,0:T(8,128)(2,1)S(1)}, u32[]{:S(2)}, u32[]{:S(2)}) %collective-permute-start) | collective-permute-done | bytes 229408 | tf_op jit(solution)/shard_map/ppermute | solution.py:20
  1.8 2.9 %collective-permute-start.1 = (bf16[32,1792]{1,0:T(8,128)(2,1)S(1)}, bf16[32,1792]{1,0:T(8,128)(2,1)S(1)}, u32[]{:S(2)}, u32[]{:S(2)}) collective-permute-start(bf16[32,1792]{1,0:T(8,128)(2,1)S(1)} %get-tuple-element.32), channel_id=1, source_target_pairs={{0,2},{1,3},{2,0},{3,1},{4,6},{5,7},{6,4},{7,5},{8,10},{9,11},{10,... | collective-permute-start | bytes 344072 | tf_op jit(solution)/shard_map/ppermute | solution.py:20
  4.8 3.4 %collective-permute-done.1.far_ref = bf16[32,1792]{1,0:T(8,128)(2,1)S(1)} collective-permute-done((bf16[32,1792]{1,0:T(8,128)(2,1)S(1)}, bf16[32,1792]{1,0:T(8,128)(2,1)S(1)}, u32[]{:S(2)}, u32[]{:S(2)}) %collective-permute-start.1) | collective-permute-done | bytes 114720 | tf_op jit(solution)/shard_map/ppermute | solution.py:20
  8.2 0.5 %shard_map.85 = (f32[32,896]{1,0:T(8,128)S(1)}, bf16[16,1920]{1,0:T(8,128)(2,1)S(1)}, bf16[16,1920]{1,0:T(8,128)(2,1)S(1)}, bf16[16,1920]{1,0:T(8,128)(2,1)S(1)}, bf16[16,1920]{1,0:T(8,128)(2,1)S(1)}) custom-call(f32[32,3584]{1,0:T(8,128)S(1)} %copy-done.3, f32[32,1792]{1,0:T(8,128)S(1)} %get-tuple-element.31.chip_ref, ...), custom_call_target="tpu_custom_call" | custom-call | flops 4294967296 | bytes 1243136 | tf_op jit(solution)/shard_map/pallas_call | solution.py:31
  8.7 3.9 %collective-permute-start.2 = (bf16[16,1920]{1,0:T(8,128)(2,1)S(1)}, bf16[16,1920]{1,0:T(8,128)(2,1)S(1)}, u32[]{:S(2)}, u32[]{:S(2)}) collective-permute-start(bf16[16,1920]{1,0:T(8,128)(2,1)S(1)} %get-tuple-element.36), channel_id=1, source_target_pairs={{0,12},{4,8},{8,4},{12,0},{1,13},{5,9},{9,5},{13,1},{2,14},{6,10},... | collective-permute-start | bytes 184328 | tf_op jit(solution)/shard_map/ppermute | solution.py:20
  12.6 0.6 %collective-permute-start.4 = (bf16[16,1920]{1,0:T(8,128)(2,1)S(1)}, bf16[16,1920]{1,0:T(8,128)(2,1)S(1)}, u32[]{:S(2)}, u32[]{:S(2)}) collective-permute-start(bf16[16,1920]{1,0:T(8,128)(2,1)S(1)} %get-tuple-element.38), channel_id=1, source_target_pairs={{0,4},{4,0},{8,12},{12,8},{1,5},{5,1},{9,13},{13,9},{2,6},{6,2},{1... | collective-permute-start | bytes 184328 | tf_op jit(solution)/shard_map/ppermute | solution.py:20
  13.2 2.3 %collective-permute-done.2.refs_0_ = bf16[16,1920]{1,0:T(8,128)(2,1)S(1)} collective-permute-done((bf16[16,1920]{1,0:T(8,128)(2,1)S(1)}, bf16[16,1920]{1,0:T(8,128)(2,1)S(1)}, u32[]{:S(2)}, u32[]{:S(2)}) %collective-permute-start.2) | collective-permute-done | bytes 61472 | tf_op jit(solution)/shard_map/ppermute | solution.py:20
  15.5 2.2 %collective-permute-done.3.refs_1_ = bf16[16,1920]{1,0:T(8,128)(2,1)S(1)} collective-permute-done((bf16[16,1920]{1,0:T(8,128)(2,1)S(1)}, bf16[16,1920]{1,0:T(8,128)(2,1)S(1)}, u32[]{:S(2)}, u32[]{:S(2)}) %collective-permute-start.3) | collective-permute-done | bytes 61472 | tf_op jit(solution)/shard_map/ppermute | solution.py:20
  17.7 0.0 copy-start.2
  17.8 0.1 collective-permute-start.5
  17.9 0.5 %shard_map.87 = (f32[80,256]{1,0:T(8,128)S(1)}, f32[80,256]{1,0:T(8,128)S(1)}) custom-call(bf16[64,1920]{1,0:T(8,128)(2,1)S(1)} %shard_map.86.own_ref, bf16[1,3584,256]{2,1,0:T(8,128)(2,1)S(1)} %copy-done, bf16[1,3584,256]{2,1,0:T(8,128)(2,1)S(1)} %copy-done.1), custom_call_target="tpu_custom_call" | custom-call | flops 4294967296 | bytes 4079616 | tf_op jit(solution)/shard_map/pallas_call | solution.py:31
  18.3 1.0 %collective-permute-done.5.other_ref = bf16[64,1920]{1,0:T(8,128)(2,1)S(1)} collective-permute-done((bf16[64,1920]{1,0:T(8,128)(2,1)S(1)}, bf16[64,1920]{1,0:T(8,128)(2,1)S(1)}, u32[]{:S(2)}, u32[]{:S(2)}) %collective-permute-start.5) | collective-permute-done | bytes 245792 | tf_op jit(solution)/shard_map/ppermute | solution.py:20
  19.3 0.7 %shard_map.88 = (bf16[80,256]{1,0:T(8,128)(2,1)S(1)}, bf16[72,1792]{1,0:T(8,128)(2,1)S(1)}) custom-call(bf16[64,1920]{1,0:T(8,128)(2,1)S(1)} %shard_map.86.own_ref, bf16[64,1920]{1,0:T(8,128)(2,1)S(1)} %collective-permute-done.5.other_ref, f32[80,256]{1,0:T(8,128)S(1)} %get-tuple-element.40.gated_ref, f32[80,256]{1,0:T(8,128)S(1)} %get-tuple-element.41.upward_ref, ...), custom_call_target="tpu_custom_call" | custom-call | flops 4294967296 | bytes 6459392 | tf_op jit(solution)/shard_map/pallas_call | solution.py:31
  20.1 0.2 collective-permute-start.6
  20.3 0.3 shard_map.89.kept_ref
  20.5 1.1 %collective-permute-done.6.near_ref = bf16[72,1792]{1,0:T(8,128)(2,1)S(1)} collective-permute-done((bf16[72,1792]{1,0:T(8,128)(2,1)S(1)}, bf16[72,1792]{1,0:T(8,128)(2,1)S(1)}, u32[]{:S(2)}, u32[]{:S(2)}) %collective-permute-start.6) | collective-permute-done | bytes 258080 | tf_op jit(solution)/shard_map/ppermute | solution.py:20
  21.7 0.1 shard_map.90
  21.7 1.6 %collective-permute-start.7 = (bf16[32,1024]{1,0:T(8,128)(2,1)S(1)}, bf16[32,1024]{1,0:T(8,128)(2,1)S(1)}, u32[]{:S(2)}, u32[]{:S(2)}) collective-permute-start(bf16[32,1024]{1,0:T(8,128)(2,1)S(1)} %get-tuple-element.45), channel_id=1, source_target_pairs={{0,2},{1,3},{2,0},{3,1},{4,6},{5,7},{6,4},{7,5},{8,10},{9,11},{10,... | collective-permute-start | bytes 196616 | tf_op jit(solution)/shard_map/ppermute | solution.py:20
  23.3 0.5 %collective-permute-start.10 = (bf16[32,1024]{1,0:T(8,128)(2,1)S(1)}, bf16[32,1024]{1,0:T(8,128)(2,1)S(1)}, u32[]{:S(2)}, u32[]{:S(2)}) collective-permute-start(bf16[32,1024]{1,0:T(8,128)(2,1)S(1)} %get-tuple-element.48), channel_id=1, source_target_pairs={{0,2},{1,3},{2,0},{3,1},{4,6},{5,7},{6,4},{7,5},{8,10},{9,11},{10,... | collective-permute-start | bytes 196616 | tf_op jit(solution)/shard_map/ppermute | solution.py:20
  23.8 2.6 %collective-permute-done.7.far_ref = bf16[32,1024]{1,0:T(8,128)(2,1)S(1)} collective-permute-done((bf16[32,1024]{1,0:T(8,128)(2,1)S(1)}, bf16[32,1024]{1,0:T(8,128)(2,1)S(1)}, u32[]{:S(2)}, u32[]{:S(2)}) %collective-permute-start.7) | collective-permute-done | bytes 65568 | tf_op jit(solution)/shard_map/ppermute | solution.py:20
  26.5 2.4 %collective-permute-start.8 = (bf16[16,1024]{1,0:T(8,128)(2,1)S(1)}, bf16[16,1024]{1,0:T(8,128)(2,1)S(1)}, u32[]{:S(2)}, u32[]{:S(2)}) collective-permute-start(bf16[16,1024]{1,0:T(8,128)(2,1)S(1)} %get-tuple-element.46), channel_id=1, source_target_pairs={{0,12},{4,8},{8,4},{12,0},{1,13},{5,9},{9,5},{13,1},{2,14},{6,10},... | collective-permute-start | bytes 98312 | tf_op jit(solution)/shard_map/ppermute | solution.py:20
  28.9 0.0 collective-permute-start.9
  28.9 0.0 collective-permute-done.10.far_ref
  29.0 2.1 %collective-permute-start.11 = (bf16[16,1024]{1,0:T(8,128)(2,1)S(1)}, bf16[16,1024]{1,0:T(8,128)(2,1)S(1)}, u32[]{:S(2)}, u32[]{:S(2)}) collective-permute-start(bf16[16,1024]{1,0:T(8,128)(2,1)S(1)} %get-tuple-element.49), channel_id=1, source_target_pairs={{0,4},{4,0},{8,12},{12,8},{1,5},{5,1},{9,13},{13,9},{2,6},{6,2},{1... | collective-permute-start | bytes 98312 | tf_op jit(solution)/shard_map/ppermute | solution.py:20
  31.1 1.5 %collective-permute-done.8.refs_0_ = bf16[16,1024]{1,0:T(8,128)(2,1)S(1)} collective-permute-done((bf16[16,1024]{1,0:T(8,128)(2,1)S(1)}, bf16[16,1024]{1,0:T(8,128)(2,1)S(1)}, u32[]{:S(2)}, u32[]{:S(2)}) %collective-permute-start.8) | collective-permute-done | bytes 32800 | tf_op jit(solution)/shard_map/ppermute | solution.py:20
  32.6 1.2 %collective-permute-done.9.refs_1_ = bf16[16,1024]{1,0:T(8,128)(2,1)S(1)} collective-permute-done((bf16[16,1024]{1,0:T(8,128)(2,1)S(1)}, bf16[16,1024]{1,0:T(8,128)(2,1)S(1)}, u32[]{:S(2)}, u32[]{:S(2)}) %collective-permute-start.9) | collective-permute-done | bytes 32800 | tf_op jit(solution)/shard_map/ppermute | solution.py:20
  33.7 0.0 collective-permute-done.11.refs_2_
  33.7 0.8 %shard_map.93 = f32[32,896]{1,0:T(8,128)} custom-call(f32[32,896]{1,0:T(8,128)S(1)} %get-tuple-element.35.hidden_ref, bf16[64,128]{1,0:T(8,128)(2,1)S(1)} %get-tuple-element.30.after_ref.mixing_ref, bf16[16,1024]{1,0:T(8,128)(2,1)S(1)} %collective-permute-done.8.refs_0_, bf16[16,1024]{1,0:T(8,128)(2,1)S(1)} %collective-permute-done.9.refs_1_, ...), custom_call_target="tpu_custom_call" | custom-call | flops 4294967296 | bytes 376832 | tf_op jit(solution)/shard_map/pallas_call | solution.py:31
  (21 shorter events, 0.1 us)
Async XLA Ops:
  0.0 0.7 %copy-start.5 = (s32[32,2]{0,1:T(2,128)S(1)}, s32[32,2]{0,1:T(2,128)}, u32[]{:S(2)}) copy-start(s32[32,2]{0,1:T(2,128)} %param.11) | copy-start | bytes 772
  0.0 0.7 %copy-start.6 = (f32[32,2]{0,1:T(2,128)S(1)}, f32[32,2]{0,1:T(2,128)}, u32[]{:S(2)}) copy-start(f32[32,2]{0,1:T(2,128)} %param.12) | copy-start | bytes 772
  0.0 1.8 %collective-permute-start = (bf16[32,3584]{1,0:T(8,128)(2,1)}, bf16[32,3584]{1,0:T(8,128)(2,1)S(1)}, u32[]{:S(2)}, u32[]{:S(2)}) collective-permute-start(bf16[32,3584]{1,0:T(8,128)(2,1)} %bitcast.3), channel_id=1, source_target_pairs={{0,1},{1,0},{2,3},{3,2},{4,5},{5,4},{6,7},{7,6},{8,9},{9,8},{10,11... | collective-permute-start | bytes 688136 | tf_op jit(solution)/shard_map/ppermute | solution.py:20
  0.7 1.1 %copy-start.4 = (bf16[1,32,3584]{2,1,0:T(8,128)(2,1)S(1)}, bf16[1,32,3584]{2,1,0:T(8,128)(2,1)}, u32[]{:S(2)}) copy-start(bf16[1,32,3584]{2,1,0:T(8,128)(2,1)} %param.9) | copy-start | bytes 688132
  1.8 3.0 %copy-start.7 = (f32[3584]{0:T(1024)S(1)}, f32[3584]{0:T(1024)}, u32[]{:S(2)}) copy-start(f32[3584]{0:T(1024)} %param.10) | copy-start | bytes 43012
  1.8 6.4 %copy-start.3 = (f32[32,3584]{1,0:T(8,128)S(1)}, f32[32,3584]{1,0:T(8,128)}, u32[]{:S(2)}) copy-start(f32[32,3584]{1,0:T(8,128)} %residual_ref.1) | copy-start | bytes 1376260
  1.8 6.4 %collective-permute-start.1 = (bf16[32,1792]{1,0:T(8,128)(2,1)S(1)}, bf16[32,1792]{1,0:T(8,128)(2,1)S(1)}, u32[]{:S(2)}, u32[]{:S(2)}) collective-permute-start(bf16[32,1792]{1,0:T(8,128)(2,1)S(1)} %get-tuple-element.32), channel_id=1, source_target_pairs={{0,2},{1,3},{2,0},{3,1},{4,6},{5,7},{6,4},{7,5},{8,10},{9,11},{10,... | collective-permute-start | bytes 344072 | tf_op jit(solution)/shard_map/ppermute | solution.py:20
  8.2 9.6 %copy-start = (bf16[1,3584,256]{2,1,0:T(8,128)(2,1)S(1)}, bf16[1,3584,256]{2,1,0:T(8,128)(2,1)}, u32[]{:S(2)}) copy-start(bf16[1,3584,256]{2,1,0:T(8,128)(2,1)} %gate_ref.3) | copy-start | bytes 5505028
  8.2 9.6 %copy-start.1 = (bf16[1,3584,256]{2,1,0:T(8,128)(2,1)S(1)}, bf16[1,3584,256]{2,1,0:T(8,128)(2,1)}, u32[]{:S(2)}) copy-start(bf16[1,3584,256]{2,1,0:T(8,128)(2,1)} %up_ref.3) | copy-start | bytes 5505028
  8.7 6.9 %collective-permute-start.2 = (bf16[16,1920]{1,0:T(8,128)(2,1)S(1)}, bf16[16,1920]{1,0:T(8,128)(2,1)S(1)}, u32[]{:S(2)}, u32[]{:S(2)}) collective-permute-start(bf16[16,1920]{1,0:T(8,128)(2,1)S(1)} %get-tuple-element.36), channel_id=1, source_target_pairs={{0,12},{4,8},{8,4},{12,0},{1,13},{5,9},{9,5},{13,1},{2,14},{6,10},... | collective-permute-start | bytes 184328 | tf_op jit(solution)/shard_map/ppermute | solution.py:20
  12.6 5.1 %collective-permute-start.3 = (bf16[16,1920]{1,0:T(8,128)(2,1)S(1)}, bf16[16,1920]{1,0:T(8,128)(2,1)S(1)}, u32[]{:S(2)}, u32[]{:S(2)}) collective-permute-start(bf16[16,1920]{1,0:T(8,128)(2,1)S(1)} %get-tuple-element.37), channel_id=1, source_target_pairs={{0,8},{4,12},{8,0},{12,4},{1,9},{5,13},{9,1},{13,5},{2,10},{6,14},... | collective-permute-start | bytes 184328 | tf_op jit(solution)/shard_map/ppermute | solution.py:20
  12.6 5.1 %collective-permute-start.4 = (bf16[16,1920]{1,0:T(8,128)(2,1)S(1)}, bf16[16,1920]{1,0:T(8,128)(2,1)S(1)}, u32[]{:S(2)}, u32[]{:S(2)}) collective-permute-start(bf16[16,1920]{1,0:T(8,128)(2,1)S(1)} %get-tuple-element.38), channel_id=1, source_target_pairs={{0,4},{4,0},{8,12},{12,8},{1,5},{5,1},{9,13},{13,9},{2,6},{6,2},{1... | collective-permute-start | bytes 184328 | tf_op jit(solution)/shard_map/ppermute | solution.py:20
  17.7 1.6 %copy-start.2 = (bf16[1,256,3584]{2,1,0:T(8,128)(2,1)S(1)}, bf16[1,256,3584]{2,1,0:T(8,128)(2,1)}, u32[]{:S(2)}) copy-start(bf16[1,256,3584]{2,1,0:T(8,128)(2,1)} %down_ref.3) | copy-start | bytes 5505028
  17.8 1.6 %collective-permute-start.5 = (bf16[64,1920]{1,0:T(8,128)(2,1)S(1)}, bf16[64,1920]{1,0:T(8,128)(2,1)S(1)}, u32[]{:S(2)}, u32[]{:S(2)}) collective-permute-start(bf16[64,1920]{1,0:T(8,128)(2,1)S(1)} %shard_map.86.own_ref), channel_id=1, source_target_pairs={{0,1},{1,0},{2,3},{3,2},{4,5},{5,4},{6,7},{7,6},{8,9},{9,8},{10,11... | collective-permute-start | bytes 737288 | tf_op jit(solution)/shard_map/ppermute | solution.py:20
  20.1 1.6 %collective-permute-start.6 = (bf16[72,1792]{1,0:T(8,128)(2,1)S(1)}, bf16[72,1792]{1,0:T(8,128)(2,1)S(1)}, u32[]{:S(2)}, u32[]{:S(2)}) collective-permute-start(bf16[72,1792]{1,0:T(8,128)(2,1)S(1)} %get-tuple-element.43), channel_id=1, source_target_pairs={{0,1},{1,0},{2,3},{3,2},{4,5},{5,4},{6,7},{7,6},{8,9},{9,8},{10,11... | collective-permute-start | bytes 774152 | tf_op jit(solution)/shard_map/ppermute | solution.py:20
  21.7 4.7 %collective-permute-start.7 = (bf16[32,1024]{1,0:T(8,128)(2,1)S(1)}, bf16[32,1024]{1,0:T(8,128)(2,1)S(1)}, u32[]{:S(2)}, u32[]{:S(2)}) collective-permute-start(bf16[32,1024]{1,0:T(8,128)(2,1)S(1)} %get-tuple-element.45), channel_id=1, source_target_pairs={{0,2},{1,3},{2,0},{3,1},{4,6},{5,7},{6,4},{7,5},{8,10},{9,11},{10,... | collective-permute-start | bytes 196616 | tf_op jit(solution)/shard_map/ppermute | solution.py:20
  23.3 5.6 %collective-permute-start.10 = (bf16[32,1024]{1,0:T(8,128)(2,1)S(1)}, bf16[32,1024]{1,0:T(8,128)(2,1)S(1)}, u32[]{:S(2)}, u32[]{:S(2)}) collective-permute-start(bf16[32,1024]{1,0:T(8,128)(2,1)S(1)} %get-tuple-element.48), channel_id=1, source_target_pairs={{0,2},{1,3},{2,0},{3,1},{4,6},{5,7},{6,4},{7,5},{8,10},{9,11},{10,... | collective-permute-start | bytes 196616 | tf_op jit(solution)/shard_map/ppermute | solution.py:20
  26.5 6.1 %collective-permute-start.8 = (bf16[16,1024]{1,0:T(8,128)(2,1)S(1)}, bf16[16,1024]{1,0:T(8,128)(2,1)S(1)}, u32[]{:S(2)}, u32[]{:S(2)}) collective-permute-start(bf16[16,1024]{1,0:T(8,128)(2,1)S(1)} %get-tuple-element.46), channel_id=1, source_target_pairs={{0,12},{4,8},{8,4},{12,0},{1,13},{5,9},{9,5},{13,1},{2,14},{6,10},... | collective-permute-start | bytes 98312 | tf_op jit(solution)/shard_map/ppermute | solution.py:20
  28.9 4.8 %collective-permute-start.9 = (bf16[16,1024]{1,0:T(8,128)(2,1)S(1)}, bf16[16,1024]{1,0:T(8,128)(2,1)S(1)}, u32[]{:S(2)}, u32[]{:S(2)}) collective-permute-start(bf16[16,1024]{1,0:T(8,128)(2,1)S(1)} %get-tuple-element.47), channel_id=1, source_target_pairs={{0,8},{4,12},{8,0},{12,4},{1,9},{5,13},{9,1},{13,5},{2,10},{6,14},... | collective-permute-start | bytes 98312 | tf_op jit(solution)/shard_map/ppermute | solution.py:20
  29.0 4.8 %collective-permute-start.11 = (bf16[16,1024]{1,0:T(8,128)(2,1)S(1)}, bf16[16,1024]{1,0:T(8,128)(2,1)S(1)}, u32[]{:S(2)}, u32[]{:S(2)}) collective-permute-start(bf16[16,1024]{1,0:T(8,128)(2,1)S(1)} %get-tuple-element.49), channel_id=1, source_target_pairs={{0,4},{4,0},{8,12},{12,8},{1,5},{5,1},{9,13},{13,9},{2,6},{6,2},{1... | collective-permute-start | bytes 98312 | tf_op jit(solution)/shard_map/ppermute | solution.py:20

commit v4 on v3

--- a/solution.py
+++ b/solution.py
@@ -66,7 +66,7 @@
     spread_ref[...] = onehot(iota(shape, 0) == iota(shape, 1) % rows).astype(BF16)
 
 
-def table_kernel(experts, rows, chunks, before_ref, spread_ref, ids_ref, gates_ref, table_ref, tails_ref, mixing_ref):
+def table_kernel(experts, rows, chunks, before_ref, spread_ref, ids_ref, gates_ref, table_ref, slots_ref, tails_ref, mixing_ref):
     expert = lax.axis_index("expert")
     relative = ids_ref[...] ^ expert
     gates = gates_ref[...]
@@ -81,9 +81,10 @@
     slot = iota((MAIN, rows), 0).astype(F32)
     pieces = [onehot(position[k : k + 1] == slot) for k in range(experts)]
     tail = onehot(position == float(MAIN))
-    rest = table_ref.shape[0] - experts * MAIN - 8
+    rest = LANES - experts * MAIN - 8
     table = jnp.concatenate([*pieces, tail, jnp.zeros((rest, rows), F32)], axis=0)
-    table_ref[...] = table.astype(BF16)
+    table_ref[...] = table[: experts * MAIN].astype(BF16)
+    slots_ref[...] = table.T
     wide = jnp.concatenate([jnp.broadcast_to(tail[k : k + 1], (MAIN, rows)) for k in range(experts)], axis=0)
     spread = dot(wide.astype(BF16), spread_ref[...])
     shape = (experts * MAIN, rows * chunks)
@@ -104,38 +105,36 @@
         sent_ref[:, o * quarter : (o + 1) * quarter] = total.astype(BF16)
 
 
-def dispatch_kernel(quarter, experts, residual_ref, chip_ref, far_ref, gain_ref, table_ref, tails_ref, hidden_ref, *block_refs):
+def dispatch_kernel(quarter, experts, residual_ref, chip_ref, far_ref, gain_ref, table_ref, slots_ref, tails_ref, hidden_ref, *block_refs):
     tensor = lax.axis_index("tensor")
     side = tensor % 2
     rows = chip_ref.shape[0]
-    squares = jnp.zeros((rows, 1), F32)
+    squares = jnp.zeros((rows, LANES), F32)
     gained = []
     for o in range(2):
         here = slice(o * quarter, (o + 1) * quarter)
         columns = strip(2 * o + side, quarter)
         hidden = residual_ref[:, columns] + chip_ref[:, here] + far_ref[:, here].astype(F32)
-        squares = squares + jnp.sum(hidden * hidden, axis=1, keepdims=True)
+        for i in range(quarter // LANES):
+            part = hidden[:, i * LANES : (i + 1) * LANES]
+            squares = squares + part * part
         gained.append((hidden * gain_ref[:, columns]).astype(BF16))
 
         @pl.when(o == tensor // 2)
         def _():
             hidden_ref[...] = hidden
 
-    table = table_ref[...]
-    main = table[: experts * MAIN]
-    lanes = jnp.sum(jnp.where(iota((rows, rows), 0) == iota((rows, rows), 1), squares, 0.0), axis=0, keepdims=True)
-    high = lanes.astype(BF16).astype(F32)
-    pick = iota((MAIN, rows), 0)
-    pair = jnp.where(pick == 0, high, jnp.where(pick == 1, lanes - high, 0.0)).astype(BF16)
-    slots = dot(pair, table, ((1,), (1,)))
+    squares = jnp.sum(slots_ref[...] * jnp.sum(squares, axis=1, keepdims=True), axis=0, keepdims=True)
+    high = squares.astype(BF16).astype(F32)
+    low = squares - high
     for o in range(2):
-        picked = dot(main, gained[o]).astype(BF16)
+        picked = dot(table_ref[...], gained[o]).astype(BF16)
         for k in range(experts):
             block_refs[k][:, o * quarter : (o + 1) * quarter] = picked[k * MAIN : (k + 1) * MAIN]
     parts = [g[:, i * LANES : (i + 1) * LANES] for g in gained for i in range(quarter // LANES)]
     tile = dot(tails_ref[...], jnp.concatenate(parts, axis=0))
     row = iota(tile.shape, 0) % MAIN
-    tile = jnp.where(row == MAIN - 2, slots[0:1], jnp.where(row == MAIN - 1, slots[1:2], tile)).astype(BF16)
+    tile = jnp.where(row == MAIN - 2, high, jnp.where(row == MAIN - 1, low, tile)).astype(BF16)
     for k in range(experts):
         block_refs[k][:, 2 * quarter :] = tile[k * MAIN : (k + 1) * MAIN]
 
@@ -263,9 +262,14 @@
     before, spread = call(
         functools.partial(constant_kernel, rows), (out((rows, rows), BF16), out((rows, rows * chunks), BF16))
     )
-    table, tails, mixing = call(
+    table, slots, tails, mixing = call(
         functools.partial(table_kernel, experts, rows, chunks),
-        (out((LANES, rows), BF16), out((experts * MAIN, rows * chunks), BF16), out((2 * rows, LANES), BF16)),
+        (
+            out((experts * MAIN, rows), BF16),
+            out((rows, LANES), F32),
+            out((experts * MAIN, rows * chunks), BF16),
+            out((2 * rows, LANES), BF16),
+        ),
         before,
         spread,
         expert_ids.T,
@@ -284,20 +288,21 @@
         far,
         norm_gain[None],
         table,
+        slots,
         tails,
     )
     arrived = [*[xor_permute(blocks[k], "expert", k) for k in reversed(steps)], blocks[0]]
     packed = out((experts * MAIN, width + LANES), BF16)
     (arrived,) = call(functools.partial(pack_kernel, experts), (packed,), *arrived, flops=0)
     other = xor_permute(arrived, "tensor", 1)
-    main, slots = experts * MAIN, (experts + 1) * MAIN
+    main, slot_count = experts * MAIN, (experts + 1) * MAIN
     packed_width, used = quarter + LANES, main + 8
     hidden_count = w_gate.shape[2]
-    sums = out((slots, hidden_count), F32)
+    sums = out((slot_count, hidden_count), F32)
     gated, upward = call(functools.partial(own_kernel, quarter, experts), (sums, sums), arrived, w_gate, w_up)
     active, sent = call(
         functools.partial(other_kernel, quarter, experts),
-        (out((slots, hidden_count), BF16), out((used, width), BF16)),
+        (out((slot_count, hidden_count), BF16), out((used, width), BF16)),
         arrived,
         other,
         gated,

time: 34.7 us -> 34.6 us (level)
  no operation moved by 1% of the time
where the time goes in v4:
time: 34.6 us; the launch traced here: 34.4 us
  waiting for transfers between devices  16.2 us (47%)
  starting transfers between devices  14.8 us (43%)
  Pallas kernels  3 us (9%)
    ppermute x12, waiting for transfers between devices, xor_permute(): return lax.ppermute(value, axis, [(i, i ^ step) for i in range(count)])  16.2 us
    ppermute x12, starting transfers between devices, xor_permute(): return lax.ppermute(value, axis, [(i, i ^ step) for i in range(count)])  14.8 us
    pallas_call x12, Pallas kernels, call(): pl.pallas_call(kernel, out_shape=tuple(outs), in_specs=[vmem_spec] * len(...  3 us
  transfers between devices with their start and end apart: 12, of which 9 were waited for; matrix products, arithmetic and copies ran while one was open for 0% of the time, Pallas kernels for 3%

profile of v4, /device:TPU:0, one launch (start us, length us, event | category | flops | bytes accessed | tf_op | source)
XLA Modules:
  0.0 34.4 jit_solution(3706559391741439490)
XLA Ops:
  0.0 0.5 %collective-permute-start = (bf16[32,3584]{1,0:T(8,128)(2,1)}, bf16[32,3584]{1,0:T(8,128)(2,1)S(1)}, u32[]{:S(2)}, u32[]{:S(2)}) collective-permute-start(bf16[32,3584]{1,0:T(8,128)(2,1)} %bitcast.3), channel_id=1, source_target_pairs={{0,1},{1,0},{2,3},{3,2},{4,5},{5,4},{6,7},{7,6},{8,9},{9,8},{10,11... | collective-permute-start | bytes 688136 | tf_op jit(solution)/shard_map/ppermute | solution.py:20
  0.5 0.2 copy-done.5
  0.7 0.0 copy-done.6
  0.7 0.3 shard_map.83
  1.0 0.8 %collective-permute-done.near_ref = bf16[32,3584]{1,0:T(8,128)(2,1)S(1)} collective-permute-done((bf16[32,3584]{1,0:T(8,128)(2,1)}, bf16[32,3584]{1,0:T(8,128)(2,1)S(1)}, u32[]{:S(2)}, u32[]{:S(2)}) %collective-permute-start) | collective-permute-done | bytes 229408 | tf_op jit(solution)/shard_map/ppermute | solution.py:20
  1.8 2.9 %collective-permute-start.1 = (bf16[32,1792]{1,0:T(8,128)(2,1)S(1)}, bf16[32,1792]{1,0:T(8,128)(2,1)S(1)}, u32[]{:S(2)}, u32[]{:S(2)}) collective-permute-start(bf16[32,1792]{1,0:T(8,128)(2,1)S(1)} %get-tuple-element.33), channel_id=1, source_target_pairs={{0,2},{1,3},{2,0},{3,1},{4,6},{5,7},{6,4},{7,5},{8,10},{9,11},{10,... | collective-permute-start | bytes 344072 | tf_op jit(solution)/shard_map/ppermute | solution.py:20
  4.8 3.4 %collective-permute-done.1.far_ref = bf16[32,1792]{1,0:T(8,128)(2,1)S(1)} collective-permute-done((bf16[32,1792]{1,0:T(8,128)(2,1)S(1)}, bf16[32,1792]{1,0:T(8,128)(2,1)S(1)}, u32[]{:S(2)}, u32[]{:S(2)}) %collective-permute-start.1) | collective-permute-done | bytes 114720 | tf_op jit(solution)/shard_map/ppermute | solution.py:20
  8.2 0.3 shard_map.85
  8.5 3.9 %collective-permute-start.2 = (bf16[16,1920]{1,0:T(8,128)(2,1)S(1)}, bf16[16,1920]{1,0:T(8,128)(2,1)S(1)}, u32[]{:S(2)}, u32[]{:S(2)}) collective-permute-start(bf16[16,1920]{1,0:T(8,128)(2,1)S(1)} %get-tuple-element.38), channel_id=1, source_target_pairs={{0,12},{4,8},{8,4},{12,0},{1,13},{5,9},{9,5},{13,1},{2,14},{6,10},... | collective-permute-start | bytes 184328 | tf_op jit(solution)/shard_map/ppermute | solution.py:20
  12.4 0.0 collective-permute-start.3
  12.4 0.6 %collective-permute-start.4 = (bf16[16,1920]{1,0:T(8,128)(2,1)S(1)}, bf16[16,1920]{1,0:T(8,128)(2,1)S(1)}, u32[]{:S(2)}, u32[]{:S(2)}) collective-permute-start(bf16[16,1920]{1,0:T(8,128)(2,1)S(1)} %get-tuple-element.40), channel_id=1, source_target_pairs={{0,4},{4,0},{8,12},{12,8},{1,5},{5,1},{9,13},{13,9},{2,6},{6,2},{1... | collective-permute-start | bytes 184328 | tf_op jit(solution)/shard_map/ppermute | solution.py:20
  13.1 2.3 %collective-permute-done.2.refs_0_ = bf16[16,1920]{1,0:T(8,128)(2,1)S(1)} collective-permute-done((bf16[16,1920]{1,0:T(8,128)(2,1)S(1)}, bf16[16,1920]{1,0:T(8,128)(2,1)S(1)}, u32[]{:S(2)}, u32[]{:S(2)}) %collective-permute-start.2) | collective-permute-done | bytes 61472 | tf_op jit(solution)/shard_map/ppermute | solution.py:20
  15.4 2.2 %collective-permute-done.3.refs_1_ = bf16[16,1920]{1,0:T(8,128)(2,1)S(1)} collective-permute-done((bf16[16,1920]{1,0:T(8,128)(2,1)S(1)}, bf16[16,1920]{1,0:T(8,128)(2,1)S(1)}, u32[]{:S(2)}, u32[]{:S(2)}) %collective-permute-start.3) | collective-permute-done | bytes 61472 | tf_op jit(solution)/shard_map/ppermute | solution.py:20
  17.6 0.0 collective-permute-done.4.refs_2_
  17.6 0.0 copy-start.2
  17.6 0.1 collective-permute-start.5
  17.7 0.5 %shard_map.87 = (f32[80,256]{1,0:T(8,128)S(1)}, f32[80,256]{1,0:T(8,128)S(1)}) custom-call(bf16[64,1920]{1,0:T(8,128)(2,1)S(1)} %shard_map.86.own_ref, bf16[1,3584,256]{2,1,0:T(8,128)(2,1)S(1)} %copy-done, bf16[1,3584,256]{2,1,0:T(8,128)(2,1)S(1)} %copy-done.1), custom_call_target="tpu_custom_call" | custom-call | flops 4294967296 | bytes 4079616 | tf_op jit(solution)/shard_map/pallas_call | solution.py:31
  18.2 1.0 %collective-permute-done.5.other_ref = bf16[64,1920]{1,0:T(8,128)(2,1)S(1)} collective-permute-done((bf16[64,1920]{1,0:T(8,128)(2,1)S(1)}, bf16[64,1920]{1,0:T(8,128)(2,1)S(1)}, u32[]{:S(2)}, u32[]{:S(2)}) %collective-permute-start.5) | collective-permute-done | bytes 245792 | tf_op jit(solution)/shard_map/ppermute | solution.py:20
  19.2 0.7 %shard_map.88 = (bf16[80,256]{1,0:T(8,128)(2,1)S(1)}, bf16[72,1792]{1,0:T(8,128)(2,1)S(1)}) custom-call(bf16[64,1920]{1,0:T(8,128)(2,1)S(1)} %shard_map.86.own_ref, bf16[64,1920]{1,0:T(8,128)(2,1)S(1)} %collective-permute-done.5.other_ref, f32[80,256]{1,0:T(8,128)S(1)} %get-tuple-element.42.gated_ref, f32[80,256]{1,0:T(8,128)S(1)} %get-tuple-element.43.upward_ref, ...), custom_call_target="tpu_custom_call" | custom-call | flops 4294967296 | bytes 6459392 | tf_op jit(solution)/shard_map/pallas_call | solution.py:31
  19.9 0.2 collective-permute-start.6
  20.1 0.3 shard_map.89.kept_ref
  20.4 1.1 %collective-permute-done.6.near_ref = bf16[72,1792]{1,0:T(8,128)(2,1)S(1)} collective-permute-done((bf16[72,1792]{1,0:T(8,128)(2,1)S(1)}, bf16[72,1792]{1,0:T(8,128)(2,1)S(1)}, u32[]{:S(2)}, u32[]{:S(2)}) %collective-permute-start.6) | collective-permute-done | bytes 258080 | tf_op jit(solution)/shard_map/ppermute | solution.py:20
  21.5 0.1 shard_map.90
  21.6 1.6 %collective-permute-start.7 = (bf16[32,1024]{1,0:T(8,128)(2,1)S(1)}, bf16[32,1024]{1,0:T(8,128)(2,1)S(1)}, u32[]{:S(2)}, u32[]{:S(2)}) collective-permute-start(bf16[32,1024]{1,0:T(8,128)(2,1)S(1)} %get-tuple-element.47), channel_id=1, source_target_pairs={{0,2},{1,3},{2,0},{3,1},{4,6},{5,7},{6,4},{7,5},{8,10},{9,11},{10,... | collective-permute-start | bytes 196616 | tf_op jit(solution)/shard_map/ppermute | solution.py:20
  23.2 0.5 %collective-permute-start.10 = (bf16[32,1024]{1,0:T(8,128)(2,1)S(1)}, bf16[32,1024]{1,0:T(8,128)(2,1)S(1)}, u32[]{:S(2)}, u32[]{:S(2)}) collective-permute-start(bf16[32,1024]{1,0:T(8,128)(2,1)S(1)} %get-tuple-element.50), channel_id=1, source_target_pairs={{0,2},{1,3},{2,0},{3,1},{4,6},{5,7},{6,4},{7,5},{8,10},{9,11},{10,... | collective-permute-start | bytes 196616 | tf_op jit(solution)/shard_map/ppermute | solution.py:20
  23.7 2.6 %collective-permute-done.7.far_ref = bf16[32,1024]{1,0:T(8,128)(2,1)S(1)} collective-permute-done((bf16[32,1024]{1,0:T(8,128)(2,1)S(1)}, bf16[32,1024]{1,0:T(8,128)(2,1)S(1)}, u32[]{:S(2)}, u32[]{:S(2)}) %collective-permute-start.7) | collective-permute-done | bytes 65568 | tf_op jit(solution)/shard_map/ppermute | solution.py:20
  26.3 2.4 %collective-permute-start.8 = (bf16[16,1024]{1,0:T(8,128)(2,1)S(1)}, bf16[16,1024]{1,0:T(8,128)(2,1)S(1)}, u32[]{:S(2)}, u32[]{:S(2)}) collective-permute-start(bf16[16,1024]{1,0:T(8,128)(2,1)S(1)} %get-tuple-element.48), channel_id=1, source_target_pairs={{0,12},{4,8},{8,4},{12,0},{1,13},{5,9},{9,5},{13,1},{2,14},{6,10},... | collective-permute-start | bytes 98312 | tf_op jit(solution)/shard_map/ppermute | solution.py:20
  28.8 0.0 collective-permute-start.9
  28.8 2.1 %collective-permute-start.11 = (bf16[16,1024]{1,0:T(8,128)(2,1)S(1)}, bf16[16,1024]{1,0:T(8,128)(2,1)S(1)}, u32[]{:S(2)}, u32[]{:S(2)}) collective-permute-start(bf16[16,1024]{1,0:T(8,128)(2,1)S(1)} %get-tuple-element.51), channel_id=1, source_target_pairs={{0,4},{4,0},{8,12},{12,8},{1,5},{5,1},{9,13},{13,9},{2,6},{6,2},{1... | collective-permute-start | bytes 98312 | tf_op jit(solution)/shard_map/ppermute | solution.py:20
  30.9 1.5 %collective-permute-done.8.refs_0_ = bf16[16,1024]{1,0:T(8,128)(2,1)S(1)} collective-permute-done((bf16[16,1024]{1,0:T(8,128)(2,1)S(1)}, bf16[16,1024]{1,0:T(8,128)(2,1)S(1)}, u32[]{:S(2)}, u32[]{:S(2)}) %collective-permute-start.8) | collective-permute-done | bytes 32800 | tf_op jit(solution)/shard_map/ppermute | solution.py:20
  32.4 1.2 %collective-permute-done.9.refs_1_ = bf16[16,1024]{1,0:T(8,128)(2,1)S(1)} collective-permute-done((bf16[16,1024]{1,0:T(8,128)(2,1)S(1)}, bf16[16,1024]{1,0:T(8,128)(2,1)S(1)}, u32[]{:S(2)}, u32[]{:S(2)}) %collective-permute-start.9) | collective-permute-done | bytes 32800 | tf_op jit(solution)/shard_map/ppermute | solution.py:20
  33.6 0.8 %shard_map.93 = f32[32,896]{1,0:T(8,128)} custom-call(f32[32,896]{1,0:T(8,128)S(1)} %get-tuple-element.37.hidden_ref, bf16[64,128]{1,0:T(8,128)(2,1)S(1)} %get-tuple-element.31.after_ref.mixing_ref, bf16[16,1024]{1,0:T(8,128)(2,1)S(1)} %collective-permute-done.8.refs_0_, bf16[16,1024]{1,0:T(8,128)(2,1)S(1)} %collective-permute-done.9.refs_1_, ...), custom_call_target="tpu_custom_call" | custom-call | flops 4294967296 | bytes 376832 | tf_op jit(solution)/shard_map/pallas_call | solution.py:31
  (21 shorter events, 0.1 us)
Async XLA Ops:
  0.0 0.7 %copy-start.5 = (s32[32,2]{0,1:T(2,128)S(1)}, s32[32,2]{0,1:T(2,128)}, u32[]{:S(2)}) copy-start(s32[32,2]{0,1:T(2,128)} %param.11) | copy-start | bytes 772
  0.0 0.7 %copy-start.6 = (f32[32,2]{0,1:T(2,128)S(1)}, f32[32,2]{0,1:T(2,128)}, u32[]{:S(2)}) copy-start(f32[32,2]{0,1:T(2,128)} %param.12) | copy-start | bytes 772
  0.0 1.8 %collective-permute-start = (bf16[32,3584]{1,0:T(8,128)(2,1)}, bf16[32,3584]{1,0:T(8,128)(2,1)S(1)}, u32[]{:S(2)}, u32[]{:S(2)}) collective-permute-start(bf16[32,3584]{1,0:T(8,128)(2,1)} %bitcast.3), channel_id=1, source_target_pairs={{0,1},{1,0},{2,3},{3,2},{4,5},{5,4},{6,7},{7,6},{8,9},{9,8},{10,11... | collective-permute-start | bytes 688136 | tf_op jit(solution)/shard_map/ppermute | solution.py:20
  0.7 1.1 %copy-start.4 = (bf16[1,32,3584]{2,1,0:T(8,128)(2,1)S(1)}, bf16[1,32,3584]{2,1,0:T(8,128)(2,1)}, u32[]{:S(2)}) copy-start(bf16[1,32,3584]{2,1,0:T(8,128)(2,1)} %param.9) | copy-start | bytes 688132
  1.8 3.0 %copy-start.7 = (f32[3584]{0:T(1024)S(1)}, f32[3584]{0:T(1024)}, u32[]{:S(2)}) copy-start(f32[3584]{0:T(1024)} %param.10) | copy-start | bytes 43012
  1.8 6.4 %copy-start.3 = (f32[32,3584]{1,0:T(8,128)S(1)}, f32[32,3584]{1,0:T(8,128)}, u32[]{:S(2)}) copy-start(f32[32,3584]{1,0:T(8,128)} %residual_ref.1) | copy-start | bytes 1376260
  1.8 6.4 %collective-permute-start.1 = (bf16[32,1792]{1,0:T(8,128)(2,1)S(1)}, bf16[32,1792]{1,0:T(8,128)(2,1)S(1)}, u32[]{:S(2)}, u32[]{:S(2)}) collective-permute-start(bf16[32,1792]{1,0:T(8,128)(2,1)S(1)} %get-tuple-element.33), channel_id=1, source_target_pairs={{0,2},{1,3},{2,0},{3,1},{4,6},{5,7},{6,4},{7,5},{8,10},{9,11},{10,... | collective-permute-start | bytes 344072 | tf_op jit(solution)/shard_map/ppermute | solution.py:20
  8.2 9.5 %copy-start = (bf16[1,3584,256]{2,1,0:T(8,128)(2,1)S(1)}, bf16[1,3584,256]{2,1,0:T(8,128)(2,1)}, u32[]{:S(2)}) copy-start(bf16[1,3584,256]{2,1,0:T(8,128)(2,1)} %gate_ref.3) | copy-start | bytes 5505028
  8.2 9.5 %copy-start.1 = (bf16[1,3584,256]{2,1,0:T(8,128)(2,1)S(1)}, bf16[1,3584,256]{2,1,0:T(8,128)(2,1)}, u32[]{:S(2)}) copy-start(bf16[1,3584,256]{2,1,0:T(8,128)(2,1)} %up_ref.3) | copy-start | bytes 5505028
  8.5 6.9 %collective-permute-start.2 = (bf16[16,1920]{1,0:T(8,128)(2,1)S(1)}, bf16[16,1920]{1,0:T(8,128)(2,1)S(1)}, u32[]{:S(2)}, u32[]{:S(2)}) collective-permute-start(bf16[16,1920]{1,0:T(8,128)(2,1)S(1)} %get-tuple-element.38), channel_id=1, source_target_pairs={{0,12},{4,8},{8,4},{12,0},{1,13},{5,9},{9,5},{13,1},{2,14},{6,10},... | collective-permute-start | bytes 184328 | tf_op jit(solution)/shard_map/ppermute | solution.py:20
  12.4 5.1 %collective-permute-start.3 = (bf16[16,1920]{1,0:T(8,128)(2,1)S(1)}, bf16[16,1920]{1,0:T(8,128)(2,1)S(1)}, u32[]{:S(2)}, u32[]{:S(2)}) collective-permute-start(bf16[16,1920]{1,0:T(8,128)(2,1)S(1)} %get-tuple-element.39), channel_id=1, source_target_pairs={{0,8},{4,12},{8,0},{12,4},{1,9},{5,13},{9,1},{13,5},{2,10},{6,14},... | collective-permute-start | bytes 184328 | tf_op jit(solution)/shard_map/ppermute | solution.py:20
  12.4 5.1 %collective-permute-start.4 = (bf16[16,1920]{1,0:T(8,128)(2,1)S(1)}, bf16[16,1920]{1,0:T(8,128)(2,1)S(1)}, u32[]{:S(2)}, u32[]{:S(2)}) collective-permute-start(bf16[16,1920]{1,0:T(8,128)(2,1)S(1)} %get-tuple-element.40), channel_id=1, source_target_pairs={{0,4},{4,0},{8,12},{12,8},{1,5},{5,1},{9,13},{13,9},{2,6},{6,2},{1... | collective-permute-start | bytes 184328 | tf_op jit(solution)/shard_map/ppermute | solution.py:20
  17.6 1.6 %copy-start.2 = (bf16[1,256,3584]{2,1,0:T(8,128)(2,1)S(1)}, bf16[1,256,3584]{2,1,0:T(8,128)(2,1)}, u32[]{:S(2)}) copy-start(bf16[1,256,3584]{2,1,0:T(8,128)(2,1)} %down_ref.3) | copy-start | bytes 5505028
  17.6 1.6 %collective-permute-start.5 = (bf16[64,1920]{1,0:T(8,128)(2,1)S(1)}, bf16[64,1920]{1,0:T(8,128)(2,1)S(1)}, u32[]{:S(2)}, u32[]{:S(2)}) collective-permute-start(bf16[64,1920]{1,0:T(8,128)(2,1)S(1)} %shard_map.86.own_ref), channel_id=1, source_target_pairs={{0,1},{1,0},{2,3},{3,2},{4,5},{5,4},{6,7},{7,6},{8,9},{9,8},{10,11... | collective-permute-start | bytes 737288 | tf_op jit(solution)/shard_map/ppermute | solution.py:20
  19.9 1.6 %collective-permute-start.6 = (bf16[72,1792]{1,0:T(8,128)(2,1)S(1)}, bf16[72,1792]{1,0:T(8,128)(2,1)S(1)}, u32[]{:S(2)}, u32[]{:S(2)}) collective-permute-start(bf16[72,1792]{1,0:T(8,128)(2,1)S(1)} %get-tuple-element.45), channel_id=1, source_target_pairs={{0,1},{1,0},{2,3},{3,2},{4,5},{5,4},{6,7},{7,6},{8,9},{9,8},{10,11... | collective-permute-start | bytes 774152 | tf_op jit(solution)/shard_map/ppermute | solution.py:20
  21.6 4.7 %collective-permute-start.7 = (bf16[32,1024]{1,0:T(8,128)(2,1)S(1)}, bf16[32,1024]{1,0:T(8,128)(2,1)S(1)}, u32[]{:S(2)}, u32[]{:S(2)}) collective-permute-start(bf16[32,1024]{1,0:T(8,128)(2,1)S(1)} %get-tuple-element.47), channel_id=1, source_target_pairs={{0,2},{1,3},{2,0},{3,1},{4,6},{5,7},{6,4},{7,5},{8,10},{9,11},{10,... | collective-permute-start | bytes 196616 | tf_op jit(solution)/shard_map/ppermute | solution.py:20
  23.2 5.6 %collective-permute-start.10 = (bf16[32,1024]{1,0:T(8,128)(2,1)S(1)}, bf16[32,1024]{1,0:T(8,128)(2,1)S(1)}, u32[]{:S(2)}, u32[]{:S(2)}) collective-permute-start(bf16[32,1024]{1,0:T(8,128)(2,1)S(1)} %get-tuple-element.50), channel_id=1, source_target_pairs={{0,2},{1,3},{2,0},{3,1},{4,6},{5,7},{6,4},{7,5},{8,10},{9,11},{10,... | collective-permute-start | bytes 196616 | tf_op jit(solution)/shard_map/ppermute | solution.py:20
  26.3 6.1 %collective-permute-start.8 = (bf16[16,1024]{1,0:T(8,128)(2,1)S(1)}, bf16[16,1024]{1,0:T(8,128)(2,1)S(1)}, u32[]{:S(2)}, u32[]{:S(2)}) collective-permute-start(bf16[16,1024]{1,0:T(8,128)(2,1)S(1)} %get-tuple-element.48), channel_id=1, source_target_pairs={{0,12},{4,8},{8,4},{12,0},{1,13},{5,9},{9,5},{13,1},{2,14},{6,10},... | collective-permute-start | bytes 98312 | tf_op jit(solution)/shard_map/ppermute | solution.py:20
  28.8 4.8 %collective-permute-start.9 = (bf16[16,1024]{1,0:T(8,128)(2,1)S(1)}, bf16[16,1024]{1,0:T(8,128)(2,1)S(1)}, u32[]{:S(2)}, u32[]{:S(2)}) collective-permute-start(bf16[16,1024]{1,0:T(8,128)(2,1)S(1)} %get-tuple-element.49), channel_id=1, source_target_pairs={{0,8},{4,12},{8,0},{12,4},{1,9},{5,13},{9,1},{13,5},{2,10},{6,14},... | collective-permute-start | bytes 98312 | tf_op jit(solution)/shard_map/ppermute | solution.py:20
  28.8 4.8 %collective-permute-start.11 = (bf16[16,1024]{1,0:T(8,128)(2,1)S(1)}, bf16[16,1024]{1,0:T(8,128)(2,1)S(1)}, u32[]{:S(2)}, u32[]{:S(2)}) collective-permute-start(bf16[16,1024]{1,0:T(8,128)(2,1)S(1)} %get-tuple-element.51), channel_id=1, source_target_pairs={{0,4},{4,0},{8,12},{12,8},{1,5},{5,1},{9,13},{13,9},{2,6},{6,2},{1... | collective-permute-start | bytes 98312 | tf_op jit(solution)/shard_map/ppermute | solution.py:20

commit v5 on v4

--- a/solution.py
+++ b/solution.py
@@ -139,8 +139,8 @@
         block_refs[k][:, 2 * quarter :] = tile[k * MAIN : (k + 1) * MAIN]
 
 
-def pack_kernel(experts, *refs):
-    for ref, k in zip(refs, reversed(range(experts))):
+def pack_kernel(order, *refs):
+    for ref, k in zip(refs, order):
         refs[-1][k * MAIN : (k + 1) * MAIN] = ref[...]
 
 
@@ -241,9 +241,9 @@
         ref[...] = (own_ref[here] + far_ref[i * MAIN : (i + 1) * MAIN].astype(F32)).astype(BF16)
 
 
-def combine_kernel(experts, quarter, hidden_ref, mixing_ref, *refs):
+def combine_kernel(order, quarter, hidden_ref, mixing_ref, *refs):
     rows = hidden_ref.shape[0]
-    blocks = [ref[...] for ref in refs[:experts]][::-1]
+    blocks = [refs[order.index(k)][...] for k in range(len(order))]
     last = jnp.concatenate(unpack([block[:, quarter:] for block in blocks], quarter // LANES), axis=1)
     slots = jnp.concatenate([*[block[:, :quarter] for block in blocks], last], axis=0)
     both = dot(mixing_ref[:, : slots.shape[0]], slots)
@@ -256,7 +256,7 @@
     quarter = features // 4
     width = 2 * quarter
     chunks = width // LANES
-    steps = range(1, experts)
+    out_order, back_order = (2, 3, 1, 0), (3, 1, 2, 0)
     part = attention_part[0]
     near = xor_permute(part, "tensor", 1)
     before, spread = call(
@@ -291,9 +291,9 @@
         slots,
         tails,
     )
-    arrived = [*[xor_permute(blocks[k], "expert", k) for k in reversed(steps)], blocks[0]]
+    arrived = [*[xor_permute(blocks[k], "expert", k) for k in out_order[:-1]], blocks[0]]
     packed = out((experts * MAIN, width + LANES), BF16)
-    (arrived,) = call(functools.partial(pack_kernel, experts), (packed,), *arrived, flops=0)
+    (arrived,) = call(functools.partial(pack_kernel, out_order), (packed,), *arrived, flops=0)
     other = xor_permute(arrived, "tensor", 1)
     main, slot_count = experts * MAIN, (experts + 1) * MAIN
     packed_width, used = quarter + LANES, main + 8
@@ -325,9 +325,9 @@
     block = out((MAIN, packed_width), BF16)
     farthest = call(functools.partial(far_kernel, rest), [block] * early, own, far)
     blocks = [*call(functools.partial(far_kernel, 0), [block] * (experts - early), own, others), *farthest]
-    blocks = [*[xor_permute(blocks[k], "expert", k) for k in reversed(steps)], blocks[0]]
+    blocks = [*[xor_permute(blocks[k], "expert", k) for k in back_order[:-1]], blocks[0]]
     (result,) = call(
-        functools.partial(combine_kernel, experts, quarter), (out((rows, quarter), F32),), hidden, mixing, *blocks
+        functools.partial(combine_kernel, back_order, quarter), (out((rows, quarter), F32),), hidden, mixing, *blocks
     )
     return result
 

time: 34.6 us -> 34.5 us (level)
  transfers between devices with their start and end apart: 12 -> 12, of which waited for: 9 -> 10; matrix products, arithmetic and copies ran while one was open for 0% -> 0% of each run, Pallas kernels for 3% -> 3%
where the time goes in v5:
time: 34.5 us; the launch traced here: 34.3 us
  waiting for transfers between devices  16.3 us (47%)
  starting transfers between devices  14.7 us (43%)
  Pallas kernels  3 us (9%)
    ppermute x12, waiting for transfers between devices, xor_permute(): return lax.ppermute(value, axis, [(i, i ^ step) for i in range(count)])  16.3 us
    ppermute x12, starting transfers between devices, xor_permute(): return lax.ppermute(value, axis, [(i, i ^ step) for i in range(count)])  14.7 us
    pallas_call x12, Pallas kernels, call(): pl.pallas_call(kernel, out_shape=tuple(outs), in_specs=[vmem_spec] * len(...  3 us
  transfers between devices with their start and end apart: 12, of which 10 were waited for; matrix products, arithmetic and copies ran while one was open for 0% of the time, Pallas kernels for 3%

profile of v5, /device:TPU:0, one launch (start us, length us, event | category | flops | bytes accessed | tf_op | source)
XLA Modules:
  0.0 34.3 jit_solution(8003930110534178771)
XLA Ops:
  0.0 0.5 %collective-permute-start = (bf16[32,3584]{1,0:T(8,128)(2,1)}, bf16[32,3584]{1,0:T(8,128)(2,1)S(1)}, u32[]{:S(2)}, u32[]{:S(2)}) collective-permute-start(bf16[32,3584]{1,0:T(8,128)(2,1)} %bitcast.3), channel_id=1, source_target_pairs={{0,1},{1,0},{2,3},{3,2},{4,5},{5,4},{6,7},{7,6},{8,9},{9,8},{10,11... | collective-permute-start | bytes 688136 | tf_op jit(solution)/shard_map/ppermute | solution.py:20
  0.5 0.2 copy-done.5
  0.7 0.0 copy-done.6
  0.7 0.3 shard_map.83
  1.0 0.8 %collective-permute-done.near_ref = bf16[32,3584]{1,0:T(8,128)(2,1)S(1)} collective-permute-done((bf16[32,3584]{1,0:T(8,128)(2,1)}, bf16[32,3584]{1,0:T(8,128)(2,1)S(1)}, u32[]{:S(2)}, u32[]{:S(2)}) %collective-permute-start) | collective-permute-done | bytes 229408 | tf_op jit(solution)/shard_map/ppermute | solution.py:20
  1.8 2.9 %collective-permute-start.1 = (bf16[32,1792]{1,0:T(8,128)(2,1)S(1)}, bf16[32,1792]{1,0:T(8,128)(2,1)S(1)}, u32[]{:S(2)}, u32[]{:S(2)}) collective-permute-start(bf16[32,1792]{1,0:T(8,128)(2,1)S(1)} %get-tuple-element.33), channel_id=1, source_target_pairs={{0,2},{1,3},{2,0},{3,1},{4,6},{5,7},{6,4},{7,5},{8,10},{9,11},{10,... | collective-permute-start | bytes 344072 | tf_op jit(solution)/shard_map/ppermute | solution.py:20
  4.8 3.4 %collective-permute-done.1.far_ref = bf16[32,1792]{1,0:T(8,128)(2,1)S(1)} collective-permute-done((bf16[32,1792]{1,0:T(8,128)(2,1)S(1)}, bf16[32,1792]{1,0:T(8,128)(2,1)S(1)}, u32[]{:S(2)}, u32[]{:S(2)}) %collective-permute-start.1) | collective-permute-done | bytes 114720 | tf_op jit(solution)/shard_map/ppermute | solution.py:20
  8.2 0.3 shard_map.85
  8.5 2.9 %collective-permute-start.2 = (bf16[16,1920]{1,0:T(8,128)(2,1)S(1)}, bf16[16,1920]{1,0:T(8,128)(2,1)S(1)}, u32[]{:S(2)}, u32[]{:S(2)}) collective-permute-start(bf16[16,1920]{1,0:T(8,128)(2,1)S(1)} %get-tuple-element.38), channel_id=1, source_target_pairs={{0,8},{4,12},{8,0},{12,4},{1,9},{5,13},{9,1},{13,5},{2,10},{6,14},... | collective-permute-start | bytes 184328 | tf_op jit(solution)/shard_map/ppermute | solution.py:20
  11.4 1.3 %collective-permute-start.3 = (bf16[16,1920]{1,0:T(8,128)(2,1)S(1)}, bf16[16,1920]{1,0:T(8,128)(2,1)S(1)}, u32[]{:S(2)}, u32[]{:S(2)}) collective-permute-start(bf16[16,1920]{1,0:T(8,128)(2,1)S(1)} %get-tuple-element.39), channel_id=1, source_target_pairs={{0,12},{4,8},{8,4},{12,0},{1,13},{5,9},{9,5},{13,1},{2,14},{6,10},... | collective-permute-start | bytes 184328 | tf_op jit(solution)/shard_map/ppermute | solution.py:20
  12.8 0.2 collective-permute-start.4
  13.0 1.0 %collective-permute-done.2.refs_0_ = bf16[16,1920]{1,0:T(8,128)(2,1)S(1)} collective-permute-done((bf16[16,1920]{1,0:T(8,128)(2,1)S(1)}, bf16[16,1920]{1,0:T(8,128)(2,1)S(1)}, u32[]{:S(2)}, u32[]{:S(2)}) %collective-permute-start.2) | collective-permute-done | bytes 61472 | tf_op jit(solution)/shard_map/ppermute | solution.py:20
  13.9 3.6 %collective-permute-done.3.refs_1_ = bf16[16,1920]{1,0:T(8,128)(2,1)S(1)} collective-permute-done((bf16[16,1920]{1,0:T(8,128)(2,1)S(1)}, bf16[16,1920]{1,0:T(8,128)(2,1)S(1)}, u32[]{:S(2)}, u32[]{:S(2)}) %collective-permute-start.3) | collective-permute-done | bytes 61472 | tf_op jit(solution)/shard_map/ppermute | solution.py:20
  17.5 0.1 collective-permute-done.4.refs_2_
  17.7 0.0 copy-start.2
  17.7 0.1 collective-permute-start.5
  17.8 0.5 %shard_map.87 = (f32[80,256]{1,0:T(8,128)S(1)}, f32[80,256]{1,0:T(8,128)S(1)}) custom-call(bf16[64,1920]{1,0:T(8,128)(2,1)S(1)} %shard_map.86.own_ref, bf16[1,3584,256]{2,1,0:T(8,128)(2,1)S(1)} %copy-done, bf16[1,3584,256]{2,1,0:T(8,128)(2,1)S(1)} %copy-done.1), custom_call_target="tpu_custom_call" | custom-call | flops 4294967296 | bytes 4079616 | tf_op jit(solution)/shard_map/pallas_call | solution.py:31
  18.2 1.0 %collective-permute-done.5.other_ref = bf16[64,1920]{1,0:T(8,128)(2,1)S(1)} collective-permute-done((bf16[64,1920]{1,0:T(8,128)(2,1)S(1)}, bf16[64,1920]{1,0:T(8,128)(2,1)S(1)}, u32[]{:S(2)}, u32[]{:S(2)}) %collective-permute-start.5) | collective-permute-done | bytes 245792 | tf_op jit(solution)/shard_map/ppermute | solution.py:20
  19.2 0.7 %shard_map.88 = (bf16[80,256]{1,0:T(8,128)(2,1)S(1)}, bf16[72,1792]{1,0:T(8,128)(2,1)S(1)}) custom-call(bf16[64,1920]{1,0:T(8,128)(2,1)S(1)} %shard_map.86.own_ref, bf16[64,1920]{1,0:T(8,128)(2,1)S(1)} %collective-permute-done.5.other_ref, f32[80,256]{1,0:T(8,128)S(1)} %get-tuple-element.42.gated_ref, f32[80,256]{1,0:T(8,128)S(1)} %get-tuple-element.43.upward_ref, ...), custom_call_target="tpu_custom_call" | custom-call | flops 4294967296 | bytes 6459392 | tf_op jit(solution)/shard_map/pallas_call | solution.py:31
  20.0 0.2 collective-permute-start.6
  20.2 0.3 shard_map.89.kept_ref
  20.4 1.1 %collective-permute-done.6.near_ref = bf16[72,1792]{1,0:T(8,128)(2,1)S(1)} collective-permute-done((bf16[72,1792]{1,0:T(8,128)(2,1)S(1)}, bf16[72,1792]{1,0:T(8,128)(2,1)S(1)}, u32[]{:S(2)}, u32[]{:S(2)}) %collective-permute-start.6) | collective-permute-done | bytes 258080 | tf_op jit(solution)/shard_map/ppermute | solution.py:20
  21.6 0.1 shard_map.90
  21.7 1.6 %collective-permute-start.7 = (bf16[32,1024]{1,0:T(8,128)(2,1)S(1)}, bf16[32,1024]{1,0:T(8,128)(2,1)S(1)}, u32[]{:S(2)}, u32[]{:S(2)}) collective-permute-start(bf16[32,1024]{1,0:T(8,128)(2,1)S(1)} %get-tuple-element.47), channel_id=1, source_target_pairs={{0,2},{1,3},{2,0},{3,1},{4,6},{5,7},{6,4},{7,5},{8,10},{9,11},{10,... | collective-permute-start | bytes 196616 | tf_op jit(solution)/shard_map/ppermute | solution.py:20
  23.2 0.5 %collective-permute-start.9 = (bf16[32,1024]{1,0:T(8,128)(2,1)S(1)}, bf16[32,1024]{1,0:T(8,128)(2,1)S(1)}, u32[]{:S(2)}, u32[]{:S(2)}) collective-permute-start(bf16[32,1024]{1,0:T(8,128)(2,1)S(1)} %get-tuple-element.49), channel_id=1, source_target_pairs={{0,2},{1,3},{2,0},{3,1},{4,6},{5,7},{6,4},{7,5},{8,10},{9,11},{10,... | collective-permute-start | bytes 196616 | tf_op jit(solution)/shard_map/ppermute | solution.py:20
  23.7 2.6 %collective-permute-done.7.far_ref = bf16[32,1024]{1,0:T(8,128)(2,1)S(1)} collective-permute-done((bf16[32,1024]{1,0:T(8,128)(2,1)S(1)}, bf16[32,1024]{1,0:T(8,128)(2,1)S(1)}, u32[]{:S(2)}, u32[]{:S(2)}) %collective-permute-start.7) | collective-permute-done | bytes 65568 | tf_op jit(solution)/shard_map/ppermute | solution.py:20
  26.4 2.3 %collective-permute-start.8 = (bf16[16,1024]{1,0:T(8,128)(2,1)S(1)}, bf16[16,1024]{1,0:T(8,128)(2,1)S(1)}, u32[]{:S(2)}, u32[]{:S(2)}) collective-permute-start(bf16[16,1024]{1,0:T(8,128)(2,1)S(1)} %get-tuple-element.48), channel_id=1, source_target_pairs={{0,12},{4,8},{8,4},{12,0},{1,13},{5,9},{9,5},{13,1},{2,14},{6,10},... | collective-permute-start | bytes 98312 | tf_op jit(solution)/shard_map/ppermute | solution.py:20
  28.7 2.2 %collective-permute-start.10 = (bf16[16,1024]{1,0:T(8,128)(2,1)S(1)}, bf16[16,1024]{1,0:T(8,128)(2,1)S(1)}, u32[]{:S(2)}, u32[]{:S(2)}) collective-permute-start(bf16[16,1024]{1,0:T(8,128)(2,1)S(1)} %get-tuple-element.50), channel_id=1, source_target_pairs={{0,4},{4,0},{8,12},{12,8},{1,5},{5,1},{9,13},{13,9},{2,6},{6,2},{1... | collective-permute-start | bytes 98312 | tf_op jit(solution)/shard_map/ppermute | solution.py:20
  31.0 1.5 %collective-permute-done.8.refs_0_ = bf16[16,1024]{1,0:T(8,128)(2,1)S(1)} collective-permute-done((bf16[16,1024]{1,0:T(8,128)(2,1)S(1)}, bf16[16,1024]{1,0:T(8,128)(2,1)S(1)}, u32[]{:S(2)}, u32[]{:S(2)}) %collective-permute-start.8) | collective-permute-done | bytes 32800 | tf_op jit(solution)/shard_map/ppermute | solution.py:20
  32.5 1.1 %collective-permute-done.11.refs_2_ = bf16[16,1024]{1,0:T(8,128)(2,1)S(1)} collective-permute-done((bf16[16,1024]{1,0:T(8,128)(2,1)S(1)}, bf16[16,1024]{1,0:T(8,128)(2,1)S(1)}, u32[]{:S(2)}, u32[]{:S(2)}) %collective-permute-start.11) | collective-permute-done | bytes 32800 | tf_op jit(solution)/shard_map/ppermute | solution.py:20
  33.5 0.0 collective-permute-done.10.refs_1_
  33.5 0.8 %shard_map.93 = f32[32,896]{1,0:T(8,128)} custom-call(f32[32,896]{1,0:T(8,128)S(1)} %get-tuple-element.37.hidden_ref, bf16[64,128]{1,0:T(8,128)(2,1)S(1)} %get-tuple-element.31.after_ref.mixing_ref, bf16[16,1024]{1,0:T(8,128)(2,1)S(1)} %collective-permute-done.8.refs_0_, bf16[16,1024]{1,0:T(8,128)(2,1)S(1)} %collective-permute-done.10.refs_1_, ...), custom_call_target="tpu_custom_call" | custom-call | flops 4294967296 | bytes 376832 | tf_op jit(solution)/shard_map/pallas_call | solution.py:31
  (21 shorter events, 0.1 us)
Async XLA Ops:
  0.0 0.7 %copy-start.5 = (s32[32,2]{0,1:T(2,128)S(1)}, s32[32,2]{0,1:T(2,128)}, u32[]{:S(2)}) copy-start(s32[32,2]{0,1:T(2,128)} %param.11) | copy-start | bytes 772
  0.0 0.7 %copy-start.6 = (f32[32,2]{0,1:T(2,128)S(1)}, f32[32,2]{0,1:T(2,128)}, u32[]{:S(2)}) copy-start(f32[32,2]{0,1:T(2,128)} %param.12) | copy-start | bytes 772
  0.0 1.8 %collective-permute-start = (bf16[32,3584]{1,0:T(8,128)(2,1)}, bf16[32,3584]{1,0:T(8,128)(2,1)S(1)}, u32[]{:S(2)}, u32[]{:S(2)}) collective-permute-start(bf16[32,3584]{1,0:T(8,128)(2,1)} %bitcast.3), channel_id=1, source_target_pairs={{0,1},{1,0},{2,3},{3,2},{4,5},{5,4},{6,7},{7,6},{8,9},{9,8},{10,11... | collective-permute-start | bytes 688136 | tf_op jit(solution)/shard_map/ppermute | solution.py:20
  0.7 1.1 %copy-start.4 = (bf16[1,32,3584]{2,1,0:T(8,128)(2,1)S(1)}, bf16[1,32,3584]{2,1,0:T(8,128)(2,1)}, u32[]{:S(2)}) copy-start(bf16[1,32,3584]{2,1,0:T(8,128)(2,1)} %param.9) | copy-start | bytes 688132
  1.8 3.0 %copy-start.7 = (f32[3584]{0:T(1024)S(1)}, f32[3584]{0:T(1024)}, u32[]{:S(2)}) copy-start(f32[3584]{0:T(1024)} %param.10) | copy-start | bytes 43012
  1.8 6.4 %copy-start.3 = (f32[32,3584]{1,0:T(8,128)S(1)}, f32[32,3584]{1,0:T(8,128)}, u32[]{:S(2)}) copy-start(f32[32,3584]{1,0:T(8,128)} %residual_ref.1) | copy-start | bytes 1376260
  1.8 6.4 %collective-permute-start.1 = (bf16[32,1792]{1,0:T(8,128)(2,1)S(1)}, bf16[32,1792]{1,0:T(8,128)(2,1)S(1)}, u32[]{:S(2)}, u32[]{:S(2)}) collective-permute-start(bf16[32,1792]{1,0:T(8,128)(2,1)S(1)} %get-tuple-element.33), channel_id=1, source_target_pairs={{0,2},{1,3},{2,0},{3,1},{4,6},{5,7},{6,4},{7,5},{8,10},{9,11},{10,... | collective-permute-start | bytes 344072 | tf_op jit(solution)/shard_map/ppermute | solution.py:20
  8.2 9.5 %copy-start = (bf16[1,3584,256]{2,1,0:T(8,128)(2,1)S(1)}, bf16[1,3584,256]{2,1,0:T(8,128)(2,1)}, u32[]{:S(2)}) copy-start(bf16[1,3584,256]{2,1,0:T(8,128)(2,1)} %gate_ref.3) | copy-start | bytes 5505028
  8.2 9.6 %copy-start.1 = (bf16[1,3584,256]{2,1,0:T(8,128)(2,1)S(1)}, bf16[1,3584,256]{2,1,0:T(8,128)(2,1)}, u32[]{:S(2)}) copy-start(bf16[1,3584,256]{2,1,0:T(8,128)(2,1)} %up_ref.3) | copy-start | bytes 5505028
  8.5 5.4 %collective-permute-start.2 = (bf16[16,1920]{1,0:T(8,128)(2,1)S(1)}, bf16[16,1920]{1,0:T(8,128)(2,1)S(1)}, u32[]{:S(2)}, u32[]{:S(2)}) collective-permute-start(bf16[16,1920]{1,0:T(8,128)(2,1)S(1)} %get-tuple-element.38), channel_id=1, source_target_pairs={{0,8},{4,12},{8,0},{12,4},{1,9},{5,13},{9,1},{13,5},{2,10},{6,14},... | collective-permute-start | bytes 184328 | tf_op jit(solution)/shard_map/ppermute | solution.py:20
  11.4 6.1 %collective-permute-start.3 = (bf16[16,1920]{1,0:T(8,128)(2,1)S(1)}, bf16[16,1920]{1,0:T(8,128)(2,1)S(1)}, u32[]{:S(2)}, u32[]{:S(2)}) collective-permute-start(bf16[16,1920]{1,0:T(8,128)(2,1)S(1)} %get-tuple-element.39), channel_id=1, source_target_pairs={{0,12},{4,8},{8,4},{12,0},{1,13},{5,9},{9,5},{13,1},{2,14},{6,10},... | collective-permute-start | bytes 184328 | tf_op jit(solution)/shard_map/ppermute | solution.py:20
  12.8 4.9 %collective-permute-start.4 = (bf16[16,1920]{1,0:T(8,128)(2,1)S(1)}, bf16[16,1920]{1,0:T(8,128)(2,1)S(1)}, u32[]{:S(2)}, u32[]{:S(2)}) collective-permute-start(bf16[16,1920]{1,0:T(8,128)(2,1)S(1)} %get-tuple-element.40), channel_id=1, source_target_pairs={{0,4},{4,0},{8,12},{12,8},{1,5},{5,1},{9,13},{13,9},{2,6},{6,2},{1... | collective-permute-start | bytes 184328 | tf_op jit(solution)/shard_map/ppermute | solution.py:20
  17.7 1.6 %copy-start.2 = (bf16[1,256,3584]{2,1,0:T(8,128)(2,1)S(1)}, bf16[1,256,3584]{2,1,0:T(8,128)(2,1)}, u32[]{:S(2)}) copy-start(bf16[1,256,3584]{2,1,0:T(8,128)(2,1)} %down_ref.3) | copy-start | bytes 5505028
  17.7 1.6 %collective-permute-start.5 = (bf16[64,1920]{1,0:T(8,128)(2,1)S(1)}, bf16[64,1920]{1,0:T(8,128)(2,1)S(1)}, u32[]{:S(2)}, u32[]{:S(2)}) collective-permute-start(bf16[64,1920]{1,0:T(8,128)(2,1)S(1)} %shard_map.86.own_ref), channel_id=1, source_target_pairs={{0,1},{1,0},{2,3},{3,2},{4,5},{5,4},{6,7},{7,6},{8,9},{9,8},{10,11... | collective-permute-start | bytes 737288 | tf_op jit(solution)/shard_map/ppermute | solution.py:20
  20.0 1.6 %collective-permute-start.6 = (bf16[72,1792]{1,0:T(8,128)(2,1)S(1)}, bf16[72,1792]{1,0:T(8,128)(2,1)S(1)}, u32[]{:S(2)}, u32[]{:S(2)}) collective-permute-start(bf16[72,1792]{1,0:T(8,128)(2,1)S(1)} %get-tuple-element.45), channel_id=1, source_target_pairs={{0,1},{1,0},{2,3},{3,2},{4,5},{5,4},{6,7},{7,6},{8,9},{9,8},{10,11... | collective-permute-start | bytes 774152 | tf_op jit(solution)/shard_map/ppermute | solution.py:20
  21.7 4.7 %collective-permute-start.7 = (bf16[32,1024]{1,0:T(8,128)(2,1)S(1)}, bf16[32,1024]{1,0:T(8,128)(2,1)S(1)}, u32[]{:S(2)}, u32[]{:S(2)}) collective-permute-start(bf16[32,1024]{1,0:T(8,128)(2,1)S(1)} %get-tuple-element.47), channel_id=1, source_target_pairs={{0,2},{1,3},{2,0},{3,1},{4,6},{5,7},{6,4},{7,5},{8,10},{9,11},{10,... | collective-permute-start | bytes 196616 | tf_op jit(solution)/shard_map/ppermute | solution.py:20
  23.2 5.5 %collective-permute-start.9 = (bf16[32,1024]{1,0:T(8,128)(2,1)S(1)}, bf16[32,1024]{1,0:T(8,128)(2,1)S(1)}, u32[]{:S(2)}, u32[]{:S(2)}) collective-permute-start(bf16[32,1024]{1,0:T(8,128)(2,1)S(1)} %get-tuple-element.49), channel_id=1, source_target_pairs={{0,2},{1,3},{2,0},{3,1},{4,6},{5,7},{6,4},{7,5},{8,10},{9,11},{10,... | collective-permute-start | bytes 196616 | tf_op jit(solution)/shard_map/ppermute | solution.py:20
  26.4 6.1 %collective-permute-start.8 = (bf16[16,1024]{1,0:T(8,128)(2,1)S(1)}, bf16[16,1024]{1,0:T(8,128)(2,1)S(1)}, u32[]{:S(2)}, u32[]{:S(2)}) collective-permute-start(bf16[16,1024]{1,0:T(8,128)(2,1)S(1)} %get-tuple-element.48), channel_id=1, source_target_pairs={{0,12},{4,8},{8,4},{12,0},{1,13},{5,9},{9,5},{13,1},{2,14},{6,10},... | collective-permute-start | bytes 98312 | tf_op jit(solution)/shard_map/ppermute | solution.py:20
  28.7 4.8 %collective-permute-start.11 = (bf16[16,1024]{1,0:T(8,128)(2,1)S(1)}, bf16[16,1024]{1,0:T(8,128)(2,1)S(1)}, u32[]{:S(2)}, u32[]{:S(2)}) collective-permute-start(bf16[16,1024]{1,0:T(8,128)(2,1)S(1)} %get-tuple-element.51), channel_id=1, source_target_pairs={{0,8},{4,12},{8,0},{12,4},{1,9},{5,13},{9,1},{13,5},{2,10},{6,14},... | collective-permute-start | bytes 98312 | tf_op jit(solution)/shard_map/ppermute | solution.py:20
  28.7 4.8 %collective-permute-start.10 = (bf16[16,1024]{1,0:T(8,128)(2,1)S(1)}, bf16[16,1024]{1,0:T(8,128)(2,1)S(1)}, u32[]{:S(2)}, u32[]{:S(2)}) collective-permute-start(bf16[16,1024]{1,0:T(8,128)(2,1)S(1)} %get-tuple-element.50), channel_id=1, source_target_pairs={{0,4},{4,0},{8,12},{12,8},{1,5},{5,1},{9,13},{13,9},{2,6},{6,2},{1... | collective-permute-start | bytes 98312 | tf_op jit(solution)/shard_map/ppermute | solution.py:20

commit v6 on v4

--- a/solution.py
+++ b/solution.py
@@ -18,6 +18,12 @@
 def xor_permute(value, axis, step):
     count = lax.axis_size(axis)
     return lax.ppermute(value, axis, [(i, i ^ step) for i in range(count)])
+
+
+def cross_permute(value, step):
+    experts, tensors = lax.axis_size("expert"), lax.axis_size("tensor")
+    pairs = [(e * tensors + t, (e ^ step) * tensors + (t ^ 1)) for e in range(experts) for t in range(tensors)]
+    return lax.ppermute(value, ("expert", "tensor"), pairs)
 
 
 def split_pair(value):
@@ -206,7 +212,7 @@
     gated, upward = gated * inverse, upward * inverse
     active = (gated / (1.0 + jnp.exp(-gated)) * upward).astype(BF16)
     active_ref[...] = active
-    produce(quarter, active, down_ref, 1 - side, sent_ref)
+    produce(quarter, active, down_ref, side, sent_ref)
 
 
 def produce(quarter, active, down_ref, which, ref):
@@ -216,7 +222,7 @@
 
 
 def kept_kernel(quarter, active_ref, down_ref, kept_ref):
-    produce(quarter, active_ref[...], down_ref, lax.axis_index("tensor") % 2, kept_ref)
+    produce(quarter, active_ref[...], down_ref, 1 - lax.axis_index("tensor") % 2, kept_ref)
 
 
 def near_kernel(quarter, experts, kept_ref, near_ref, own_ref, far_ref, rest_ref):
@@ -325,7 +331,7 @@
     block = out((MAIN, packed_width), BF16)
     farthest = call(functools.partial(far_kernel, rest), [block] * early, own, far)
     blocks = [*call(functools.partial(far_kernel, 0), [block] * (experts - early), own, others), *farthest]
-    blocks = [*[xor_permute(blocks[k], "expert", k) for k in reversed(steps)], blocks[0]]
+    blocks = [*[cross_permute(blocks[k], k) for k in reversed(steps)], xor_permute(blocks[0], "tensor", 1)]
     (result,) = call(
         functools.partial(combine_kernel, experts, quarter), (out((rows, quarter), F32),), hidden, mixing, *blocks
     )

time: 34.6 us -> 33.7 us (0.974)
  the two profiles are of different devices: /device:TPU:0 before, /device:TPU:1 now
where the time goes in v6:
time: 33.7 us; the launch traced here: 33.5 us
  starting transfers between devices  15.8 us (47%)
  waiting for transfers between devices  14 us (42%)
  Pallas kernels  3 us (9%)
  local copies, waits for them, and re-layouts  0.66 us (2%)
    ppermute x10, waiting for transfers between devices, xor_permute(): return lax.ppermute(value, axis, [(i, i ^ step) for i in range(count)])  11.6 us
    ppermute x10, starting transfers between devices, xor_permute(): return lax.ppermute(value, axis, [(i, i ^ step) for i in range(count)])  9.99 us
    ppermute x3, starting transfers between devices, cross_permute(): return lax.ppermute(value, ('expert', 'tensor'), pairs)  5.76 us
    pallas_call x12, Pallas kernels, call(): pl.pallas_call(kernel, out_shape=tuple(outs), in_specs=[vmem_spec] * len(...  3 us
    ppermute x3, waiting for transfers between devices, cross_permute(): return lax.ppermute(value, ('expert', 'tensor'), pairs)  2.4 us
  transfers between devices with their start and end apart: 13, of which 8 were waited for; matrix products, arithmetic and copies ran while one was open for 0% of the time, Pallas kernels for 3%

profile of v6, /device:TPU:1, one launch (start us, length us, event | category | flops | bytes accessed | tf_op | source)
XLA Modules:
  0.0 33.5 jit_solution(9322091447614557215)
XLA Ops:
  0.0 0.1 collective-permute-start
  0.1 0.6 %copy-done.5 = s32[32,2]{0,1:T(2,128)S(1)} copy-done((s32[32,2]{0,1:T(2,128)S(1)}, s32[32,2]{0,1:T(2,128)}, u32[]{:S(2)}) %copy-start.5) | copy-done | bytes 280
  0.7 0.0 copy-done.6
  0.7 0.3 shard_map.83
  1.0 0.7 %collective-permute-done.near_ref = bf16[32,3584]{1,0:T(8,128)(2,1)S(1)} collective-permute-done((bf16[32,3584]{1,0:T(8,128)(2,1)}, bf16[32,3584]{1,0:T(8,128)(2,1)S(1)}, u32[]{:S(2)}, u32[]{:S(2)}) %collective-permute-start) | collective-permute-done | bytes 229408 | tf_op jit(solution)/shard_map/ppermute | solution.py:20
  1.7 2.4 %collective-permute-start.1 = (bf16[32,1792]{1,0:T(8,128)(2,1)S(1)}, bf16[32,1792]{1,0:T(8,128)(2,1)S(1)}, u32[]{:S(2)}, u32[]{:S(2)}) collective-permute-start(bf16[32,1792]{1,0:T(8,128)(2,1)S(1)} %get-tuple-element.33), channel_id=1, source_target_pairs={{0,2},{1,3},{2,0},{3,1},{4,6},{5,7},{6,4},{7,5},{8,10},{9,11},{10,... | collective-permute-start | bytes 344072 | tf_op jit(solution)/shard_map/ppermute | solution.py:20
  4.2 3.2 %collective-permute-done.1.far_ref = bf16[32,1792]{1,0:T(8,128)(2,1)S(1)} collective-permute-done((bf16[32,1792]{1,0:T(8,128)(2,1)S(1)}, bf16[32,1792]{1,0:T(8,128)(2,1)S(1)}, u32[]{:S(2)}, u32[]{:S(2)}) %collective-permute-start.1) | collective-permute-done | bytes 114720 | tf_op jit(solution)/shard_map/ppermute | solution.py:20
  7.4 0.3 shard_map.85
  7.7 3.3 %collective-permute-start.2 = (bf16[16,1920]{1,0:T(8,128)(2,1)S(1)}, bf16[16,1920]{1,0:T(8,128)(2,1)S(1)}, u32[]{:S(2)}, u32[]{:S(2)}) collective-permute-start(bf16[16,1920]{1,0:T(8,128)(2,1)S(1)} %get-tuple-element.38), channel_id=1, source_target_pairs={{0,12},{4,8},{8,4},{12,0},{1,13},{5,9},{9,5},{13,1},{2,14},{6,10},... | collective-permute-start | bytes 184328 | tf_op jit(solution)/shard_map/ppermute | solution.py:20
  11.0 0.0 collective-permute-start.3
  11.0 0.4 %collective-permute-start.4 = (bf16[16,1920]{1,0:T(8,128)(2,1)S(1)}, bf16[16,1920]{1,0:T(8,128)(2,1)S(1)}, u32[]{:S(2)}, u32[]{:S(2)}) collective-permute-start(bf16[16,1920]{1,0:T(8,128)(2,1)S(1)} %get-tuple-element.40), channel_id=1, source_target_pairs={{0,4},{4,0},{8,12},{12,8},{1,5},{5,1},{9,13},{13,9},{2,6},{6,2},{1... | collective-permute-start | bytes 184328 | tf_op jit(solution)/shard_map/ppermute | solution.py:20
  11.4 1.3 %collective-permute-done.2.refs_0_ = bf16[16,1920]{1,0:T(8,128)(2,1)S(1)} collective-permute-done((bf16[16,1920]{1,0:T(8,128)(2,1)S(1)}, bf16[16,1920]{1,0:T(8,128)(2,1)S(1)}, u32[]{:S(2)}, u32[]{:S(2)}) %collective-permute-start.2) | collective-permute-done | bytes 61472 | tf_op jit(solution)/shard_map/ppermute | solution.py:20
  12.6 3.2 %collective-permute-done.3.refs_1_ = bf16[16,1920]{1,0:T(8,128)(2,1)S(1)} collective-permute-done((bf16[16,1920]{1,0:T(8,128)(2,1)S(1)}, bf16[16,1920]{1,0:T(8,128)(2,1)S(1)}, u32[]{:S(2)}, u32[]{:S(2)}) %collective-permute-start.3) | collective-permute-done | bytes 61472 | tf_op jit(solution)/shard_map/ppermute | solution.py:20
  15.8 0.0 copy-start.2
  15.8 1.9 %collective-permute-start.5 = (bf16[64,1920]{1,0:T(8,128)(2,1)S(1)}, bf16[64,1920]{1,0:T(8,128)(2,1)S(1)}, u32[]{:S(2)}, u32[]{:S(2)}) collective-permute-start(bf16[64,1920]{1,0:T(8,128)(2,1)S(1)} %shard_map.86.own_ref), channel_id=1, source_target_pairs={{0,1},{1,0},{2,3},{3,2},{4,5},{5,4},{6,7},{7,6},{8,9},{9,8},{10,11... | collective-permute-start | bytes 737288 | tf_op jit(solution)/shard_map/ppermute | solution.py:20
  17.7 0.5 %shard_map.87 = (f32[80,256]{1,0:T(8,128)S(1)}, f32[80,256]{1,0:T(8,128)S(1)}) custom-call(bf16[64,1920]{1,0:T(8,128)(2,1)S(1)} %shard_map.86.own_ref, bf16[1,3584,256]{2,1,0:T(8,128)(2,1)S(1)} %copy-done, bf16[1,3584,256]{2,1,0:T(8,128)(2,1)S(1)} %copy-done.1), custom_call_target="tpu_custom_call" | custom-call | flops 4294967296 | bytes 4079616 | tf_op jit(solution)/shard_map/pallas_call | solution.py:37
  18.2 0.7 %collective-permute-done.5.other_ref = bf16[64,1920]{1,0:T(8,128)(2,1)S(1)} collective-permute-done((bf16[64,1920]{1,0:T(8,128)(2,1)S(1)}, bf16[64,1920]{1,0:T(8,128)(2,1)S(1)}, u32[]{:S(2)}, u32[]{:S(2)}) %collective-permute-start.5) | collective-permute-done | bytes 245792 | tf_op jit(solution)/shard_map/ppermute | solution.py:20
  18.9 0.7 %shard_map.88 = (bf16[80,256]{1,0:T(8,128)(2,1)S(1)}, bf16[72,1792]{1,0:T(8,128)(2,1)S(1)}) custom-call(bf16[64,1920]{1,0:T(8,128)(2,1)S(1)} %shard_map.86.own_ref, bf16[64,1920]{1,0:T(8,128)(2,1)S(1)} %collective-permute-done.5.other_ref, f32[80,256]{1,0:T(8,128)S(1)} %get-tuple-element.42.gated_ref, f32[80,256]{1,0:T(8,128)S(1)} %get-tuple-element.43.upward_ref, ...), custom_call_target="tpu_custom_call" | custom-call | flops 4294967296 | bytes 6459392 | tf_op jit(solution)/shard_map/pallas_call | solution.py:37
  19.6 0.4 %collective-permute-start.6 = (bf16[72,1792]{1,0:T(8,128)(2,1)S(1)}, bf16[72,1792]{1,0:T(8,128)(2,1)S(1)}, u32[]{:S(2)}, u32[]{:S(2)}) collective-permute-start(bf16[72,1792]{1,0:T(8,128)(2,1)S(1)} %get-tuple-element.45), channel_id=1, source_target_pairs={{0,1},{1,0},{2,3},{3,2},{4,5},{5,4},{6,7},{7,6},{8,9},{9,8},{10,11... | collective-permute-start | bytes 774152 | tf_op jit(solution)/shard_map/ppermute | solution.py:20
  20.0 0.3 shard_map.89.kept_ref
  20.3 0.9 %collective-permute-done.6.near_ref = bf16[72,1792]{1,0:T(8,128)(2,1)S(1)} collective-permute-done((bf16[72,1792]{1,0:T(8,128)(2,1)S(1)}, bf16[72,1792]{1,0:T(8,128)(2,1)S(1)}, u32[]{:S(2)}, u32[]{:S(2)}) %collective-permute-start.6) | collective-permute-done | bytes 258080 | tf_op jit(solution)/shard_map/ppermute | solution.py:20
  21.2 0.1 shard_map.90
  21.3 1.3 %collective-permute-start.7 = (bf16[32,1024]{1,0:T(8,128)(2,1)S(1)}, bf16[32,1024]{1,0:T(8,128)(2,1)S(1)}, u32[]{:S(2)}, u32[]{:S(2)}) collective-permute-start(bf16[32,1024]{1,0:T(8,128)(2,1)S(1)} %get-tuple-element.47), channel_id=1, source_target_pairs={{0,2},{1,3},{2,0},{3,1},{4,6},{5,7},{6,4},{7,5},{8,10},{9,11},{10,... | collective-permute-start | bytes 196616 | tf_op jit(solution)/shard_map/ppermute | solution.py:20
  22.5 0.2 collective-permute-start.10
  22.8 1.6 %collective-permute-done.7.far_ref = bf16[32,1024]{1,0:T(8,128)(2,1)S(1)} collective-permute-done((bf16[32,1024]{1,0:T(8,128)(2,1)S(1)}, bf16[32,1024]{1,0:T(8,128)(2,1)S(1)}, u32[]{:S(2)}, u32[]{:S(2)}) %collective-permute-start.7) | collective-permute-done | bytes 65568 | tf_op jit(solution)/shard_map/ppermute | solution.py:20
  24.5 4.0 %collective-permute-start.8 = (bf16[16,1024]{1,0:T(8,128)(2,1)S(1)}, bf16[16,1024]{1,0:T(8,128)(2,1)S(1)}, u32[]{:S(2)}, u32[]{:S(2)}) collective-permute-start(bf16[16,1024]{1,0:T(8,128)(2,1)S(1)} %get-tuple-element.48), channel_id=1, source_target_pairs={{0,13},{1,12},{2,15},{3,14},{4,9},{5,8},{6,11},{7,10},{8,5},{9,4},... | collective-permute-start | bytes 98312 | tf_op jit(solution)/shard_map/ppermute | solution.py:26
  28.4 1.8 %collective-permute-start.11 = (bf16[16,1024]{1,0:T(8,128)(2,1)S(1)}, bf16[16,1024]{1,0:T(8,128)(2,1)S(1)}, u32[]{:S(2)}, u32[]{:S(2)}) collective-permute-start(bf16[16,1024]{1,0:T(8,128)(2,1)S(1)} %get-tuple-element.51), channel_id=1, source_target_pairs={{0,5},{1,4},{2,7},{3,6},{4,1},{5,0},{6,3},{7,2},{8,13},{9,12},{10,... | collective-permute-start | bytes 98312 | tf_op jit(solution)/shard_map/ppermute | solution.py:26
  30.3 0.0 collective-permute-start.12
  30.3 0.0 collective-permute-done.8.refs_0_
  30.3 2.4 %collective-permute-done.9.refs_1_ = bf16[16,1024]{1,0:T(8,128)(2,1)S(1)} collective-permute-done((bf16[16,1024]{1,0:T(8,128)(2,1)S(1)}, bf16[16,1024]{1,0:T(8,128)(2,1)S(1)}, u32[]{:S(2)}, u32[]{:S(2)}) %collective-permute-start.9) | collective-permute-done | bytes 32800 | tf_op jit(solution)/shard_map/ppermute | solution.py:26
  32.7 0.0 collective-permute-done.11.refs_2_
  32.7 0.8 %shard_map.93 = f32[32,896]{1,0:T(8,128)} custom-call(f32[32,896]{1,0:T(8,128)S(1)} %get-tuple-element.37.hidden_ref, bf16[64,128]{1,0:T(8,128)(2,1)S(1)} %get-tuple-element.31.after_ref.mixing_ref, bf16[16,1024]{1,0:T(8,128)(2,1)S(1)} %collective-permute-done.8.refs_0_, bf16[16,1024]{1,0:T(8,128)(2,1)S(1)} %collective-permute-done.9.refs_1_, ...), custom_call_target="tpu_custom_call" | custom-call | flops 4294967296 | bytes 376832 | tf_op jit(solution)/shard_map/pallas_call | solution.py:37
  (23 shorter events, 0.1 us)
Async XLA Ops:
  0.0 0.7 %copy-start.5 = (s32[32,2]{0,1:T(2,128)S(1)}, s32[32,2]{0,1:T(2,128)}, u32[]{:S(2)}) copy-start(s32[32,2]{0,1:T(2,128)} %param.11) | copy-start | bytes 772
  0.0 0.7 %copy-start.6 = (f32[32,2]{0,1:T(2,128)S(1)}, f32[32,2]{0,1:T(2,128)}, u32[]{:S(2)}) copy-start(f32[32,2]{0,1:T(2,128)} %param.12) | copy-start | bytes 772
  0.0 1.7 %collective-permute-start = (bf16[32,3584]{1,0:T(8,128)(2,1)}, bf16[32,3584]{1,0:T(8,128)(2,1)S(1)}, u32[]{:S(2)}, u32[]{:S(2)}) collective-permute-start(bf16[32,3584]{1,0:T(8,128)(2,1)} %bitcast.3), channel_id=1, source_target_pairs={{0,1},{1,0},{2,3},{3,2},{4,5},{5,4},{6,7},{7,6},{8,9},{9,8},{10,11... | collective-permute-start | bytes 688136 | tf_op jit(solution)/shard_map/ppermute | solution.py:20
  0.7 1.0 %copy-start.4 = (bf16[1,32,3584]{2,1,0:T(8,128)(2,1)S(1)}, bf16[1,32,3584]{2,1,0:T(8,128)(2,1)}, u32[]{:S(2)}) copy-start(bf16[1,32,3584]{2,1,0:T(8,128)(2,1)} %param.9) | copy-start | bytes 688132
  1.7 2.4 %copy-start.7 = (f32[3584]{0:T(1024)S(1)}, f32[3584]{0:T(1024)}, u32[]{:S(2)}) copy-start(f32[3584]{0:T(1024)} %param.10) | copy-start | bytes 43012
  1.7 5.7 %copy-start.3 = (f32[32,3584]{1,0:T(8,128)S(1)}, f32[32,3584]{1,0:T(8,128)}, u32[]{:S(2)}) copy-start(f32[32,3584]{1,0:T(8,128)} %residual_ref.1) | copy-start | bytes 1376260
  1.7 5.6 %collective-permute-start.1 = (bf16[32,1792]{1,0:T(8,128)(2,1)S(1)}, bf16[32,1792]{1,0:T(8,128)(2,1)S(1)}, u32[]{:S(2)}, u32[]{:S(2)}) collective-permute-start(bf16[32,1792]{1,0:T(8,128)(2,1)S(1)} %get-tuple-element.33), channel_id=1, source_target_pairs={{0,2},{1,3},{2,0},{3,1},{4,6},{5,7},{6,4},{7,5},{8,10},{9,11},{10,... | collective-permute-start | bytes 344072 | tf_op jit(solution)/shard_map/ppermute | solution.py:20
  7.4 10.3 %copy-start = (bf16[1,3584,256]{2,1,0:T(8,128)(2,1)S(1)}, bf16[1,3584,256]{2,1,0:T(8,128)(2,1)}, u32[]{:S(2)}) copy-start(bf16[1,3584,256]{2,1,0:T(8,128)(2,1)} %gate_ref.3) | copy-start | bytes 5505028
  7.4 10.3 %copy-start.1 = (bf16[1,3584,256]{2,1,0:T(8,128)(2,1)S(1)}, bf16[1,3584,256]{2,1,0:T(8,128)(2,1)}, u32[]{:S(2)}) copy-start(bf16[1,3584,256]{2,1,0:T(8,128)(2,1)} %up_ref.3) | copy-start | bytes 5505028
  7.7 4.9 %collective-permute-start.2 = (bf16[16,1920]{1,0:T(8,128)(2,1)S(1)}, bf16[16,1920]{1,0:T(8,128)(2,1)S(1)}, u32[]{:S(2)}, u32[]{:S(2)}) collective-permute-start(bf16[16,1920]{1,0:T(8,128)(2,1)S(1)} %get-tuple-element.38), channel_id=1, source_target_pairs={{0,12},{4,8},{8,4},{12,0},{1,13},{5,9},{9,5},{13,1},{2,14},{6,10},... | collective-permute-start | bytes 184328 | tf_op jit(solution)/shard_map/ppermute | solution.py:20
  11.0 4.8 %collective-permute-start.3 = (bf16[16,1920]{1,0:T(8,128)(2,1)S(1)}, bf16[16,1920]{1,0:T(8,128)(2,1)S(1)}, u32[]{:S(2)}, u32[]{:S(2)}) collective-permute-start(bf16[16,1920]{1,0:T(8,128)(2,1)S(1)} %get-tuple-element.39), channel_id=1, source_target_pairs={{0,8},{4,12},{8,0},{12,4},{1,9},{5,13},{9,1},{13,5},{2,10},{6,14},... | collective-permute-start | bytes 184328 | tf_op jit(solution)/shard_map/ppermute | solution.py:20
  11.0 4.8 %collective-permute-start.4 = (bf16[16,1920]{1,0:T(8,128)(2,1)S(1)}, bf16[16,1920]{1,0:T(8,128)(2,1)S(1)}, u32[]{:S(2)}, u32[]{:S(2)}) collective-permute-start(bf16[16,1920]{1,0:T(8,128)(2,1)S(1)} %get-tuple-element.40), channel_id=1, source_target_pairs={{0,4},{4,0},{8,12},{12,8},{1,5},{5,1},{9,13},{13,9},{2,6},{6,2},{1... | collective-permute-start | bytes 184328 | tf_op jit(solution)/shard_map/ppermute | solution.py:20
  15.8 3.0 %copy-start.2 = (bf16[1,256,3584]{2,1,0:T(8,128)(2,1)S(1)}, bf16[1,256,3584]{2,1,0:T(8,128)(2,1)}, u32[]{:S(2)}) copy-start(bf16[1,256,3584]{2,1,0:T(8,128)(2,1)} %down_ref.3) | copy-start | bytes 5505028
  15.8 3.0 %collective-permute-start.5 = (bf16[64,1920]{1,0:T(8,128)(2,1)S(1)}, bf16[64,1920]{1,0:T(8,128)(2,1)S(1)}, u32[]{:S(2)}, u32[]{:S(2)}) collective-permute-start(bf16[64,1920]{1,0:T(8,128)(2,1)S(1)} %shard_map.86.own_ref), channel_id=1, source_target_pairs={{0,1},{1,0},{2,3},{3,2},{4,5},{5,4},{6,7},{7,6},{8,9},{9,8},{10,11... | collective-permute-start | bytes 737288 | tf_op jit(solution)/shard_map/ppermute | solution.py:20
  19.6 1.6 %collective-permute-start.6 = (bf16[72,1792]{1,0:T(8,128)(2,1)S(1)}, bf16[72,1792]{1,0:T(8,128)(2,1)S(1)}, u32[]{:S(2)}, u32[]{:S(2)}) collective-permute-start(bf16[72,1792]{1,0:T(8,128)(2,1)S(1)} %get-tuple-element.45), channel_id=1, source_target_pairs={{0,1},{1,0},{2,3},{3,2},{4,5},{5,4},{6,7},{7,6},{8,9},{9,8},{10,11... | collective-permute-start | bytes 774152 | tf_op jit(solution)/shard_map/ppermute | solution.py:20
  21.3 3.2 %collective-permute-start.7 = (bf16[32,1024]{1,0:T(8,128)(2,1)S(1)}, bf16[32,1024]{1,0:T(8,128)(2,1)S(1)}, u32[]{:S(2)}, u32[]{:S(2)}) collective-permute-start(bf16[32,1024]{1,0:T(8,128)(2,1)S(1)} %get-tuple-element.47), channel_id=1, source_target_pairs={{0,2},{1,3},{2,0},{3,1},{4,6},{5,7},{6,4},{7,5},{8,10},{9,11},{10,... | collective-permute-start | bytes 196616 | tf_op jit(solution)/shard_map/ppermute | solution.py:20
  22.5 5.9 %collective-permute-start.10 = (bf16[32,1024]{1,0:T(8,128)(2,1)S(1)}, bf16[32,1024]{1,0:T(8,128)(2,1)S(1)}, u32[]{:S(2)}, u32[]{:S(2)}) collective-permute-start(bf16[32,1024]{1,0:T(8,128)(2,1)S(1)} %get-tuple-element.50), channel_id=1, source_target_pairs={{0,2},{1,3},{2,0},{3,1},{4,6},{5,7},{6,4},{7,5},{8,10},{9,11},{10,... | collective-permute-start | bytes 196616 | tf_op jit(solution)/shard_map/ppermute | solution.py:20
  24.5 5.8 %collective-permute-start.8 = (bf16[16,1024]{1,0:T(8,128)(2,1)S(1)}, bf16[16,1024]{1,0:T(8,128)(2,1)S(1)}, u32[]{:S(2)}, u32[]{:S(2)}) collective-permute-start(bf16[16,1024]{1,0:T(8,128)(2,1)S(1)} %get-tuple-element.48), channel_id=1, source_target_pairs={{0,13},{1,12},{2,15},{3,14},{4,9},{5,8},{6,11},{7,10},{8,5},{9,4},... | collective-permute-start | bytes 98312 | tf_op jit(solution)/shard_map/ppermute | solution.py:26
  28.4 4.2 %collective-permute-start.9 = (bf16[16,1024]{1,0:T(8,128)(2,1)S(1)}, bf16[16,1024]{1,0:T(8,128)(2,1)S(1)}, u32[]{:S(2)}, u32[]{:S(2)}) collective-permute-start(bf16[16,1024]{1,0:T(8,128)(2,1)S(1)} %get-tuple-element.49), channel_id=1, source_target_pairs={{0,9},{1,8},{2,11},{3,10},{4,13},{5,12},{6,15},{7,14},{8,1},{9,0},... | collective-permute-start | bytes 98312 | tf_op jit(solution)/shard_map/ppermute | solution.py:26
  28.4 4.2 %collective-permute-start.11 = (bf16[16,1024]{1,0:T(8,128)(2,1)S(1)}, bf16[16,1024]{1,0:T(8,128)(2,1)S(1)}, u32[]{:S(2)}, u32[]{:S(2)}) collective-permute-start(bf16[16,1024]{1,0:T(8,128)(2,1)S(1)} %get-tuple-element.51), channel_id=1, source_target_pairs={{0,5},{1,4},{2,7},{3,6},{4,1},{5,0},{6,3},{7,2},{8,13},{9,12},{10,... | collective-permute-start | bytes 98312 | tf_op jit(solution)/shard_map/ppermute | solution.py:26
  30.3 2.4 %collective-permute-start.12 = (bf16[16,1024]{1,0:T(8,128)(2,1)S(1)}, bf16[16,1024]{1,0:T(8,128)(2,1)S(1)}, u32[]{:S(2)}, u32[]{:S(2)}) collective-permute-start(bf16[16,1024]{1,0:T(8,128)(2,1)S(1)} %get-tuple-element.52), channel_id=1, source_target_pairs={{0,1},{1,0},{2,3},{3,2},{4,5},{5,4},{6,7},{7,6},{8,9},{9,8},{10,11... | collective-permute-start | bytes 98312 | tf_op jit(solution)/shard_map/ppermute | solution.py:20
